TPU v7x, 32 devices: a whole 2x2x4 slice. The times are simulated.
32 devices in a mesh: members: 2 (over y), shard: 4 (over z), dp: 4 (over x, core).
Axes of the slice: x: 2, y: 2, z: 4, core: 2. Of those that a mesh axis runs over, the one named last changes fastest.
Arguments:
- table: bfloat16 [1024, 3072], P(None, 'shard'), may hold values from -6 to 6
- indices: int32 [8192], P(('members', 'dp')), parts along dimension 0, may hold values from 0 to 1023
- grad_out: bfloat16 [8192, 8192], P(('members', 'dp'), 'shard'), parts along dimension 0, may hold values from -6 to 6
- mean: float32 [6144, 8192], P(('members', 'dp'), 'shard'), parts along dimension 0, may hold values from -6 to 6
- precision: float32 [6144, 8192], P(('members', 'dp'), 'shard'), parts along dimension 0, may hold values from 0.3 to 3
- block_salts: int32 [32], P('members'), parts along dimension 0, may hold values from 0 to 1073741823
Outputs:
- new_mean: float32 [6144, 8192], P(('members', 'dp'), 'shard'), parts along dimension 0
- new_precision: float32 [6144, 8192], P(('members', 'dp'), 'shard'), parts along dimension 0
There are 2 independent parts, one for each index of `members`. A program takes and returns all parts, laid end to end along the dimension named above; an argument that names none is the same for every part. Nothing has to cross between parts.
All inputs are finite; a program needn't handle non-finite values.
Results may differ from a plain program's by a relative error of at most 0.0035.
Values may be sent and summed in bfloat16 or wider, within the bound.
No kernel may reach another device: no remote copies, remote signals or barrier semaphores. Data moves between devices by JAX's collectives and lax.ppermute only.
A program may use at most 192 MiB of HBM per device.

v0:
```python
import jax
import jax.numpy as jnp
from jax import lax
from jax.sharding import PartitionSpec as P


def hashed_noise(rows, cols, salt_value, full_ff):
    value = rows * full_ff + cols
    mixed = jnp.bitwise_xor(value, salt_value)
    mixed = mixed * 73244475
    mixed = jnp.bitwise_xor(mixed, jnp.right_shift(jnp.bitwise_and(mixed, 2147483647), 16))
    mixed = mixed * 73244475
    mixed = jnp.bitwise_xor(mixed, jnp.right_shift(jnp.bitwise_and(mixed, 2147483647), 16))
    kept = jnp.right_shift(jnp.bitwise_and(mixed, 2147483647), 7).astype(jnp.float32)
    return 1.7320508075688772 * (2.0 * (kept + 0.5) / 16777216.0 - 1.0)


def sample_block(mean_rows, prec_rows, row_start, col_start, salt_rows, full_ff, inv_root):
    rows = row_start + jnp.arange(mean_rows.shape[0], dtype=jnp.int32)[:, None]
    cols = col_start + jnp.arange(mean_rows.shape[1], dtype=jnp.int32)[None, :]
    noise = hashed_noise(rows, cols, salt_rows, full_ff)
    theta = mean_rows + 0.5 * noise / jnp.sqrt(prec_rows + 0.1)
    return (theta * inv_root).astype(jnp.bfloat16)


def on_device(table, indices, grad_out, mean, precision, block_salts):
    rows_blk = mean.shape[0]
    cols_blk = mean.shape[1]
    n_shard = lax.axis_size("shard")
    dp_pos = lax.axis_index("dp")
    shard_pos = lax.axis_index("shard")
    full_ff = cols_blk * n_shard
    whole_table = None
    whole_table = lax.all_gather(table, "shard", axis=1, tiled=True)
    feats = jnp.take(whole_table, indices, axis=0)
    width = feats.shape[1]
    inv_root = 1.0 / jnp.sqrt(jnp.float32(width))
    inv_width = 1.0 / jnp.float32(width)
    col_start = shard_pos * cols_blk
    own_salt = lax.dynamic_index_in_dim(
        block_salts, dp_pos * n_shard + shard_pos, 0, keepdims=False
    )
    own_weight = sample_block(
        mean, precision, dp_pos * rows_blk, col_start, own_salt, full_ff, inv_root
    )
    pre = jnp.dot(
        feats,
        lax.all_gather(own_weight, "dp", axis=0, tiled=True),
        preferred_element_type=jnp.float32,
    )
    sig = jax.nn.sigmoid(pre)
    slope = (grad_out.astype(jnp.float32) * sig * (1.0 + pre * (1.0 - sig))).astype(jnp.bfloat16)
    slope_wide = slope.astype(jnp.float32)
    slope_sq = (slope_wide * slope_wide).astype(jnp.bfloat16)
    feats_wide = feats.astype(jnp.float32)
    feats_sq = (feats_wide * feats_wide).astype(jnp.bfloat16)
    contract = (((0,), (0,)), ((), ()))
    grad_part = (
        lax.dot_general(feats, slope, contract, preferred_element_type=jnp.float32) * inv_root
    )
    sq_part = (
        lax.dot_general(feats_sq, slope_sq, contract, preferred_element_type=jnp.float32)
        * inv_width
    )
    summed = lax.psum_scatter(
        jnp.concatenate([grad_part, sq_part], axis=1).astype(jnp.bfloat16),
        "dp",
        scatter_dimension=0,
        tiled=True,
    ).astype(jnp.float32)
    grad = summed[:, :cols_blk]
    sq_sum = summed[:, cols_blk:]
    new_precision = 0.7 * precision + 0.3 * sq_sum
    new_mean = mean - 0.5 * (grad + 0.1 * mean) / (new_precision + 0.1)
    return (new_mean, new_precision)


def solution(mesh):
    in_specs = (
        P(None, "shard"),
        P(("members", "dp")),
        P(("members", "dp"), "shard"),
        P(("members", "dp"), "shard"),
        P(("members", "dp"), "shard"),
        P("members"),
    )
    out_specs = (P(("members", "dp"), "shard"), P(("members", "dp"), "shard"))
    return jax.shard_map(
        on_device, mesh=mesh, in_specs=in_specs, out_specs=out_specs, check_vma=False
    )
```

profile of v0, /device:TPU:0, one launch (start us, length us, event | category | flops | bytes accessed | tf_op | source)
XLA Modules:
  0.0 504.9 jit_solution(5925079462637556487)
XLA Ops:
  7.2 0.0 all-gather.3.cloned.1.call-start
  7.2 0.7 all-gather.3.cloned.1.call-update
  7.9 0.0 all-gather.5.cloned.1.call-start
  8.0 6.6 %copy.12 = f32[768,2048]{0,1:T(8,128)} copy(f32[768,2048]{1,0:T(8,128)} %param.9) | data formatting | bytes 12582912 | tf_op args[3]
  14.5 0.0 copy-start.2
  14.5 6.7 %copy.8 = f32[768,2048]{0,1:T(8,128)} copy(f32[768,2048]{1,0:T(8,128)} %param.10) | data formatting | bytes 12582912 | tf_op args[4]
  21.2 0.0 copy-done.2
  21.2 0.6 dynamic_slice.4
  21.9 0.0 copy-start.1
  21.9 10.0 %multiply_convert_fusion.6 = bf16[768,2048]{0,1:T(8,128)(2,1)} fusion(f32[768,2048]{0,1:T(8,128)} %copy.12, f32[768,2048]{0,1:T(8,128)} %copy.8, s32[]{:T(128)} %bitcast, s32[2048]{0:T(1024)S(1)} %iota_add_fusion, s32[768]{0:T(1024)S(1)} %add_multiply_fusion), kind=kLoop, calls=%fused_computation.13 | loop fusion | flops 34603008 | bytes 15739908 | tf_op jit(solution)/shard_map/convert_element_type | solution.py:23
  31.9 0.0 all-gather.5.cloned.1.call-update
  31.9 0.0 reduce-scatter.2.cloned.1.call-start
  32.0 0.0 copy-done.1
  32.0 95.7 %all-gather.3.cloned.1.call-done = bf16[1024,3072]{1,0:T(8,128)(2,1)} async-done(((bf16[1024,768]{1,0:T(8,128)(2,1)}), bf16[1024,3072]{1,0:T(8,128)(2,1)}) %all-gather.3.cloned.1.call-update) | async-done | bytes 6291472 | tf_op jit(solution)/shard_map/all_gather | solution.py:34
  127.7 15.8 %gather_fusion = bf16[1024,3072]{1,0:T(8,128)(2,1)} fusion(bf16[1024,3072]{1,0:T(8,128)(2,1)} %all-gather.3.cloned.1.call-done, s32[1024]{0:T(1024)S(1)} %fusion.4), kind=kCustom, calls=%fused_computation | custom fusion | bytes 12587008 | tf_op jit(solution)/shard_map/jit(_take)/gather | solution.py:35
  143.5 66.1 %all-gather.5.cloned.1.call-done = bf16[3072,2048]{0,1:T(8,128)(2,1)} async-done(((bf16[768,2048]{0,1:T(8,128)(2,1)}), bf16[3072,2048]{0,1:T(8,128)(2,1)}) %all-gather.5.cloned.1.call-update) | async-done | bytes 12582928 | tf_op jit(solution)/shard_map/all_gather | solution.py:48
  209.5 22.2 %multiply_convert_fusion.4 = bf16[1024,2048]{1,0:T(8,128)(2,1)} fusion(bf16[1024,2048]{1,0:T(8,128)(2,1)} %param.8, bf16[3072,2048]{0,1:T(8,128)(2,1)} %all-gather.5.cloned.1.call-done, bf16[1024,3072]{1,0:T(8,128)(2,1)} %gather_fusion, pred[1024]{0:T(1024)(128)(4,1)S(1)} %compare_and_fusion), kind=kOutput, calls=%fused_computation.6 | convolution fusion | flops 12909019136 | bytes 27264000 | tf_op jit(solution)/shard_map/dot_general | solution.py:46
  231.7 0.0 copy-start
  231.7 21.3 %multiply_convert_fusion = bf16[3072,2048]{0,1:T(8,128)(2,1)} fusion(bf16[1024,2048]{1,0:T(8,128)(2,1)} %multiply_convert_fusion.4, bf16[1024,3072]{1,0:T(8,128)(2,1)} %gather_fusion, pred[1024]{0:T(1024)(128)(4,1)S(1)} %compare_and_fusion), kind=kOutput, calls=%fused_computation.2 | convolution fusion | flops 12916359168 | bytes 23069696 | tf_op jit(solution)/shard_map/dot_general | solution.py:62
  253.0 0.0 copy-done
  253.0 18.4 %multiply_convert_fusion.1 = bf16[3072,2048]{0,1:T(8,128)(2,1)} fusion(bf16[1024,2048]{1,0:T(8,128)(2,1)} %multiply_convert_fusion.4, bf16[1024,3072]{1,0:T(8,128)(2,1)S(1)} %copy-done, pred[1024]{0:T(1024)(128)(4,1)S(1)} %compare_and_fusion), kind=kOutput, calls=%fused_computation.3 | convolution fusion | flops 12900630528 | bytes 23069696 | tf_op jit(solution)/shard_map/dot_general | solution.py:59
  271.4 20.5 %pad_maximum_fusion = bf16[3072,4096]{0,1:T(8,128)(2,1)} fusion(bf16[3072,2048]{0,1:T(8,128)(2,1)} %multiply_convert_fusion, bf16[3072,2048]{0,1:T(8,128)(2,1)} %multiply_convert_fusion.1), kind=kLoop, calls=%fused_computation.1 | loop fusion | flops 50331648 | bytes 50331648 | tf_op jit(solution)/shard_map/concatenate | solution.py:66
  291.9 0.0 reduce-scatter.2.cloned.1.call-update
  291.9 180.6 %reduce-scatter.2.cloned.1.call-done = bf16[768,4096]{0,1:T(8,128)(2,1)} async-done(((bf16[3072,4096]{0,1:T(8,128)(2,1)}), bf16[768,4096]{0,1:T(8,128)(2,1)}) %reduce-scatter.2.cloned.1.call-update) | async-done | bytes 6291472 | tf_op jit(solution)/shard_map/reduce_scatter | solution.py:65
  472.5 3.8 convert_element_type.36
  476.3 9.0 %fusion.3 = (f32[768,2048]{0,1:T(8,128)}, f32[768,2048]{0,1:T(8,128)}) fusion(f32[768,2048]{0,1:T(8,128)} %copy.12, f32[768,4096]{0,1:T(8,128)S(1)} %convert_element_type.36, f32[768,2048]{0,1:T(8,128)} %copy.8), kind=kLoop, calls=%fused_computation.12 | loop fusion | flops 14155776 | bytes 37748736 | tf_op jit(solution)/shard_map/sub | solution.py:74
  485.3 6.6 %copy.13 = f32[768,2048]{1,0:T(8,128)} copy(f32[768,2048]{0,1:T(8,128)} %get-tuple-element.4) | data formatting | bytes 12582912
  491.8 6.6 %copy.14 = f32[768,2048]{1,0:T(8,128)} copy(f32[768,2048]{0,1:T(8,128)} %get-tuple-element.5) | data formatting | bytes 12582912
  (4 shorter events, 0.0 us)
Async XLA Ops:
  7.2 120.5 %all-gather.3.cloned.1.call-start = ((), (), s32[]{:S(2)}) async-start(), calls=%async_computation.1 | async-start | bytes 7864320 | tf_op jit(solution)/shard_map/all_gather | solution.py:34
  7.9 201.6 %all-gather.5.cloned.1.call-start = ((), (), s32[]{:S(2)}) async-start(), calls=%async_computation.2 | async-start | bytes 15728640 | tf_op jit(solution)/shard_map/all_gather | solution.py:48
  14.5 6.7 %copy-start.2 = (s32[16]{0:T(128)S(1)}, s32[16]{0:T(128)}, u32[]{:S(2)}) copy-start(s32[16]{0:T(128)} %param.11) | copy-start | bytes 196
  21.9 10.1 %copy-start.1 = (s32[1024]{0:T(1024)S(1)}, s32[1024]{0:T(1024)}, u32[]{:S(2)}) copy-start(s32[1024]{0:T(1024)} %param.7) | copy-start | bytes 12292
  31.9 440.6 %reduce-scatter.2.cloned.1.call-start = ((), (), s32[]{:S(2)}) async-start(), calls=%async_computation.3 | async-start | bytes 31457280 | tf_op jit(solution)/shard_map/reduce_scatter | solution.py:65
  231.7 21.3 %copy-start = (bf16[1024,3072]{1,0:T(8,128)(2,1)S(1)}, bf16[1024,3072]{1,0:T(8,128)(2,1)}, u32[]{:S(2)}) copy-start(bf16[1024,3072]{1,0:T(8,128)(2,1)} %gather_fusion) | copy-start | bytes 18874372
Sparse Core Ops, SparseCore 0:
  9.6 118.0 all-gather.2
  129.2 80.2 all-gather.4
  292.1 180.4 reduce-scatter.1
where the time goes:
time: 506 us; the launch traced here: 505 us
  waiting for transfers between devices  343 us (68%)
  matrix products  61.9 us (12%)
  other arithmetic  43.2 us (9%)
  local copies, waits for them, and re-layouts  42.9 us (8%)
  between operations  13.8 us (3%)
    reduce_scatter x1, waiting for transfers between devices, on_device(): lax.psum_scatter(jnp.concatenate([grad_part, sq_part], axis=1).astype(jnp...  181 us
    all_gather x1, waiting for transfers between devices, on_device(): whole_table = lax.all_gather(table, 'shard', axis=1, tiled=True)  95.7 us
    all_gather x1, waiting for transfers between devices, on_device(): lax.all_gather(own_weight, 'dp', axis=0, tiled=True)  66.1 us
    unnamed x10, local copies, waits for them, and re-layouts  26.4 us
    dot_general x1, matrix products, on_device(): jnp.dot(feats, lax.all_gather(own_weight, 'dp', axis=0, tiled=True), pref...  22.2 us
    dot_general x1, matrix products, on_device(): lax.dot_general(feats_sq, slope_sq, contract, preferred_element_type=jnp....  21.3 us
    concatenate x1, other arithmetic, on_device(): jnp.concatenate([grad_part, sq_part], axis=1).astype(jnp.bfloat16)  20.5 us
    dot_general x1, matrix products, on_device(): lax.dot_general(feats, slope, contract, preferred_element_type=jnp.float32)  18.4 us
  transfers between devices with their start and end apart: 3, of which 3 were waited for; matrix products, arithmetic and copies ran while one was open for 8% of the time, Pallas kernels for 0%

commit v1 on v0

v1 whole, which is shorter than its diff:
```python
import functools

import jax
import jax.numpy as jnp
from jax import lax
from jax.sharding import PartitionSpec as P

F32 = jnp.float32
BF16 = jnp.bfloat16


def hashed_noise(rows, cols, salt_value, full_ff):
    value = rows * full_ff + cols
    mixed = jnp.bitwise_xor(value, salt_value)
    mixed = mixed * 73244475
    mixed = jnp.bitwise_xor(mixed, jnp.right_shift(jnp.bitwise_and(mixed, 2147483647), 16))
    mixed = mixed * 73244475
    mixed = jnp.bitwise_xor(mixed, jnp.right_shift(jnp.bitwise_and(mixed, 2147483647), 16))
    kept = jnp.right_shift(jnp.bitwise_and(mixed, 2147483647), 7).astype(jnp.float32)
    return 1.7320508075688772 * (2.0 * (kept + 0.5) / 16777216.0 - 1.0)


def sample_block(mean_rows, prec_rows, row_start, col_start, salt_rows, full_ff, inv_root):
    rows = row_start + jnp.arange(mean_rows.shape[0], dtype=jnp.int32)[:, None]
    cols = col_start + jnp.arange(mean_rows.shape[1], dtype=jnp.int32)[None, :]
    noise = hashed_noise(rows, cols, salt_rows, full_ff)
    theta = mean_rows + 0.5 * noise / jnp.sqrt(prec_rows + 0.1)
    return (theta * inv_root).astype(BF16)


def dot(a, b):
    return jnp.dot(a, b, preferred_element_type=F32)


def dot_t(a, b):
    return lax.dot_general(a, b, (((0,), (0,)), ((), ())), preferred_element_type=F32)


def square(a):
    wide = a.astype(F32)
    return (wide * wide).astype(BF16)


def one_hot(idx, n_rows):
    return (idx[:, None] == jnp.arange(n_rows, dtype=jnp.int32)[None, :]).astype(BF16)


def row_sums(idx, go, n_rows):
    hot = one_hot(idx, n_rows)
    return dot_t(hot, go), dot_t(hot, square(go))


def slopes(pre, total, total_sq):
    sig = jax.nn.sigmoid(pre)
    h = sig * (1.0 + pre * (1.0 - sig))
    return (h * total).astype(BF16), (h * h * total_sq).astype(BF16)


def update(grad, sq_sum, mean, precision):
    new_precision = 0.7 * precision + 0.3 * sq_sum
    new_mean = mean - 0.5 * (grad + 0.1 * mean) / (new_precision + 0.1)
    return new_mean, new_precision


def own_sample(mean, precision, block_salts, dp_pos, shard_pos, n_shard, width):
    rows_blk, cols_blk = mean.shape
    inv_root = 1.0 / jnp.sqrt(F32(width))
    salt = lax.dynamic_index_in_dim(block_salts, dp_pos * n_shard + shard_pos, 0, keepdims=False)
    return sample_block(
        mean, precision, dp_pos * rows_blk, shard_pos * cols_blk, salt, cols_blk * n_shard, inv_root
    )


def general(table, indices, grad_out, mean, precision, block_salts):
    n_dp, n_shard = lax.axis_size("dp"), lax.axis_size("shard")
    dp_pos, shard_pos = lax.axis_index("dp"), lax.axis_index("shard")
    n_rows, width = table.shape[0], table.shape[1] * n_shard
    rows_blk = mean.shape[0]
    whole = lax.all_gather(table, "shard", axis=1, tiled=True)
    tab = lax.dynamic_slice_in_dim(whole, dp_pos * rows_blk, rows_blk, 1)
    weight = own_sample(mean, precision, block_salts, dp_pos, shard_pos, n_shard, width)
    pre = lax.psum_scatter(dot(tab, weight), "dp", scatter_dimension=1, tiled=True)
    go = lax.all_to_all(grad_out, "dp", 1, 0, tiled=True)
    idx = lax.all_gather(indices, "dp", axis=0, tiled=True)
    s, s2 = slopes(pre, *row_sums(idx, go, n_rows))
    s = lax.all_gather(s, "dp", axis=1, tiled=True)
    s2 = lax.all_gather(s2, "dp", axis=1, tiled=True)
    grad = dot_t(tab, s) * (1.0 / jnp.sqrt(F32(width)))
    sq_sum = dot_t(square(tab), s2) * (1.0 / F32(width))
    return update(grad, sq_sum, mean, precision)


CORE = [(j, j ^ 1) for j in range(4)]
CHIP = [(j, j ^ 2) for j in range(4)]


def table_steps():
    low = [
        [((0, 0), (1, 0)), ((1, 0), (2, 1)), ((1, 1), (0, 1))],
        [((1, 0), (2, 0)), ((2, 1), (3, 1))],
        [((2, 0), (3, 0))],
    ]
    steps = []
    for moves in low:
        pairs = []
        for (z, c), (z2, c2) in moves:
            pairs.append((z * 4 + c, z2 * 4 + c2))
            pairs.append(((3 - z) * 4 + 3 - c, (3 - z2) * 4 + 3 - c2))
        steps.append(pairs)
    return steps


def fetch_table(table, dp_pos, shard_pos, pieces):
    rows = table.shape[0] // pieces
    steps = table_steps()
    out = []
    for k in range(pieces):
        own = table[k * rows : (k + 1) * rows]
        first = lax.ppermute(own, ("shard", "dp"), steps[0])
        second = lax.ppermute(first, ("shard", "dp"), steps[1])
        third = lax.ppermute(second, ("shard", "dp"), steps[2])
        got = jnp.where(shard_pos == dp_pos, own, first + second + third)
        out.append(got)
    return out


def on_device(table, indices, grad_out, mean, precision, block_salts):
    n_shard = lax.axis_size("shard")
    dp_pos, shard_pos = lax.axis_index("dp"), lax.axis_index("shard")
    n_rows, width = table.shape[0], table.shape[1] * n_shard
    part = mean.shape[1] // 4
    chunks = 2
    cut = part // chunks
    mine, other = dp_pos, dp_pos ^ 2

    def cols(a, owner, k=None):
        if k is None:
            return lax.dynamic_slice_in_dim(a, owner * part, part, 1)
        return lax.dynamic_slice_in_dim(a, owner * part + k * cut, cut, 1)

    idx_core = lax.ppermute(indices, "dp", CORE)
    idx_far = lax.ppermute(jnp.concatenate([indices, idx_core]), "dp", CHIP)
    go_far0 = lax.ppermute(cols(grad_out, other), "dp", CHIP)
    go_pass = lax.ppermute(cols(grad_out, other ^ 1), "dp", CORE)
    go_core = lax.ppermute(cols(grad_out, mine ^ 1), "dp", CORE)
    go_far1 = lax.ppermute(go_pass, "dp", CHIP)
    go_near = jnp.concatenate([cols(grad_out, mine), go_core], 0)
    idx_near = jnp.concatenate([indices, idx_core], 0)

    tabs = fetch_table(table, dp_pos, shard_pos, 2)
    tab = jnp.concatenate(tabs, 0)
    tab_core = jnp.concatenate([lax.ppermute(t, "dp", CORE) for t in tabs], 0)

    weight = own_sample(mean, precision, block_salts, dp_pos, shard_pos, n_shard, width)
    w_core_far = lax.ppermute(cols(weight, other ^ 1), "dp", CORE)
    w_core_near = lax.ppermute(cols(weight, mine ^ 1), "dp", CORE)
    w_far = cols(weight, other)
    w_near = cols(weight, mine)

    near_sums = row_sums(idx_near, go_near, n_rows)
    far_sums = row_sums(idx_far, jnp.concatenate([go_far0, go_far1], 0), n_rows)
    total = near_sums[0] + far_sums[0]
    total_sq = near_sums[1] + far_sums[1]
    pre_near = dot(tab, w_near) + dot(tab_core, w_core_near)

    pieces = []
    for k in range(chunks):
        c = slice(k * cut, (k + 1) * cut)
        out = (dot(tab, w_far[:, c]) + dot(tab_core, w_core_far[:, c])).astype(BF16)
        pre = pre_near[:, c] + lax.ppermute(out, "dp", CHIP).astype(F32)
        s, s2 = slopes(pre, total[:, c], total_sq[:, c])
        s_both = jnp.concatenate([s, s2], 0)
        far = lax.ppermute(s_both, "dp", CHIP)
        core = lax.ppermute(s_both, "dp", CORE)
        core_far = lax.ppermute(far, "dp", CORE)
        pieces.append((s_both, core, far, core_far))

    tab_sq = square(tab)
    inv_root = 1.0 / jnp.sqrt(F32(width))
    inv_width = 1.0 / F32(width)
    new_mean, new_precision = jnp.zeros_like(mean), jnp.zeros_like(precision)
    for n, flip in enumerate((0, 1, 2, 3)):
        for k in range(chunks):
            s_both = pieces[k][n]
            grad = dot_t(tab, s_both[:n_rows]) * inv_root
            sq_sum = dot_t(tab_sq, s_both[n_rows:]) * inv_width
            a, b = update(grad, sq_sum, cols(mean, mine ^ flip, k), cols(precision, mine ^ flip, k))
            start = (mine ^ flip) * part + k * cut
            new_mean = lax.dynamic_update_slice_in_dim(new_mean, a, start, 1)
            new_precision = lax.dynamic_update_slice_in_dim(new_precision, b, start, 1)
    return new_mean, new_precision


def solution(mesh):
    in_specs = (
        P(None, "shard"),
        P(("members", "dp")),
        P(("members", "dp"), "shard"),
        P(("members", "dp"), "shard"),
        P(("members", "dp"), "shard"),
        P("members"),
    )
    out_specs = (P(("members", "dp"), "shard"), P(("members", "dp"), "shard"))
    fits = mesh.shape["dp"] == 4 and mesh.shape["shard"] == 4
    return jax.shard_map(
        on_device if fits else general,
        mesh=mesh,
        in_specs=in_specs,
        out_specs=out_specs,
        check_vma=False,
    )
```

time: 506 us -> 200 us (0.40)
  waiting for transfers between devices: 343 us -> 91.5 us
  starting transfers between devices: 0.12 us -> 46.4 us
  matrix products: 61.9 us -> 29.7 us
  other arithmetic: 43.2 us -> 13.8 us
  local copies, waits for them, and re-layouts: 42.9 us -> 17.1 us
  between operations: 13.8 us -> 1.13 us
    reduce_scatter x1 -> x0, waiting for transfers between devices: 181 us -> none  [on_device(): lax.psum_scatter(jnp.concatenate([grad_part, sq_part], axis=1).astype(jnp...]
    all_gather x2 -> x0, waiting for transfers between devices: 162 us -> none  [the longest x1 95.7 us: on_device(): whole_table = lax.all_gather(table, 'shard', axis=1, tiled=True)]
    ppermute x0 -> x24, waiting for transfers between devices: none -> 91.5 us  [the longest x2 38.4 us: on_device(): far = lax.ppermute(s_both, 'dp', CHIP)]
    ppermute x0 -> x24, starting transfers between devices: none -> 46.4 us  [the longest x2 19.5 us: fetch_table(): first = lax.ppermute(own, ('shard', 'dp'), steps[0])]
    dot_general x3 -> x26, matrix products: 61.9 us -> 29.7 us  [the longest x20 25.1 us: dot_t(): lax.dot_general(a, b, (((0,), (0,)), ((), ())), preferred_element_type=F32)]
    concatenate x1 -> x2, other arithmetic: 20.5 us -> 0.14 us  [on_device(): s_both = jnp.concatenate([s, s2], 0)]
    unnamed x10 -> x27, local copies, waits for them, and re-layouts: 26.4 us -> 6.97 us
    gather x1 -> x0, local copies, waits for them, and re-layouts: 15.8 us -> none  [on_device(): feats = jnp.take(whole_table, indices, axis=0)]
  transfers between devices with their start and end apart: 3 -> 24, of which waited for: 3 -> 9; matrix products, arithmetic and copies ran while one was open for 8% -> 26% of each run, Pallas kernels for 0% -> 0%
where the time goes in v1:
time: 200 us
  waiting for transfers between devices  91.5 us (46%)
  starting transfers between devices  46.4 us (23%)
  matrix products  29.7 us (15%)
  local copies, waits for them, and re-layouts  17.1 us (9%)
  other arithmetic  13.8 us (7%)
    ppermute x2, waiting for transfers between devices, on_device(): far = lax.ppermute(s_both, 'dp', CHIP)  38.4 us
    dot_general x20, matrix products, dot_t(): lax.dot_general(a, b, (((0,), (0,)), ((), ())), preferred_element_type=F32)  25.1 us
    ppermute x2, waiting for transfers between devices, on_device(): pre = pre_near[:, c] + lax.ppermute(out, 'dp', CHIP).astype(F32)  20.1 us
    ppermute x2, starting transfers between devices, fetch_table(): first = lax.ppermute(own, ('shard', 'dp'), steps[0])  19.5 us
    ppermute x1, waiting for transfers between devices, on_device(): go_far1 = lax.ppermute(go_pass, 'dp', CHIP)  15.9 us
    ppermute x2, waiting for transfers between devices, fetch_table(): first = lax.ppermute(own, ('shard', 'dp'), steps[0])  12.4 us
    convert_element_type x1, other arithmetic, sample_block(): return (theta * inv_root).astype(BF16)  8.36 us
    unnamed x27, local copies, waits for them, and re-layouts  6.97 us
  transfers between devices with their start and end apart: 24, of which 9 were waited for; matrix products, arithmetic and copies ran while one was open for 26% of the time, Pallas kernels for 0%

profile of v1, /device:TPU:0, one launch (start us, length us, event | category | flops | bytes accessed | tf_op | source)
XLA Modules:
  0.0 199.7 jit_solution(13368303412635873283)
XLA Ops:
  0.6 1.2 slice.73
  1.8 5.0 %collective-permute-start.3 = (bf16[512,768]{1,0:T(8,128)(2,1)S(1)}, bf16[512,768]{1,0:T(8,128)(2,1)S(1)}, u32[]{:S(2)}, u32[]{:S(2)}) collective-permute-start(bf16[512,768]{1,0:T(8,128)(2,1)S(1)} %slice.73), channel_id=1, source_target_pairs={{0,4},{15,11},{4,9},{11,6},{5,1},{10,14},{16,20},{31,27},{20,25},{... | collective-permute-start | bytes 2359304 | tf_op jit(solution)/shard_map/ppermute | solution.py:119
  6.8 9.4 %collective-permute-done.3 = bf16[512,768]{1,0:T(8,128)(2,1)S(1)} collective-permute-done((bf16[512,768]{1,0:T(8,128)(2,1)S(1)}, bf16[512,768]{1,0:T(8,128)(2,1)S(1)}, u32[]{:S(2)}, u32[]{:S(2)}) %collective-permute-start.3) | collective-permute-done | bytes 786464 | tf_op jit(solution)/shard_map/ppermute | solution.py:119
  16.2 1.5 collective-permute-start.4
  17.8 1.5 collective-permute-start.5
  19.3 4.1 %constant_dynamic-slice_fusion.3 = (bf16[1024,512]{1,0:T(8,128)(2,1)}, bf16[1024,512]{1,0:T(8,128)(2,1)}, bf16[1024,512]{1,0:T(8,128)(2,1)S(1)}, bf16[1024,512]{1,0:T(8,128)(2,1)}) fusion(bf16[1024,2048]{1,0:T(8,128)(2,1)} %param.8, s32[]{:T(128)S(6)} %select_n.34, s32[]{:T(128)S(6)} %select_n.39, s32[]{:T(128)S(6)} %select_n.41, s32[]{:T(128)S(6)} %select_n.40), kind=kLoop, calls=%fused_computation.138 | loop fusion | bytes 8388624 | tf_op jit(solution)/shard_map/dynamic_slice | solution.py:138
  23.4 2.8 %add_select_fusion = (bf16[512,768]{1,0:T(8,128)(2,1)}, bf16[512,768]{1,0:T(8,128)(2,1)}) fusion(bf16[512,768]{1,0:T(8,128)(2,1)} %collective-permute-done.5, bf16[512,768]{1,0:T(8,128)(2,1)S(1)} %collective-permute-done.3, bf16[512,768]{1,0:T(8,128)(2,1)} %collective-permute-done.4, pred[]{:T(512)S(6)} %eq.14, bf16[1024,768]{1,0:T(8,128)(2,1)S(1)} %copy-done.2), kind=kLoop, calls=%fused_computation.102 | loop fusion | flops 1179648 | bytes 5505025 | tf_op jit(solution)/shard_map/jit(_where)/select_n | solution.py:122
  26.2 14.5 %collective-permute-start = (bf16[512,768]{1,0:T(8,128)(2,1)}, bf16[512,768]{1,0:T(8,128)(2,1)}, u32[]{:S(2)}, u32[]{:S(2)}) collective-permute-start(bf16[512,768]{1,0:T(8,128)(2,1)} %get-tuple-element.15), channel_id=1, source_target_pairs={{0,4},{15,11},{4,9},{11,6},{5,1},{10,14},{16,20},{31,27},{20,25},{... | collective-permute-start | bytes 2359304 | tf_op jit(solution)/shard_map/ppermute | solution.py:119
  40.7 0.2 collective-permute-start.14
  40.9 4.7 %collective-permute-start.11 = (s32[1024]{0:T(1024)S(1)}, s32[1024]{0:T(1024)S(1)}, u32[]{:S(2)}, u32[]{:S(2)}) collective-permute-start(s32[1024]{0:T(1024)S(1)} %copy-done.6), channel_id=1, source_target_pairs={{0,1},{1,0},{2,3},{3,2},{4,5},{5,4},{6,7},{7,6},{8,9},{9,8},{10,11... | collective-permute-start | bytes 12296 | tf_op jit(solution)/shard_map/ppermute | solution.py:141
  45.7 0.5 dynamic_slice.77
  46.2 0.4 collective-permute-start.16
  46.6 3.0 %collective-permute-done = bf16[512,768]{1,0:T(8,128)(2,1)} collective-permute-done((bf16[512,768]{1,0:T(8,128)(2,1)}, bf16[512,768]{1,0:T(8,128)(2,1)}, u32[]{:S(2)}, u32[]{:S(2)}) %collective-permute-start) | collective-permute-done | bytes 786464 | tf_op jit(solution)/shard_map/ppermute | solution.py:119
  49.6 1.6 collective-permute-start.1
  51.2 8.4 %multiply_convert_fusion = bf16[768,2048]{1,0:T(8,128)(2,1)S(1)} fusion(f32[768,2048]{1,0:T(8,128)} %param.9, f32[768,2048]{1,0:T(8,128)} %param.10, s32[]{:T(128)} %bitcast, s32[2048]{0:T(1024)S(1)} %iota_add_fusion, s32[768]{0:T(1024)S(1)} %add_multiply_fusion.2), kind=kLoop, calls=%fused_computation.6 | loop fusion | flops 34603008 | bytes 15739908 | tf_op jit(solution)/shard_map/convert_element_type | solution.py:28
  59.6 1.4 constant_dynamic-slice_fusion.5
  61.0 3.5 %collective-permute-done.14 = bf16[1024,512]{1,0:T(8,128)(2,1)} collective-permute-done((bf16[1024,512]{1,0:T(8,128)(2,1)}, bf16[1024,512]{1,0:T(8,128)(2,1)}, u32[]{:S(2)}, u32[]{:S(2)}) %collective-permute-start.14) | collective-permute-done | bytes 1048608 | tf_op jit(solution)/shard_map/ppermute | solution.py:143
  64.5 5.3 %collective-permute-start.8 = (bf16[768,512]{1,0:T(8,128)(2,1)}, bf16[768,512]{1,0:T(8,128)(2,1)S(1)}, u32[]{:S(2)}, u32[]{:S(2)}) collective-permute-start(bf16[768,512]{1,0:T(8,128)(2,1)} %get-tuple-element.12), channel_id=1, source_target_pairs={{0,1},{1,0},{2,3},{3,2},{4,5},{5,4},{6,7},{7,6},{8,9},{9,8},{10,11... | collective-permute-start | bytes 2359304 | tf_op jit(solution)/shard_map/ppermute | solution.py:156
  69.7 1.3 constant_dynamic-update-slice_fusion.4
  71.0 15.9 %collective-permute-done.16 = bf16[1024,512]{1,0:T(8,128)(2,1)} collective-permute-done((bf16[1024,512]{1,0:T(8,128)(2,1)}, bf16[1024,512]{1,0:T(8,128)(2,1)}, u32[]{:S(2)}, u32[]{:S(2)}) %collective-permute-start.16) | collective-permute-done | bytes 1048608 | tf_op jit(solution)/shard_map/ppermute | solution.py:146
  86.9 1.3 constant_dynamic-update-slice_fusion.3
  88.3 1.0 collective-permute-start.2
  89.3 1.3 collective-permute-done.13
  90.6 2.8 %fusion.1 = f32[1024,512]{1,0:T(8,128)S(1)} fusion(bf16[2048,512]{1,0:T(8,128)(2,1)S(1)} %constant_dynamic-update-slice_fusion.3, s32[2048]{0:T(1024)S(1)} %collective-permute-done.13), kind=kOutput, calls=%fused_computation.2 | convolution fusion | flops 2149580800 | bytes 4202496 | tf_op jit(solution)/shard_map/dot_general | solution.py:36
  93.5 4.2 %fusion.8 = f32[1024,512]{1,0:T(8,128)S(1)} fusion(f32[1024,512]{1,0:T(8,128)S(1)} %fusion.1, s32[2048]{0:T(1024)S(1)} %constant_dynamic-update-slice_fusion.13, bf16[1024,512]{1,0:T(8,128)(2,1)} %collective-permute-done.12, bf16[1024,512]{1,0:T(8,128)(2,1)S(1)} %copy-done.5), kind=kOutput, calls=%fused_computation.17 | convolution fusion | flops 2154299392 | bytes 6299648 | tf_op jit(solution)/shard_map/dot_general | solution.py:36
  97.7 1.3 collective-permute-start.7
  99.0 1.5 add_select_fusion.1
  100.6 2.8 %fusion = f32[1024,512]{1,0:T(8,128)S(1)} fusion(s32[2048]{0:T(1024)S(1)} %collective-permute-done.13, bf16[2048,512]{1,0:T(8,128)(2,1)S(1)} %constant_dynamic-update-slice_fusion.3), kind=kOutput, calls=%fused_computation.1 | convolution fusion | flops 2152726528 | bytes 4202496 | tf_op jit(solution)/shard_map/dot_general | solution.py:36
  103.4 4.0 %fusion.9 = f32[1024,512]{1,0:T(8,128)S(1)} fusion(f32[1024,512]{1,0:T(8,128)S(1)} %fusion, s32[2048]{0:T(1024)S(1)} %constant_dynamic-update-slice_fusion.13, bf16[1024,512]{1,0:T(8,128)(2,1)} %collective-permute-done.12, bf16[1024,512]{1,0:T(8,128)(2,1)S(1)} %copy-done.5), kind=kOutput, calls=%fused_computation.18 | convolution fusion | flops 2156396544 | bytes 6299648 | tf_op jit(solution)/shard_map/dot_general | solution.py:36
  107.6 0.6 fusion.77
  108.2 0.9 fusion.11
  109.1 6.7 %collective-permute-start.17 = (bf16[1024,256]{1,0:T(8,128)(2,1)S(1)}, bf16[1024,256]{1,0:T(8,128)(2,1)S(1)}, u32[]{:S(2)}, u32[]{:S(2)}) collective-permute-start(bf16[1024,256]{1,0:T(8,128)(2,1)S(1)} %fusion.11), channel_id=1, source_target_pairs={{0,2},{1,3},{2,0},{3,1},{4,6},{5,7},{6,4},{7,5},{8,10},{9,11},{10,... | collective-permute-start | bytes 1572872 | tf_op jit(solution)/shard_map/ppermute | solution.py:170
  115.8 0.6 fusion.80
  116.4 0.6 fusion.10
  117.1 1.0 fusion.88
  118.1 1.0 convolution_add_fusion
  119.1 9.5 %collective-permute-done.17 = bf16[1024,256]{1,0:T(8,128)(2,1)S(1)} collective-permute-done((bf16[1024,256]{1,0:T(8,128)(2,1)S(1)}, bf16[1024,256]{1,0:T(8,128)(2,1)S(1)}, u32[]{:S(2)}, u32[]{:S(2)}) %collective-permute-start.17) | collective-permute-done | bytes 524320 | tf_op jit(solution)/shard_map/ppermute | solution.py:170
  128.5 10.6 %collective-permute-done.10 = bf16[1024,256]{1,0:T(8,128)(2,1)S(1)} collective-permute-done((bf16[1024,256]{1,0:T(8,128)(2,1)S(1)}, bf16[1024,256]{1,0:T(8,128)(2,1)S(1)}, u32[]{:S(2)}, u32[]{:S(2)}) %collective-permute-start.10) | collective-permute-done | bytes 524320 | tf_op jit(solution)/shard_map/ppermute | solution.py:170
  139.1 1.0 fusion.61
  140.3 1.8 collective-permute-start.20
  142.4 0.3 collective-permute-start.21
  142.7 0.8 broadcast.63.clone
  143.5 0.7 constant_dynamic-update-slice_fusion.5
  144.2 0.7 constant_dynamic-update-slice_fusion.12
  144.9 0.8 broadcast.63
  145.7 0.9 slice-done.3
  146.6 0.7 fusion.59
  147.2 0.7 fusion.53
  148.0 18.4 %collective-permute-done.20 = bf16[2048,256]{1,0:T(8,128)(2,1)S(1)} collective-permute-done((bf16[2048,256]{1,0:T(8,128)(2,1)S(1)}, bf16[2048,256]{1,0:T(8,128)(2,1)S(1)}, u32[]{:S(2)}, u32[]{:S(2)}) %collective-permute-start.20) | collective-permute-done | bytes 1048608 | tf_op jit(solution)/shard_map/ppermute | solution.py:173
  166.4 0.7 constant_dynamic-update-slice_fusion.11
  167.0 0.7 constant_dynamic-update-slice_fusion.10
  167.7 0.7 constant_dynamic-update-slice_fusion.9
  168.4 20.0 %collective-permute-done.21 = bf16[2048,256]{1,0:T(8,128)(2,1)S(1)} collective-permute-done((bf16[2048,256]{1,0:T(8,128)(2,1)S(1)}, bf16[2048,256]{1,0:T(8,128)(2,1)S(1)}, u32[]{:S(2)}, u32[]{:S(2)}) %collective-permute-start.21) | collective-permute-done | bytes 1048608 | tf_op jit(solution)/shard_map/ppermute | solution.py:173
  188.4 0.7 fusion.47
  189.1 0.7 fusion.41
  189.8 0.7 constant_dynamic-update-slice_fusion.8
  190.5 1.0 fusion.35
  191.4 0.7 fusion.29
  192.2 0.7 constant_dynamic-update-slice_fusion.7
  192.8 0.7 fusion.23
  193.6 0.7 constant_dynamic-update-slice_fusion.6
  194.3 0.7 fusion.17
  195.0 2.0 copy-done.1
  197.0 2.7 %copy-done = f32[768,2048]{1,0:T(8,128)} copy-done((f32[768,2048]{1,0:T(8,128)}, f32[768,2048]{1,0:T(8,128)S(1)}, u32[]{:S(2)}) %copy-start) | copy-done | bytes 6291480
  (56 shorter events, 0.9 us)
Async XLA Ops:
  1.8 14.4 %collective-permute-start.3 = (bf16[512,768]{1,0:T(8,128)(2,1)S(1)}, bf16[512,768]{1,0:T(8,128)(2,1)S(1)}, u32[]{:S(2)}, u32[]{:S(2)}) collective-permute-start(bf16[512,768]{1,0:T(8,128)(2,1)S(1)} %slice.73), channel_id=1, source_target_pairs={{0,4},{15,11},{4,9},{11,6},{5,1},{10,14},{16,20},{31,27},{20,25},{... | collective-permute-start | bytes 2359304 | tf_op jit(solution)/shard_map/ppermute | solution.py:119
  16.2 1.5 collective-permute-start.4
  17.8 5.6 %collective-permute-start.5 = (bf16[512,768]{1,0:T(8,128)(2,1)}, bf16[512,768]{1,0:T(8,128)(2,1)}, u32[]{:S(2)}, u32[]{:S(2)}) collective-permute-start(bf16[512,768]{1,0:T(8,128)(2,1)} %collective-permute-done.4), channel_id=1, source_target_pairs={{8,12},{7,3},{24,28},{23,19}} | collective-permute-start | bytes 2359304 | tf_op jit(solution)/shard_map/ppermute | solution.py:121
  19.3 4.1 %copy-start.2 = (bf16[1024,768]{1,0:T(8,128)(2,1)S(1)}, bf16[1024,768]{1,0:T(8,128)(2,1)}, u32[]{:S(2)}) copy-start(bf16[1024,768]{1,0:T(8,128)(2,1)} %param.6) | copy-start | bytes 4718596
  23.4 17.5 %copy-start.6 = (s32[1024]{0:T(1024)S(1)}, s32[1024]{0:T(1024)}, u32[]{:S(2)}) copy-start(s32[1024]{0:T(1024)} %param.7) | copy-start | bytes 12292
  23.4 22.3 %copy-start.7 = (s32[16]{0:T(128)S(1)}, s32[16]{0:T(128)}, u32[]{:S(2)}) copy-start(s32[16]{0:T(128)} %param.11) | copy-start | bytes 196
  23.4 22.8 %collective-permute-start.15 = (bf16[1024,512]{1,0:T(8,128)(2,1)S(1)}, bf16[1024,512]{1,0:T(8,128)(2,1)}, u32[]{:S(2)}, u32[]{:S(2)}) collective-permute-start(bf16[1024,512]{1,0:T(8,128)(2,1)S(1)} %get-tuple-element.8), channel_id=1, source_target_pairs={{0,1},{1,0},{2,3},{3,2},{4,5},{5,4},{6,7},{7,6},{8,9},{9,8},{10,11... | collective-permute-start | bytes 3145736 | tf_op jit(solution)/shard_map/ppermute | solution.py:144
  26.2 23.4 %collective-permute-start = (bf16[512,768]{1,0:T(8,128)(2,1)}, bf16[512,768]{1,0:T(8,128)(2,1)}, u32[]{:S(2)}, u32[]{:S(2)}) collective-permute-start(bf16[512,768]{1,0:T(8,128)(2,1)} %get-tuple-element.15), channel_id=1, source_target_pairs={{0,4},{15,11},{4,9},{11,6},{5,1},{10,14},{16,20},{31,27},{20,25},{... | collective-permute-start | bytes 2359304 | tf_op jit(solution)/shard_map/ppermute | solution.py:119
  40.7 23.8 %collective-permute-start.14 = (bf16[1024,512]{1,0:T(8,128)(2,1)}, bf16[1024,512]{1,0:T(8,128)(2,1)}, u32[]{:S(2)}, u32[]{:S(2)}) collective-permute-start(bf16[1024,512]{1,0:T(8,128)(2,1)} %get-tuple-element.9), channel_id=1, source_target_pairs={{0,2},{1,3},{2,0},{3,1},{4,6},{5,7},{6,4},{7,5},{8,10},{9,11},{10,... | collective-permute-start | bytes 3145736 | tf_op jit(solution)/shard_map/ppermute | solution.py:143
  40.9 20.1 %collective-permute-start.11 = (s32[1024]{0:T(1024)S(1)}, s32[1024]{0:T(1024)S(1)}, u32[]{:S(2)}, u32[]{:S(2)}) collective-permute-start(s32[1024]{0:T(1024)S(1)} %copy-done.6), channel_id=1, source_target_pairs={{0,1},{1,0},{2,3},{3,2},{4,5},{5,4},{6,7},{7,6},{8,9},{9,8},{10,11... | collective-permute-start | bytes 12296 | tf_op jit(solution)/shard_map/ppermute | solution.py:141
  45.6 47.8 %collective-permute-start.12 = (bf16[1024,512]{1,0:T(8,128)(2,1)}, bf16[1024,512]{1,0:T(8,128)(2,1)}, u32[]{:S(2)}, u32[]{:S(2)}) collective-permute-start(bf16[1024,512]{1,0:T(8,128)(2,1)} %get-tuple-element.7), channel_id=1, source_target_pairs={{0,1},{1,0},{2,3},{3,2},{4,5},{5,4},{6,7},{7,6},{8,9},{9,8},{10,11... | collective-permute-start | bytes 3145736 | tf_op jit(solution)/shard_map/ppermute | solution.py:145
  46.2 40.7 %collective-permute-start.16 = (bf16[1024,512]{1,0:T(8,128)(2,1)}, bf16[1024,512]{1,0:T(8,128)(2,1)}, u32[]{:S(2)}, u32[]{:S(2)}) collective-permute-start(bf16[1024,512]{1,0:T(8,128)(2,1)} %collective-permute-done.15), channel_id=1, source_target_pairs={{0,2},{1,3},{2,0},{3,1},{4,6},{5,7},{6,4},{7,5},{8,10},{9,11},{10,... | collective-permute-start | bytes 3145736 | tf_op jit(solution)/shard_map/ppermute | solution.py:146
  49.6 38.6 %collective-permute-start.1 = (bf16[512,768]{1,0:T(8,128)(2,1)}, bf16[512,768]{1,0:T(8,128)(2,1)}, u32[]{:S(2)}, u32[]{:S(2)}) collective-permute-start(bf16[512,768]{1,0:T(8,128)(2,1)} %collective-permute-done), channel_id=1, source_target_pairs={{4,8},{11,7},{9,13},{6,2},{20,24},{27,23},{25,29},{22,18}} | collective-permute-start | bytes 2359304 | tf_op jit(solution)/shard_map/ppermute | solution.py:120
  61.0 46.6 %collective-permute-start.9 = (bf16[768,512]{1,0:T(8,128)(2,1)}, bf16[768,512]{1,0:T(8,128)(2,1)S(1)}, u32[]{:S(2)}, u32[]{:S(2)}) collective-permute-start(bf16[768,512]{1,0:T(8,128)(2,1)} %get-tuple-element.13), channel_id=1, source_target_pairs={{0,1},{1,0},{2,3},{3,2},{4,5},{5,4},{6,7},{7,6},{8,9},{9,8},{10,11... | collective-permute-start | bytes 2359304 | tf_op jit(solution)/shard_map/ppermute | solution.py:155
  64.5 52.6 %collective-permute-start.8 = (bf16[768,512]{1,0:T(8,128)(2,1)}, bf16[768,512]{1,0:T(8,128)(2,1)S(1)}, u32[]{:S(2)}, u32[]{:S(2)}) collective-permute-start(bf16[768,512]{1,0:T(8,128)(2,1)} %get-tuple-element.12), channel_id=1, source_target_pairs={{0,1},{1,0},{2,3},{3,2},{4,5},{5,4},{6,7},{7,6},{8,9},{9,8},{10,11... | collective-permute-start | bytes 2359304 | tf_op jit(solution)/shard_map/ppermute | solution.py:156
  86.9 3.7 %collective-permute-start.13 = (s32[2048]{0:T(1024)S(1)}, s32[2048]{0:T(1024)S(1)}, u32[]{:S(2)}, u32[]{:S(2)}) collective-permute-start(s32[2048]{0:T(1024)S(1)} %constant_dynamic-update-slice_fusion.13), channel_id=1, source_target_pairs={{0,2},{1,3},{2,0},{3,1},{4,6},{5,7},{6,4},{7,5},{8,10},{9,11},{10,... | collective-permute-start | bytes 24584 | tf_op jit(solution)/shard_map/ppermute | solution.py:142
  88.2 5.2 %copy-start.5 = (bf16[1024,512]{1,0:T(8,128)(2,1)S(1)}, bf16[1024,512]{1,0:T(8,128)(2,1)}, u32[]{:S(2)}) copy-start(bf16[1024,512]{1,0:T(8,128)(2,1)} %get-tuple-element.6) | copy-start | bytes 3145732
  88.3 10.7 %collective-permute-start.2 = (bf16[512,768]{1,0:T(8,128)(2,1)}, bf16[512,768]{1,0:T(8,128)(2,1)S(1)}, u32[]{:S(2)}, u32[]{:S(2)}) collective-permute-start(bf16[512,768]{1,0:T(8,128)(2,1)} %collective-permute-done.1), channel_id=1, source_target_pairs={{8,12},{7,3},{24,28},{23,19}} | collective-permute-start | bytes 2359304 | tf_op jit(solution)/shard_map/ppermute | solution.py:121
  93.4 4.2 %copy-start.4 = (bf16[512,768]{1,0:T(8,128)(2,1)S(1)}, bf16[512,768]{1,0:T(8,128)(2,1)}, u32[]{:S(2)}) copy-start(bf16[512,768]{1,0:T(8,128)(2,1)} %get-tuple-element.14) | copy-start | bytes 2359300
  93.4 5.5 %copy-start.3 = (bf16[1024,768]{1,0:T(8,128)(2,1)S(1)}, bf16[1024,768]{1,0:T(8,128)(2,1)}, u32[]{:S(2)}) copy-start(bf16[1024,768]{1,0:T(8,128)(2,1)} %param.6) | copy-start | bytes 4718596
  97.7 9.9 %collective-permute-start.7 = (bf16[512,768]{1,0:T(8,128)(2,1)S(1)}, bf16[512,768]{1,0:T(8,128)(2,1)S(1)}, u32[]{:S(2)}, u32[]{:S(2)}) collective-permute-start(bf16[512,768]{1,0:T(8,128)(2,1)S(1)} %copy-done.4), channel_id=1, source_target_pairs={{0,1},{1,0},{2,3},{3,2},{4,5},{5,4},{6,7},{7,6},{8,9},{9,8},{10,11... | collective-permute-start | bytes 2359304 | tf_op jit(solution)/shard_map/ppermute | solution.py:152
  100.5 7.0 %collective-permute-start.6 = (bf16[512,768]{1,0:T(8,128)(2,1)S(1)}, bf16[512,768]{1,0:T(8,128)(2,1)S(1)}, u32[]{:S(2)}, u32[]{:S(2)}) collective-permute-start(bf16[512,768]{1,0:T(8,128)(2,1)S(1)} %add_select_fusion.1), channel_id=1, source_target_pairs={{0,1},{1,0},{2,3},{3,2},{4,5},{5,4},{6,7},{7,6},{8,9},{9,8},{10,11... | collective-permute-start | bytes 2359304 | tf_op jit(solution)/shard_map/ppermute | solution.py:152
  109.1 19.4 %collective-permute-start.17 = (bf16[1024,256]{1,0:T(8,128)(2,1)S(1)}, bf16[1024,256]{1,0:T(8,128)(2,1)S(1)}, u32[]{:S(2)}, u32[]{:S(2)}) collective-permute-start(bf16[1024,256]{1,0:T(8,128)(2,1)S(1)} %fusion.11), channel_id=1, source_target_pairs={{0,2},{1,3},{2,0},{3,1},{4,6},{5,7},{6,4},{7,5},{8,10},{9,11},{10,... | collective-permute-start | bytes 1572872 | tf_op jit(solution)/shard_map/ppermute | solution.py:170
  117.0 22.1 %collective-permute-start.10 = (bf16[1024,256]{1,0:T(8,128)(2,1)S(1)}, bf16[1024,256]{1,0:T(8,128)(2,1)S(1)}, u32[]{:S(2)}, u32[]{:S(2)}) collective-permute-start(bf16[1024,256]{1,0:T(8,128)(2,1)S(1)} %fusion.10), channel_id=1, source_target_pairs={{0,2},{1,3},{2,0},{3,1},{4,6},{5,7},{6,4},{7,5},{8,10},{9,11},{10,... | collective-permute-start | bytes 1572872 | tf_op jit(solution)/shard_map/ppermute | solution.py:170
  139.1 4.4 %slice-start = ((s8[6291456]{0:T(1024)(128)(4,1)}), s8[2097152]{0:T(1024)(128)(4,1)S(1)}, s32[]{:S(2)}) async-start(s8[6291456]{0:T(1024)(128)(4,1)} %bitcast.10), calls=%async_computation | async-start | bytes 4194304
  140.1 3.3 %slice-start.1 = ((s8[6291456]{0:T(1024)(128)(4,1)}), s8[4194304]{0:T(1024)(128)(4,1)S(1)}, s32[]{:S(2)}) async-start(s8[6291456]{0:T(1024)(128)(4,1)} %bitcast.10), calls=%async_computation.1 | async-start | bytes 8388608
  140.2 26.1 %collective-permute-start.18 = (bf16[2048,256]{1,0:T(8,128)(2,1)S(1)}, bf16[2048,256]{1,0:T(8,128)(2,1)S(1)}, u32[]{:S(2)}, u32[]{:S(2)}) collective-permute-start(bf16[2048,256]{1,0:T(8,128)(2,1)S(1)} %pad_maximum_fusion.4), channel_id=1, source_target_pairs={{0,1},{1,0},{2,3},{3,2},{4,5},{5,4},{6,7},{7,6},{8,9},{9,8},{10,11... | collective-permute-start | bytes 3145736 | tf_op jit(solution)/shard_map/ppermute | solution.py:174
  140.3 26.0 %collective-permute-start.20 = (bf16[2048,256]{1,0:T(8,128)(2,1)S(1)}, bf16[2048,256]{1,0:T(8,128)(2,1)S(1)}, u32[]{:S(2)}, u32[]{:S(2)}) collective-permute-start(bf16[2048,256]{1,0:T(8,128)(2,1)S(1)} %pad_maximum_fusion.4), channel_id=1, source_target_pairs={{0,2},{1,3},{2,0},{3,1},{4,6},{5,7},{6,4},{7,5},{8,10},{9,11},{10,... | collective-permute-start | bytes 3145736 | tf_op jit(solution)/shard_map/ppermute | solution.py:173
  142.2 24.8 %collective-permute-start.19 = (bf16[2048,256]{1,0:T(8,128)(2,1)S(1)}, bf16[2048,256]{1,0:T(8,128)(2,1)S(1)}, u32[]{:S(2)}, u32[]{:S(2)}) collective-permute-start(bf16[2048,256]{1,0:T(8,128)(2,1)S(1)} %pad_maximum_fusion.5), channel_id=1, source_target_pairs={{0,1},{1,0},{2,3},{3,2},{4,5},{5,4},{6,7},{7,6},{8,9},{9,8},{10,11... | collective-permute-start | bytes 3145736 | tf_op jit(solution)/shard_map/ppermute | solution.py:174
  142.4 45.9 %collective-permute-start.21 = (bf16[2048,256]{1,0:T(8,128)(2,1)S(1)}, bf16[2048,256]{1,0:T(8,128)(2,1)S(1)}, u32[]{:S(2)}, u32[]{:S(2)}) collective-permute-start(bf16[2048,256]{1,0:T(8,128)(2,1)S(1)} %pad_maximum_fusion.5), channel_id=1, source_target_pairs={{0,2},{1,3},{2,0},{3,1},{4,6},{5,7},{6,4},{7,5},{8,10},{9,11},{10,... | collective-permute-start | bytes 3145736 | tf_op jit(solution)/shard_map/ppermute | solution.py:173
  143.5 2.2 %slice-start.2 = ((s8[6291456]{0:T(1024)(128)(4,1)}), s8[4194304]{0:T(1024)(128)(4,1)S(1)}, s32[]{:S(2)}) async-start(s8[6291456]{0:T(1024)(128)(4,1)} %bitcast.12), calls=%async_computation.2 | async-start | bytes 8388608
  144.2 2.4 %slice-start.3 = ((s8[6291456]{0:T(1024)(128)(4,1)}), s8[2097152]{0:T(1024)(128)(4,1)S(1)}, s32[]{:S(2)}) async-start(s8[6291456]{0:T(1024)(128)(4,1)} %bitcast.12), calls=%async_computation.3 | async-start | bytes 4194304
  166.3 25.8 %collective-permute-start.22 = (bf16[2048,256]{1,0:T(8,128)(2,1)S(1)}, bf16[2048,256]{1,0:T(8,128)(2,1)S(1)}, u32[]{:S(2)}, u32[]{:S(2)}) collective-permute-start(bf16[2048,256]{1,0:T(8,128)(2,1)S(1)} %collective-permute-done.20), channel_id=1, source_target_pairs={{0,1},{1,0},{2,3},{3,2},{4,5},{5,4},{6,7},{7,6},{8,9},{9,8},{10,11... | collective-permute-start | bytes 3145736 | tf_op jit(solution)/shard_map/ppermute | solution.py:175
  188.4 5.2 %collective-permute-start.23 = (bf16[2048,256]{1,0:T(8,128)(2,1)S(1)}, bf16[2048,256]{1,0:T(8,128)(2,1)S(1)}, u32[]{:S(2)}, u32[]{:S(2)}) collective-permute-start(bf16[2048,256]{1,0:T(8,128)(2,1)S(1)} %collective-permute-done.21), channel_id=1, source_target_pairs={{0,1},{1,0},{2,3},{3,2},{4,5},{5,4},{6,7},{7,6},{8,9},{9,8},{10,11... | collective-permute-start | bytes 3145736 | tf_op jit(solution)/shard_map/ppermute | solution.py:175
  194.2 2.7 %copy-start.1 = (f32[768,2048]{1,0:T(8,128)}, f32[768,2048]{1,0:T(8,128)S(1)}, u32[]{:S(2)}) copy-start(f32[768,2048]{1,0:T(8,128)S(1)} %get-tuple-element.30) | copy-start | bytes 18874372
  197.0 2.7 %copy-start = (f32[768,2048]{1,0:T(8,128)}, f32[768,2048]{1,0:T(8,128)S(1)}, u32[]{:S(2)}) copy-start(f32[768,2048]{1,0:T(8,128)S(1)} %fusion.17) | copy-start | bytes 18874372

commit v2 on v1

v2 whole, which is shorter than its diff:
```python
import functools

import jax
import jax.numpy as jnp
from jax import lax
from jax.experimental import pallas as pl
from jax.experimental.pallas import tpu as pltpu
from jax.sharding import PartitionSpec as P

F32 = jnp.float32
BF16 = jnp.bfloat16


def hashed_noise(rows, cols, salt_value, full_ff):
    value = rows * full_ff + cols
    mixed = jnp.bitwise_xor(value, salt_value)
    mixed = mixed * 73244475
    mixed = jnp.bitwise_xor(mixed, jnp.right_shift(jnp.bitwise_and(mixed, 2147483647), 16))
    mixed = mixed * 73244475
    mixed = jnp.bitwise_xor(mixed, jnp.right_shift(jnp.bitwise_and(mixed, 2147483647), 16))
    kept = jnp.right_shift(jnp.bitwise_and(mixed, 2147483647), 7).astype(jnp.float32)
    return 1.7320508075688772 * (2.0 * (kept + 0.5) / 16777216.0 - 1.0)


def sample_block(mean_rows, prec_rows, row_start, col_start, salt_rows, full_ff, inv_root):
    rows = row_start + jnp.arange(mean_rows.shape[0], dtype=jnp.int32)[:, None]
    cols = col_start + jnp.arange(mean_rows.shape[1], dtype=jnp.int32)[None, :]
    noise = hashed_noise(rows, cols, salt_rows, full_ff)
    theta = mean_rows + 0.5 * noise / jnp.sqrt(prec_rows + 0.1)
    return (theta * inv_root).astype(BF16)


def dot(a, b):
    return jnp.dot(a, b, preferred_element_type=F32)


def dot_t(a, b):
    return lax.dot_general(a, b, (((0,), (0,)), ((), ())), preferred_element_type=F32)


def square(a):
    wide = a.astype(F32)
    return (wide * wide).astype(BF16)


def one_hot(idx, n_rows):
    return (idx[:, None] == jnp.arange(n_rows, dtype=jnp.int32)[None, :]).astype(BF16)


def row_sums(idx, go, n_rows):
    hot = one_hot(idx, n_rows)
    return dot_t(hot, go), dot_t(hot, square(go))


def slopes(pre, total, total_sq):
    sig = jax.nn.sigmoid(pre)
    h = sig * (1.0 + pre * (1.0 - sig))
    return (h * total).astype(BF16), (h * h * total_sq).astype(BF16)


def update(grad, sq_sum, mean, precision):
    new_precision = 0.7 * precision + 0.3 * sq_sum
    new_mean = mean - 0.5 * (grad + 0.1 * mean) / (new_precision + 0.1)
    return new_mean, new_precision


def own_sample(mean, precision, block_salts, dp_pos, shard_pos, n_shard, width):
    rows_blk, cols_blk = mean.shape
    inv_root = 1.0 / jnp.sqrt(F32(width))
    salt = lax.dynamic_index_in_dim(block_salts, dp_pos * n_shard + shard_pos, 0, keepdims=False)
    return sample_block(
        mean, precision, dp_pos * rows_blk, shard_pos * cols_blk, salt, cols_blk * n_shard, inv_root
    )


def general(table, indices, grad_out, mean, precision, block_salts):
    n_dp, n_shard = lax.axis_size("dp"), lax.axis_size("shard")
    dp_pos, shard_pos = lax.axis_index("dp"), lax.axis_index("shard")
    n_rows, width = table.shape[0], table.shape[1] * n_shard
    rows_blk = mean.shape[0]
    whole = lax.all_gather(table, "shard", axis=1, tiled=True)
    tab = lax.dynamic_slice_in_dim(whole, dp_pos * rows_blk, rows_blk, 1)
    weight = own_sample(mean, precision, block_salts, dp_pos, shard_pos, n_shard, width)
    pre = lax.psum_scatter(dot(tab, weight), "dp", scatter_dimension=1, tiled=True)
    go = lax.all_to_all(grad_out, "dp", 1, 0, tiled=True)
    idx = lax.all_gather(indices, "dp", axis=0, tiled=True)
    s, s2 = slopes(pre, *row_sums(idx, go, n_rows))
    s = lax.all_gather(s, "dp", axis=1, tiled=True)
    s2 = lax.all_gather(s2, "dp", axis=1, tiled=True)
    grad = dot_t(tab, s) * (1.0 / jnp.sqrt(F32(width)))
    sq_sum = dot_t(square(tab), s2) * (1.0 / F32(width))
    return update(grad, sq_sum, mean, precision)


CORE = [(j, j ^ 1) for j in range(4)]
CHIP = [(j, j ^ 2) for j in range(4)]
CROSS = [(j, j ^ 3) for j in range(4)]


def table_moves():
    near = [((0, 0), (1, 0)), ((0, 1), (2, 0)), ((1, 0), (0, 1)), ((1, 1), (2, 1))]
    far = [((0, 0), (3, 0)), ((1, 0), (3, 1))]
    both = []
    for moves in (near, far):
        pairs = []
        for (z, d), (z2, d2) in moves:
            pairs.append((z * 4 + d, z2 * 4 + d2))
            pairs.append(((3 - z) * 4 + 3 - d, (3 - z2) * 4 + 3 - d2))
        both.append(pairs)
    return both


TILE = 256
VMEM_LIMIT = 60 * 1024 * 1024
FINAL_LIMIT = 28 * 1024 * 1024


def call(kernel, scalars, grid, ins, outs, deps=(), scratch=(), alias=None, limit=VMEM_LIMIT, cost=(1, 1)):
    n_in, n_out, n_dep = len(ins), len(outs), len(deps)

    def body(*refs):
        sc = refs[0]
        in_refs = refs[1 : 1 + n_in]
        rest = refs[1 + n_in + n_dep :]
        kernel(sc, in_refs, rest[:n_out], rest[n_out:])

    in_specs = [pl.BlockSpec(b, m) for _, b, m in ins]
    in_specs += [pl.BlockSpec(memory_space=pl.ANY)] * n_dep
    got = pl.pallas_call(
        body,
        grid_spec=pltpu.PrefetchScalarGridSpec(
            num_scalar_prefetch=1,
            grid=grid,
            in_specs=in_specs,
            out_specs=[pl.BlockSpec(b, m) for _, _, b, m in outs],
            scratch_shapes=list(scratch),
        ),
        out_shape=[jax.ShapeDtypeStruct(s, d) for s, d, _, _ in outs],
        input_output_aliases={1 + n_in + i: o for i, o in (alias or {}).items()},
        compiler_params=pltpu.CompilerParams(vmem_limit_bytes=VMEM_LIMIT),
        cost_estimate=pl.CostEstimate(flops=cost[0], bytes_accessed=cost[1], transcendentals=0),
    )(scalars, *[a for a, _, _ in ins], *deps)
    return got


def after(x, *deps):
    return lax.optimization_barrier((x, *deps))[0]


def sample_parts(scal, mean, precision, part, full_ff, width, deps=()):
    rows, _ = mean.shape
    step, strip = rows // 2, 16
    flips = (3, 1, 2, 0)
    inv_root = 1.0 / (width ** 0.5)

    def flip_of(g):
        return jnp.where(g == 0, flips[0], jnp.where(g == 1, flips[1], jnp.where(g == 2, flips[2], flips[3])))

    def kernel(sc, ins, outs, scratch):
        g, r = pl.program_id(0), pl.program_id(1)
        start = (sc[2] + r * step) * full_ff + sc[3] + (sc[0] ^ flip_of(g)) * part
        salt = sc[1]
        base = (
            lax.broadcasted_iota(jnp.int32, (strip, part), 0) * full_ff
            + lax.broadcasted_iota(jnp.int32, (strip, part), 1)
        )

        def strip_of(n):
            at = pl.ds(pl.multiple_of(n * strip, strip), strip)
            mixed = (base + (start + n * (strip * full_ff))) ^ salt
            mixed = mixed * 73244475
            mixed = mixed ^ ((mixed & 2147483647) >> 16)
            mixed = mixed * 73244475
            mixed = mixed ^ ((mixed & 2147483647) >> 16)
            kept = ((mixed & 2147483647) >> 7).astype(F32)
            noise = 1.7320508075688772 * (2.0 * (kept + 0.5) / 16777216.0 - 1.0)
            theta = ins[0][at, :] + 0.5 * noise * lax.rsqrt(ins[1][at, :] + 0.1)
            return at, (theta * inv_root).astype(BF16)

        for m in range(4):
            @pl.when(g == m)
            def _(m=m):
                @pl.loop(0, step // strip)
                def _(n):
                    at, w = strip_of(n)
                    outs[m][at, :] = w

    last = rows // step - 1
    block = (step, part)
    source = lambda g, r, sc: (r, sc[0] ^ flip_of(g))

    def target(m):
        return lambda g, r, sc: (jnp.where(g == m, r, jnp.where(g < m, 0, last)), 0)

    return call(
        kernel, scal, (4, rows // step),
        [(mean, block, source), (precision, block, source)],
        [((rows, part), BF16, block, target(m)) for m in range(4)],
        deps,
    )


def sum_rows(scal, groups, n_rows, part, before=None, deps=()):
    ins = []
    for idx, go, flip in groups:
        count = idx.shape[0]
        ins.append((idx.reshape(1, count), (1, count), lambda i, sc: (0, 0)))
        if flip is None:
            ins.append((go, (count, part), lambda i, sc: (0, 0)))
        else:
            ins.append((go, (count, part), lambda i, sc, f=flip: (0, sc[0] ^ f)))
    n = len(groups)
    tile = (TILE, part)
    if before is not None:
        ins += [(b, tile, lambda i, sc: (i, 0)) for b in before]

    def kernel(sc, ins, outs, scratch):
        i = pl.program_id(0)

        @pl.when(i == 0)
        def _():
            for g in range(n):
                @pl.loop(0, ins[2 * g + 1].shape[0] // 64)
                def _(k):
                    at = pl.ds(pl.multiple_of(k * 64, 64), 64)
                    wide = ins[2 * g + 1][at, :].astype(F32)
                    scratch[g][at, :] = (wide * wide).astype(BF16)

        start = lax.rem(i * TILE + sc[4], n_rows)
        total = total_sq = None
        if before is not None:
            total, total_sq = ins[2 * n][...], ins[2 * n + 1][...]
        for g in range(n):
            idx = ins[2 * g][...]
            row = start + lax.broadcasted_iota(jnp.int32, (TILE, idx.shape[1]), 0)
            hot = jnp.where(row == idx, 1.0, 0.0).astype(BF16)
            a, b = dot(hot, ins[2 * g + 1][...]), dot(hot, scratch[g][...])
            total = a if total is None else total + a
            total_sq = b if total_sq is None else total_sq + b
        outs[0][...] = total
        outs[1][...] = total_sq

    return call(
        kernel, scal, (n_rows // TILE,), ins,
        [((n_rows, part), F32, tile, lambda i, sc: (i, 0))] * 2,
        deps, scratch=[pltpu.VMEM((idx.shape[0], part), BF16) for idx, _, _ in groups],
    )


def final(scal, tab_t, tab_t_sq, pieces, mean, precision, part, width, before):
    rows, half = tab_t[0].shape
    cut = pieces[0][0][0][0].shape[1]
    n = len(pieces)
    inv_root, inv_width = 1.0 / (width ** 0.5), 1.0 / width

    def kernel(sc, ins, outs, scratch):
        for m in range(n):
            @pl.when(pl.program_id(0) == m)
            def _(m=m):
                sa, qa, sb, qb = ins[6 + 4 * m : 10 + 4 * m]
                grad = dot(ins[0][...], sa[...]) + dot(ins[1][...], sb[...])
                sq_sum = dot(ins[2][...], qa[...]) + dot(ins[3][...], qb[...])
                outs[0][...], outs[1][...] = update(grad * inv_root, sq_sum * inv_width, ins[4][...], ins[5][...])

    def place(p, sc):
        at = [(sc[0] ^ flip) * part + start for _, flip, start in pieces]
        out = at[0]
        for m in range(1, n):
            out = jnp.where(p == m, at[m], out)
        return 0, pl.multiple_of(out, 128)

    whole = lambda p, sc: (0, 0)
    block = (pl.Element(rows), pl.Element(cut))
    slots = [slot for quads, _, _ in pieces for slot in quads]
    return call(
        kernel, scal, (n,),
        [(a, a.shape, whole) for a in (*tab_t, *tab_t_sq)]
        + [(mean, block, place), (precision, block, place)]
        + [(s, (half, cut), lambda p, sc, h=h: (h, 0)) for s, h in slots],
        [(mean.shape, F32, block, place)] * 2,
        tuple(before),
        alias={0: 0, 1: 1} if before else None,
        limit=FINAL_LIMIT,
    )


def on_device(table, indices, grad_out, mean, precision, block_salts):
    n_shard = lax.axis_size("shard")
    dp_pos, shard_pos = lax.axis_index("dp"), lax.axis_index("shard")
    member = lax.axis_index("members")
    n_rows, width = table.shape[0], table.shape[1] * n_shard
    rows_blk, cols_blk = mean.shape
    count = indices.shape[0]
    part = cols_blk // 4
    half, few, most = n_rows // 2, count // 2, count * 3 // 4
    salt = lax.dynamic_index_in_dim(block_salts, dp_pos * n_shard + shard_pos, 0, keepdims=False)
    scal = jnp.stack([dp_pos, salt, dp_pos * rows_blk, shard_pos * cols_blk, member * half]).astype(jnp.int32)
    both = ("shard", "dp")
    to_near, to_far = table_moves()
    sync = lax.optimization_barrier

    def cols(a, flip, row, rows):
        return lax.dynamic_slice(a, (row, (dp_pos ^ flip) * part), (rows, part))

    idx_core, idx_chip, idx_cross = (lax.ppermute(indices, "dp", p) for p in (CORE, CHIP, CROSS))
    own_a = lax.dynamic_slice_in_dim(table, member * half, half, 0)
    near_a = lax.ppermute(own_a, both, to_near)
    far_a = lax.ppermute(own_a, both, to_far)
    x1 = cols(after(grad_out, own_a), 2, 0, count)
    x1, idx_core, idx_chip, idx_cross = sync((x1, idx_core, idx_chip, idx_cross))
    x1_in = lax.ppermute(x1, "dp", CHIP)
    x2 = cols(after(grad_out, x1), 3, 0, most)
    x2_in = lax.ppermute(x2, "dp", CROSS)
    go1 = after(grad_out, x2)
    go_mine = [cols(go1, 1, r, few) for r in (0, few)]
    go_core = [lax.ppermute(g, "dp", CORE) for g in go_mine]
    w_far_send, w_near_send, w_far, w_near = sample_parts(
        scal, mean, precision, part, cols_blk * n_shard, width, go_core
    )
    groups = [(indices, grad_out, 0), (idx_core[:few], go_core[0], None), (idx_core[few:], go_core[1], None)]
    sums = sum_rows(scal, groups, n_rows, part, None, [w_near])
    x3 = cols(after(grad_out, *sums), 3, most, count - most)
    x1_in, x2_in, near_a, far_a, w_far_send, w_near_send, w_far, w_near, s0, s1, x3 = sync(
        (x1_in, x2_in, near_a, far_a, w_far_send, w_near_send, w_far, w_near, *sums, x3)
    )
    tab_a = jnp.where(shard_pos == dp_pos, own_a, near_a + far_a)
    tab_b = lax.ppermute(tab_a, "members", [(0, 1), (1, 0)])
    core_a = lax.ppermute(tab_a, "dp", CORE)
    w_core_far = lax.ppermute(w_far_send, "dp", CORE)
    w_core_near = lax.ppermute(w_near_send, "dp", CORE)
    out_a = (dot(tab_a, w_far) + dot(core_a, w_core_far)).astype(BF16)
    pre_a = lax.ppermute(out_a, "dp", CHIP)
    own_pre_a = dot(after(tab_a, out_a), w_near) + dot(core_a, w_core_near)
    x3_in = lax.ppermute(x3, "dp", CROSS)
    groups = [(idx_chip, x1_in, None), (idx_cross[:most], x2_in, None), (idx_cross[most:], x3_in, None)]
    sums = sum_rows(scal, groups, n_rows, part, (s0, s1), [own_pre_a])
    pre_a, tab_b, s0, s1 = sync((pre_a, tab_b, *sums))
    quarter = half // 2
    core_b = [lax.ppermute(t, "dp", CORE) for t in (tab_b[:quarter], tab_b[quarter:])]
    core_b = jnp.concatenate(core_b, 0)
    out_b = (dot(tab_b, w_far) + dot(core_b, w_core_far)).astype(BF16)
    pre_b = lax.ppermute(out_b, "dp", CHIP)
    pre_a, pb = after(pre_a, out_b), after(tab_b, out_b)
    own_pre_b = dot(pb, w_near) + dot(core_b, w_core_near)

    cut = part // 2
    starts = (0, cut)

    def slopes_of(f, n, h, k):
        r, c = slice(h * half, (h + 1) * half), slice(starts[k], starts[k] + cut)
        return slopes(f[:, c].astype(F32) + n[:, c], s0[r, c], s1[r, c])

    send_a = jnp.concatenate([*slopes_of(pre_a, own_pre_a, 0, 0), *slopes_of(pre_a, own_pre_a, 0, 1)], 0)
    far_a = lax.ppermute(send_a, "dp", CHIP)
    pre_b, send_a, own_pre_b = sync((pre_b, send_a, own_pre_b))
    b0 = slopes_of(pre_b, own_pre_b, 1, 0)
    last = jnp.concatenate(slopes_of(after(pre_b, *b0), own_pre_b, 1, 1), 0)

    far_b0 = [lax.ppermute(s, "dp", CHIP) for s in b0]
    far_last = lax.ppermute(last, "dp", CHIP)
    core_a2 = lax.ppermute(send_a, "dp", CORE)
    core_b0 = [lax.ppermute(s, "dp", CORE) for s in b0]
    core_last = lax.ppermute(last, "dp", CORE)
    t0, t1 = after(tab_a, last).T, after(tab_b, last).T
    tab_t, tab_t_sq = (t0, t1), (square(t0), square(t1))

    def write(outs, *pieces):
        return final(scal, tab_t, tab_t_sq, pieces, mean, precision, part, width, outs)

    def chunk0(a, b, flip):
        return [(a, 0), (a, 1), (b[0], 0), (b[1], 0)], flip, starts[0]

    def chunk1(a, b, flip):
        return [(a, 2), (a, 3), (b, 0), (b, 1)], flip, starts[1]

    outs = write(
        (), chunk0(send_a, b0, 0), chunk1(send_a, last, 0), chunk0(core_a2, core_b0, 1), chunk1(core_a2, core_last, 1)
    )
    far_a, far_b0 = after(far_a, *outs), [after(s, *outs) for s in far_b0]
    fwd_a = lax.ppermute(far_a, "dp", CORE)
    fwd_b0 = [lax.ppermute(s, "dp", CORE) for s in far_b0]
    outs = write(outs, chunk0(far_a, far_b0, 2), chunk0(fwd_a, fwd_b0, 3))
    far_last = after(far_last, *outs)
    fwd_last = lax.ppermute(far_last, "dp", CORE)
    outs = write(outs, chunk1(far_a, far_last, 2), chunk1(fwd_a, fwd_last, 3))
    return tuple(outs)


def solution(mesh):
    in_specs = (
        P(None, "shard"),
        P(("members", "dp")),
        P(("members", "dp"), "shard"),
        P(("members", "dp"), "shard"),
        P(("members", "dp"), "shard"),
        P("members"),
    )
    out_specs = (P(("members", "dp"), "shard"), P(("members", "dp"), "shard"))
    fits = mesh.shape["dp"] == 4 and mesh.shape["shard"] == 4
    return jax.shard_map(
        on_device if fits else general,
        mesh=mesh,
        in_specs=in_specs,
        out_specs=out_specs,
        check_vma=False,
    )
```

time: 200 us -> 155 us (0.78)
  Pallas kernels: 0 us -> 56.4 us
  waiting for transfers between devices: 91.5 us -> 44.2 us
  matrix products: 29.7 us -> 6.61 us
  starting transfers between devices: 46.4 us -> 24.2 us
  other arithmetic: 13.8 us -> 4.15 us
    pallas_call x0 -> x6, Pallas kernels: none -> 56.4 us  [call(): pl.pallas_call(body, grid_spec=pltpu.PrefetchScalarGridSpec(num_scalar_pr...]
    ppermute x24 -> x30, waiting for transfers between devices: 91.5 us -> 44.2 us  [the longest x2 12.3 us: on_device(): far_b0 = [lax.ppermute(s, 'dp', CHIP) for s in b0]]
    dot_general x20 -> x0, matrix products: 25.1 us -> none  [dot_t(): lax.dot_general(a, b, (((0,), (0,)), ((), ())), preferred_element_type=F32)]
    ppermute x24 -> x30, starting transfers between devices: 46.4 us -> 24.2 us  [the longest x1 6.8 us: on_device(): far_a = lax.ppermute(own_a, both, to_far)]
    convert_element_type x1, other arithmetic: 8.36 us -> 1.47 us  [square(): return (wide * wide).astype(BF16)]
    select_n x2 -> x1, other arithmetic: 4.31 us -> 1.49 us  [on_device(): tab_a = jnp.where(shard_pos == dp_pos, own_a, near_a + far_a)]
    dot_general x6 -> x8, matrix products: 4.58 us -> 6.61 us  [dot(): return jnp.dot(a, b, preferred_element_type=F32)]
    dynamic_slice x3 -> x6, local copies, waits for them, and re-layouts: 6.02 us -> 7.25 us  [the longest x4 6.54 us: cols(): return lax.dynamic_slice(a, (row, (dp_pos ^ flip) * part), (rows, part))]
  transfers between devices with their start and end apart: 24 -> 30, of which waited for: 9 -> 16; matrix products, arithmetic and copies ran while one was open for 26% -> 9% of each run, Pallas kernels for 0% -> 32%
where the time goes in v2:
time: 155 us; the launch traced here: 154 us
  Pallas kernels  56.4 us (36%)
  waiting for transfers between devices  44.2 us (29%)
  starting transfers between devices  24.2 us (16%)
  local copies, waits for them, and re-layouts  17.4 us (11%)
  matrix products  6.61 us (4%)
  other arithmetic  4.15 us (3%)
    pallas_call x6, Pallas kernels, call(): pl.pallas_call(body, grid_spec=pltpu.PrefetchScalarGridSpec(num_scalar_pr...  56.4 us
    ppermute x2, waiting for transfers between devices, on_device(): far_b0 = [lax.ppermute(s, 'dp', CHIP) for s in b0]  12.3 us
    ppermute x1, waiting for transfers between devices, on_device(): pre_b = lax.ppermute(out_b, 'dp', CHIP)  10.1 us
    unnamed x76, local copies, waits for them, and re-layouts  7.01 us
    ppermute x1, starting transfers between devices, on_device(): far_a = lax.ppermute(own_a, both, to_far)  6.8 us
    dot_general x8, matrix products, dot(): return jnp.dot(a, b, preferred_element_type=F32)  6.61 us
    dynamic_slice x4, local copies, waits for them, and re-layouts, cols(): return lax.dynamic_slice(a, (row, (dp_pos ^ flip) * part), (rows, part))  6.54 us
    ppermute x1, waiting for transfers between devices, on_device(): x2_in = lax.ppermute(x2, 'dp', CROSS)  5.6 us
  transfers between devices with their start and end apart: 30, of which 16 were waited for; matrix products, arithmetic and copies ran while one was open for 9% of the time, Pallas kernels for 32%

profile of v2, /device:TPU:0, one launch (start us, length us, event | category | flops | bytes accessed | tf_op | source)
XLA Modules:
  0.0 154.2 jit_solution(5279882029437581064)
XLA Ops:
  0.6 3.0 %collective-permute-start.1 = (s32[1024]{0:T(1024)}, s32[1024]{0:T(1024)S(1)}, u32[]{:S(2)}, u32[]{:S(2)}) collective-permute-start(s32[1024]{0:T(1024)} %param.7), channel_id=1, source_target_pairs={{0,2},{1,3},{2,0},{3,1},{4,6},{5,7},{6,4},{7,5},{8,10},{9,11},{10,... | collective-permute-start | bytes 12296 | tf_op jit(solution)/shard_map/ppermute | solution.py:305
  4.2 1.3 constant_dynamic-slice_fusion.2
  5.6 1.3 collective-permute-done.2
  6.9 2.1 %constant_dynamic-slice_fusion.1 = bf16[768,512]{1,0:T(8,128)(2,1)} fusion(bf16[1024,2048]{1,0:T(8,128)(2,1)} %refs_2_.3, s32[]{:T(128)S(6)} %select_n.30), kind=kLoop, calls=%fused_computation.28 | loop fusion | bytes 1572868 | tf_op jit(solution)/shard_map/dynamic_slice | solution.py:303
  9.0 2.1 %constant_dynamic-slice_fusion.4 = (bf16[512,512]{1,0:T(8,128)(2,1)S(1)}, bf16[512,512]{1,0:T(8,128)(2,1)}) fusion(bf16[1024,2048]{1,0:T(8,128)(2,1)} %refs_2_.3, s32[]{:T(128)S(6)} %select_n.31), kind=kLoop, calls=%fused_computation.31 | loop fusion | bytes 2097156 | tf_op jit(solution)/shard_map/dynamic_slice | solution.py:303
  11.1 0.5 collective-permute-start.8
  11.7 6.8 %collective-permute-start.6 = (bf16[512,768]{0,1:T(8,128)(2,1)S(1)}, bf16[512,768]{0,1:T(8,128)(2,1)}, u32[]{:S(2)}, u32[]{:S(2)}) collective-permute-start(bf16[512,768]{0,1:T(8,128)(2,1)S(1)} %copy.13), channel_id=1, source_target_pairs={{0,12},{15,3},{4,13},{11,2},{16,28},{31,19},{20,29},{27,18}} | collective-permute-start | bytes 2359304 | tf_op jit(solution)/shard_map/ppermute | solution.py:308
  18.5 2.8 %collective-permute-start.5 = (bf16[512,768]{0,1:T(8,128)(2,1)S(1)}, bf16[512,768]{0,1:T(8,128)(2,1)}, u32[]{:S(2)}, u32[]{:S(2)}) collective-permute-start(bf16[512,768]{0,1:T(8,128)(2,1)S(1)} %copy.13), channel_id=1, source_target_pairs={{0,4},{15,11},{1,8},{14,7},{4,1},{11,14},{5,9},{10,6},{16,20},{31,... | collective-permute-start | bytes 2359304 | tf_op jit(solution)/shard_map/ppermute | solution.py:307
  21.4 0.7 dynamic_slice.22
  22.1 1.3 stack.20.refs_0_
  23.4 0.6 fusion.3
  24.0 0.8 copy-done.22
  24.8 12.5 %shard_map.77 = (bf16[768,512]{1,0:T(8,128)(2,1)}, bf16[768,512]{1,0:T(8,128)(2,1)}, bf16[768,512]{1,0:T(8,128)(2,1)}, bf16[768,512]{1,0:T(8,128)(2,1)}) custom-call(s32[5]{0:T(128)} %stack.20.refs_0_, f32[768,2048]{1,0:T(8,128)} %refs_5_.5, f32[768,2048]{1,0:T(8,128)} %refs_6_.5, bf16[512,512]{1,0:T(8,128)(2,1)} %copy-done.22, bf16[512,512]{1,0:T(8,128)(2,1)} %copy-done.21), custom_call_target="tpu_custom_call" | custom-call | flops 1 | bytes 1 | tf_op jit(solution)/shard_map/pallas_call | solution.py:129
  37.3 8.6 %shard_map.78 = (f32[1024,512]{1,0:T(8,128)}, f32[1024,512]{1,0:T(8,128)}) custom-call(s32[5]{0:T(128)} %stack.20.refs_0_, s32[1,1024]{1,0:T(1,128)} %bitcast.39, bf16[1024,2048]{1,0:T(8,128)(2,1)} %refs_2_.3, s32[1,512]{1,0:T(1,128)} %bitcast.37, bf16[512,512]{1,0:T(8,128)(2,1)} %copy-done.22, s32[1,512]{1,0:T(1,128)} %bitcast.36, ...), custom_call_target="tpu_custom_call" | custom-call | flops 1 | bytes 1 | tf_op jit(solution)/shard_map/pallas_call | solution.py:129
  45.9 1.1 constant_dynamic-slice_fusion.5
  47.0 5.6 %collective-permute-done.4.refs_4_ = bf16[768,512]{1,0:T(8,128)(2,1)} collective-permute-done((bf16[768,512]{1,0:T(8,128)(2,1)}, bf16[768,512]{1,0:T(8,128)(2,1)}, u32[]{:S(2)}, u32[]{:S(2)}) %collective-permute-start.4) | collective-permute-done | bytes 786464 | tf_op jit(solution)/shard_map/ppermute | solution.py:313
  52.6 1.5 add_select_fusion
  54.1 0.9 collective-permute-start.9
  55.1 0.4 collective-permute-start.14
  55.5 0.6 slice.69
  56.1 0.6 reshape.26.refs_3_
  56.7 1.5 collective-permute-start.12
  58.2 0.6 fusion.4
  58.8 1.4 fusion
  60.2 1.4 collective-permute-start.11
  61.7 0.6 fusion.5
  62.3 1.6 %convolution_add_fusion.2.refs_9_ = f32[512,512]{1,0:T(8,128)} fusion(f32[512,512]{1,0:T(8,128)S(1)} %fusion.5, bf16[512,768]{0,1:T(8,128)(2,1)S(1)} %add_select_fusion, bf16[768,512]{1,0:T(8,128)(2,1)S(1)} %copy-done.9), kind=kOutput, calls=%fused_computation.4 | convolution fusion | flops 402915328 | bytes 3670016 | tf_op jit(solution)/shard_map/dot_general | solution.py:34
  63.9 2.9 %collective-permute-done.13.refs_6_ = bf16[256,512]{1,0:T(8,128)(2,1)S(1)} collective-permute-done((bf16[256,512]{1,0:T(8,128)(2,1)S(1)}, bf16[256,512]{1,0:T(8,128)(2,1)S(1)}, u32[]{:S(2)}, u32[]{:S(2)}) %collective-permute-start.13) | collective-permute-done | bytes 262176 | tf_op jit(solution)/shard_map/ppermute | solution.py:334
  66.8 0.7 copy-done.32
  67.5 9.3 %shard_map.79 = (f32[1024,512]{1,0:T(8,128)}, f32[1024,512]{1,0:T(8,128)}) custom-call(s32[5]{0:T(128)} %stack.20.refs_0_, s32[1,1024]{1,0:T(1,128)} %bitcast.40, bf16[1024,512]{1,0:T(8,128)(2,1)} %collective-permute-done.3.refs_2_, s32[1,768]{1,0:T(1,128)} %reshape.26.refs_3_, bf16[768,512]{1,0:T(8,128)(2,1)} %collective-permute-done.4.refs_4_, ...), custom_call_target="tpu_custom_call" | custom-call | flops 1 | bytes 1 | tf_op jit(solution)/shard_map/pallas_call | solution.py:129
  76.8 1.2 collective-permute-done.11
  78.2 0.4 collective-permute-start.16
  78.6 1.2 collective-permute-done.15
  79.9 0.5 collective-permute-done.16
  80.5 0.6 fusion.6
  81.1 0.6 fusion.1
  81.7 0.7 collective-permute-start.17
  82.4 0.7 copy-done.19
  83.1 0.6 multiply_convert_fusion.9
  83.8 0.7 collective-permute-start.18
  84.5 0.6 copy-done.15
  85.1 0.6 fusion.7
  85.8 0.6 convolution_add_fusion
  86.4 10.1 %collective-permute-done.17 = bf16[512,512]{1,0:T(8,128)(2,1)S(1)} collective-permute-done((bf16[512,512]{1,0:T(8,128)(2,1)S(1)}, bf16[512,512]{1,0:T(8,128)(2,1)S(1)}, u32[]{:S(2)}, u32[]{:S(2)}) %collective-permute-start.17) | collective-permute-done | bytes 524320 | tf_op jit(solution)/shard_map/ppermute | solution.py:342
  97.1 0.6 collective-permute-start.22
  97.8 0.4 collective-permute-start.20
  98.2 1.5 multiply_convert_fusion
  99.7 0.6 collective-permute-done.21.refs_18_
  100.7 1.0 copy-done.7
  101.9 11.5 %shard_map.80 = (f32[768,2048]{1,0:T(8,128)}, f32[768,2048]{1,0:T(8,128)}) custom-call(s32[5]{0:T(128)} %stack.20.refs_0_, bf16[768,512]{1,0:T(8,128)(2,1)} %bitcast.33, bf16[768,512]{1,0:T(8,128)(2,1)} %bitcast.30, bf16[768,512]{1,0:T(8,128)(2,1)} %get-tuple-element.115.refs_3_, bf16[768,512]{1,0:T(8,128)(2,1)} %get-tuple-element.114.refs_4_, ...), custom_call_target="tpu_custom_call" | custom-call | flops 1 | bytes 1 | tf_op jit(solution)/shard_map/pallas_call | solution.py:129
  113.4 4.7 %collective-permute-done.18.refs_7_.refs_8_ = bf16[2048,256]{1,0:T(8,128)(2,1)S(1)} collective-permute-done((bf16[2048,256]{1,0:T(8,128)(2,1)S(1)}, bf16[2048,256]{1,0:T(8,128)(2,1)S(1)}, u32[]{:S(2)}, u32[]{:S(2)}) %collective-permute-start.18) | collective-permute-done | bytes 1048608 | tf_op jit(solution)/shard_map/ppermute | solution.py:354
  118.2 0.6 collective-permute-start.25
  118.8 1.4 collective-permute-start.24
  120.2 0.6 collective-permute-start.23
  120.8 6.7 %collective-permute-done.25.refs_10_ = bf16[512,256]{1,0:T(8,128)(2,1)S(1)} collective-permute-done((bf16[512,256]{1,0:T(8,128)(2,1)}, bf16[512,256]{1,0:T(8,128)(2,1)S(1)}, u32[]{:S(2)}, u32[]{:S(2)}) %collective-permute-start.25) | collective-permute-done | bytes 262176 | tf_op jit(solution)/shard_map/ppermute | solution.py:359
  127.5 5.6 %collective-permute-done.24.refs_9_ = bf16[512,256]{1,0:T(8,128)(2,1)S(1)} collective-permute-done((bf16[512,256]{1,0:T(8,128)(2,1)S(1)}, bf16[512,256]{1,0:T(8,128)(2,1)S(1)}, u32[]{:S(2)}, u32[]{:S(2)}) %collective-permute-start.24) | collective-permute-done | bytes 262176 | tf_op jit(solution)/shard_map/ppermute | solution.py:359
  133.1 0.5 collective-permute-start.28
  133.6 1.0 collective-permute-done.27.refs_13_
  135.0 0.7 copy-done.31
  135.8 1.0 copy-done.6
  136.7 7.2 %shard_map.81 = (f32[768,2048]{1,0:T(8,128)}, f32[768,2048]{1,0:T(8,128)}) custom-call(s32[5]{0:T(128)} %stack.20.refs_0_, bf16[768,512]{1,0:T(8,128)(2,1)} %bitcast.34, bf16[768,512]{1,0:T(8,128)(2,1)} %bitcast.31, bf16[768,512]{1,0:T(8,128)(2,1)} %get-tuple-element.115.refs_3_, ...), custom_call_target="tpu_custom_call", output_to_operand_aliasing={{0}: (15, {}), {1}: (16, {})} | custom-call | flops 1 | bytes 1 | tf_op jit(solution)/shard_map/pallas_call | solution.py:129
  144.1 1.8 %collective-permute-done.29.refs_13_.refs_14_ = bf16[1024,256]{1,0:T(8,128)(2,1)S(1)} collective-permute-done((bf16[1024,256]{1,0:T(8,128)(2,1)S(1)}, bf16[1024,256]{1,0:T(8,128)(2,1)S(1)}, u32[]{:S(2)}, u32[]{:S(2)}) %collective-permute-start.29) | collective-permute-done | bytes 524320 | tf_op jit(solution)/shard_map/ppermute | solution.py:384
  145.9 0.8 copy-done.17
  146.7 7.3 %shard_map.82 = (f32[768,2048]{1,0:T(8,128)}, f32[768,2048]{1,0:T(8,128)}) custom-call(s32[5]{0:T(128)} %stack.20.refs_0_, bf16[768,512]{1,0:T(8,128)(2,1)} %bitcast.35, bf16[768,512]{1,0:T(8,128)(2,1)} %bitcast.32, bf16[768,512]{1,0:T(8,128)(2,1)} %get-tuple-element.115.refs_3_, ...), custom_call_target="tpu_custom_call", output_to_operand_aliasing={{0}: (15, {}), {1}: (16, {})} | custom-call | flops 1 | bytes 1 | tf_op jit(solution)/shard_map/pallas_call | solution.py:129
  (105 shorter events, 3.3 us)
Async XLA Ops:
  0.6 3.2 %copy-start = (bf16[1024,768]{1,0:T(8,128)(2,1)S(1)}, bf16[1024,768]{1,0:T(8,128)(2,1)}, u32[]{:S(2)}) copy-start(bf16[1024,768]{1,0:T(8,128)(2,1)} %param.6) | copy-start | bytes 4718596
  0.6 4.9 %collective-permute-start.1 = (s32[1024]{0:T(1024)}, s32[1024]{0:T(1024)S(1)}, u32[]{:S(2)}, u32[]{:S(2)}) collective-permute-start(s32[1024]{0:T(1024)} %param.7), channel_id=1, source_target_pairs={{0,2},{1,3},{2,0},{3,1},{4,6},{5,7},{6,4},{7,5},{8,10},{9,11},{10,... | collective-permute-start | bytes 12296 | tf_op jit(solution)/shard_map/ppermute | solution.py:305
  3.6 1.9 %collective-permute-start = (s32[1024]{0:T(1024)}, s32[1024]{0:T(1024)S(1)}, u32[]{:S(2)}, u32[]{:S(2)}) collective-permute-start(s32[1024]{0:T(1024)} %param.7), channel_id=1, source_target_pairs={{0,1},{1,0},{2,3},{3,2},{4,5},{5,4},{6,7},{7,6},{8,9},{9,8},{10,11... | collective-permute-start | bytes 12296 | tf_op jit(solution)/shard_map/ppermute | solution.py:305
  3.7 3.2 %collective-permute-start.2 = (s32[1024]{0:T(1024)}, s32[1024]{0:T(1024)S(1)}, u32[]{:S(2)}, u32[]{:S(2)}) collective-permute-start(s32[1024]{0:T(1024)} %param.7), channel_id=1, source_target_pairs={{0,3},{1,2},{2,1},{3,0},{4,7},{5,6},{6,5},{7,4},{8,11},{9,10},{10,... | collective-permute-start | bytes 12296 | tf_op jit(solution)/shard_map/ppermute | solution.py:305
  5.5 15.9 %copy-start.36 = (s32[16]{0:T(128)S(1)}, s32[16]{0:T(128)}, u32[]{:S(2)}) copy-start(s32[16]{0:T(128)} %param.11) | copy-start | bytes 196
  5.5 31.7 %copy-start.33 = (s32[1024]{0:T(1024)}, s32[1024]{0:T(1024)S(1)}, u32[]{:S(2)}) copy-start(s32[1024]{0:T(1024)S(1)} %collective-permute-done.1) | copy-start | bytes 12292
  11.1 10.3 %collective-permute-start.8 = (bf16[512,512]{1,0:T(8,128)(2,1)S(1)}, bf16[512,512]{1,0:T(8,128)(2,1)S(1)}, u32[]{:S(2)}, u32[]{:S(2)}) collective-permute-start(bf16[512,512]{1,0:T(8,128)(2,1)S(1)} %get-tuple-element.98), channel_id=1, source_target_pairs={{0,1},{1,0},{2,3},{3,2},{4,5},{5,4},{6,7},{7,6},{8,9},{9,8},{10,11... | collective-permute-start | bytes 1572872 | tf_op jit(solution)/shard_map/ppermute | solution.py:316
  11.6 41.1 %collective-permute-start.3 = (bf16[1024,512]{1,0:T(8,128)(2,1)S(1)}, bf16[1024,512]{1,0:T(8,128)(2,1)}, u32[]{:S(2)}, u32[]{:S(2)}) collective-permute-start(bf16[1024,512]{1,0:T(8,128)(2,1)S(1)} %constant_dynamic-slice_fusion.2), channel_id=1, source_target_pairs={{0,2},{1,3},{2,0},{3,1},{4,6},{5,7},{6,4},{7,5},{8,10},{9,11},{10,... | collective-permute-start | bytes 3145736 | tf_op jit(solution)/shard_map/ppermute | solution.py:311
  11.7 35.3 %collective-permute-start.6 = (bf16[512,768]{0,1:T(8,128)(2,1)S(1)}, bf16[512,768]{0,1:T(8,128)(2,1)}, u32[]{:S(2)}, u32[]{:S(2)}) collective-permute-start(bf16[512,768]{0,1:T(8,128)(2,1)S(1)} %copy.13), channel_id=1, source_target_pairs={{0,12},{15,3},{4,13},{11,2},{16,28},{31,19},{20,29},{27,18}} | collective-permute-start | bytes 2359304 | tf_op jit(solution)/shard_map/ppermute | solution.py:308
  18.5 28.5 %collective-permute-start.5 = (bf16[512,768]{0,1:T(8,128)(2,1)S(1)}, bf16[512,768]{0,1:T(8,128)(2,1)}, u32[]{:S(2)}, u32[]{:S(2)}) collective-permute-start(bf16[512,768]{0,1:T(8,128)(2,1)S(1)} %copy.13), channel_id=1, source_target_pairs={{0,4},{15,11},{1,8},{14,7},{4,1},{11,14},{5,9},{10,6},{16,20},{31,... | collective-permute-start | bytes 2359304 | tf_op jit(solution)/shard_map/ppermute | solution.py:307
  21.3 31.3 %collective-permute-start.4 = (bf16[768,512]{1,0:T(8,128)(2,1)}, bf16[768,512]{1,0:T(8,128)(2,1)}, u32[]{:S(2)}, u32[]{:S(2)}) collective-permute-start(bf16[768,512]{1,0:T(8,128)(2,1)} %constant_dynamic-slice_fusion.1), channel_id=1, source_target_pairs={{0,3},{1,2},{2,1},{3,0},{4,7},{5,6},{6,5},{7,4},{8,11},{9,10},{10,... | collective-permute-start | bytes 2359304 | tf_op jit(solution)/shard_map/ppermute | solution.py:313
  21.3 2.6 %copy-start.21 = (bf16[512,512]{1,0:T(8,128)(2,1)}, bf16[512,512]{1,0:T(8,128)(2,1)S(1)}, u32[]{:S(2)}) copy-start(bf16[512,512]{1,0:T(8,128)(2,1)S(1)} %collective-permute-done.8.refs_4_.refs_6_) | copy-start | bytes 1572868
  21.3 2.6 %collective-permute-start.7 = (bf16[512,512]{1,0:T(8,128)(2,1)}, bf16[512,512]{1,0:T(8,128)(2,1)S(1)}, u32[]{:S(2)}, u32[]{:S(2)}) collective-permute-start(bf16[512,512]{1,0:T(8,128)(2,1)} %get-tuple-element.99), channel_id=1, source_target_pairs={{0,1},{1,0},{2,3},{3,2},{4,5},{5,4},{6,7},{7,6},{8,9},{9,8},{10,11... | collective-permute-start | bytes 1572872 | tf_op jit(solution)/shard_map/ppermute | solution.py:316
  45.9 9.1 %copy-start.35 = (bf16[768,512]{1,0:T(8,128)(2,1)S(1)}, bf16[768,512]{1,0:T(8,128)(2,1)}, u32[]{:S(2)}) copy-start(bf16[768,512]{1,0:T(8,128)(2,1)} %get-tuple-element.65) | copy-start | bytes 2359300
  45.9 9.2 %copy-start.34 = (bf16[768,512]{1,0:T(8,128)(2,1)S(1)}, bf16[768,512]{1,0:T(8,128)(2,1)}, u32[]{:S(2)}) copy-start(bf16[768,512]{1,0:T(8,128)(2,1)} %get-tuple-element.75) | copy-start | bytes 2359300
  54.1 44.1 %copy-start.3 = (bf16[512,768]{0,1:T(8,128)(2,1)}, bf16[512,768]{0,1:T(8,128)(2,1)S(1)}, u32[]{:S(2)}) copy-start(bf16[512,768]{0,1:T(8,128)(2,1)S(1)} %add_select_fusion) | copy-start | bytes 2359300
  54.1 4.7 %copy-start.13 = (bf16[768,512]{1,0:T(8,128)(2,1)S(1)}, bf16[768,512]{1,0:T(8,128)(2,1)}, u32[]{:S(2)}) copy-start(bf16[768,512]{1,0:T(8,128)(2,1)} %get-tuple-element.64) | copy-start | bytes 2359300
  54.1 4.1 %collective-permute-start.9 = (bf16[512,768]{0,1:T(8,128)(2,1)S(1)}, bf16[512,768]{0,1:T(8,128)(2,1)S(1)}, u32[]{:S(2)}, u32[]{:S(2)}) collective-permute-start(bf16[512,768]{0,1:T(8,128)(2,1)S(1)} %add_select_fusion), channel_id=1, source_target_pairs={{0,1},{1,0},{2,3},{3,2},{4,5},{5,4},{6,7},{7,6},{8,9},{9,8},{10,11... | collective-permute-start | bytes 2359304 | tf_op jit(solution)/shard_map/ppermute | solution.py:328
  55.0 3.2 %collective-permute-start.10 = (bf16[768,512]{1,0:T(8,128)(2,1)S(1)}, bf16[768,512]{1,0:T(8,128)(2,1)S(1)}, u32[]{:S(2)}, u32[]{:S(2)}) collective-permute-start(bf16[768,512]{1,0:T(8,128)(2,1)S(1)} %copy-done.35), channel_id=1, source_target_pairs={{0,1},{1,0},{2,3},{3,2},{4,5},{5,4},{6,7},{7,6},{8,9},{9,8},{10,11... | collective-permute-start | bytes 2359304 | tf_op jit(solution)/shard_map/ppermute | solution.py:329
  55.1 6.6 %collective-permute-start.14 = (bf16[768,512]{1,0:T(8,128)(2,1)S(1)}, bf16[768,512]{1,0:T(8,128)(2,1)S(1)}, u32[]{:S(2)}, u32[]{:S(2)}) collective-permute-start(bf16[768,512]{1,0:T(8,128)(2,1)S(1)} %copy-done.34), channel_id=1, source_target_pairs={{0,1},{1,0},{2,3},{3,2},{4,5},{5,4},{6,7},{7,6},{8,9},{9,8},{10,11... | collective-permute-start | bytes 2359304 | tf_op jit(solution)/shard_map/ppermute | solution.py:330
  56.7 20.1 %collective-permute-start.12 = (bf16[512,768]{0,1:T(8,128)(2,1)S(1)}, bf16[512,768]{0,1:T(8,128)(2,1)S(1)}, u32[]{:S(2)}, u32[]{:S(2)}) collective-permute-start(bf16[512,768]{0,1:T(8,128)(2,1)S(1)} %add_select_fusion), channel_id=1, source_target_pairs={{0,16},{16,0},{1,17},{17,1},{2,18},{18,2},{3,19},{19,3},{4,20},{20... | collective-permute-start | bytes 2359304 | tf_op jit(solution)/shard_map/ppermute | solution.py:327
  58.2 8.6 %collective-permute-start.13 = (bf16[256,512]{1,0:T(8,128)(2,1)S(1)}, bf16[256,512]{1,0:T(8,128)(2,1)S(1)}, u32[]{:S(2)}, u32[]{:S(2)}) collective-permute-start(bf16[256,512]{1,0:T(8,128)(2,1)S(1)} %constant_dynamic-slice_fusion.5), channel_id=1, source_target_pairs={{0,3},{1,2},{2,1},{3,0},{4,7},{5,6},{6,5},{7,4},{8,11},{9,10},{10,... | collective-permute-start | bytes 786440 | tf_op jit(solution)/shard_map/ppermute | solution.py:334
  60.2 2.0 %copy-start.9 = (bf16[768,512]{1,0:T(8,128)(2,1)S(1)}, bf16[768,512]{1,0:T(8,128)(2,1)}, u32[]{:S(2)}) copy-start(bf16[768,512]{1,0:T(8,128)(2,1)} %get-tuple-element.74.refs_7_) | copy-start | bytes 2359300
  60.2 17.8 %collective-permute-start.11 = (bf16[512,512]{1,0:T(8,128)(2,1)}, bf16[512,512]{1,0:T(8,128)(2,1)S(1)}, u32[]{:S(2)}, u32[]{:S(2)}) collective-permute-start(bf16[512,512]{1,0:T(8,128)(2,1)} %fusion), channel_id=1, source_target_pairs={{0,2},{1,3},{2,0},{3,1},{4,6},{5,7},{6,4},{7,5},{8,10},{9,11},{10,... | collective-permute-start | bytes 1572872 | tf_op jit(solution)/shard_map/ppermute | solution.py:332
  61.7 2.2 %copy-start.14 = (bf16[768,512]{1,0:T(8,128)(2,1)}, bf16[768,512]{1,0:T(8,128)(2,1)S(1)}, u32[]{:S(2)}) copy-start(bf16[768,512]{1,0:T(8,128)(2,1)S(1)} %collective-permute-done.14) | copy-start | bytes 2359300
  76.8 21.4 %copy-start.2 = (bf16[512,768]{0,1:T(8,128)(2,1)}, bf16[512,768]{0,1:T(8,128)(2,1)S(1)}, u32[]{:S(2)}) copy-start(bf16[512,768]{0,1:T(8,128)(2,1)S(1)} %collective-permute-done.12) | copy-start | bytes 2359300
  78.1 1.8 %collective-permute-start.15 = (bf16[256,768]{0,1:T(8,128)(2,1)S(1)}, bf16[256,768]{0,1:T(8,128)(2,1)S(1)}, u32[]{:S(2)}, u32[]{:S(2)}) collective-permute-start(bf16[256,768]{0,1:T(8,128)(2,1)S(1)} %get-tuple-element.111), channel_id=1, source_target_pairs={{0,1},{1,0},{2,3},{3,2},{4,5},{5,4},{6,7},{7,6},{8,9},{9,8},{10,11... | collective-permute-start | bytes 1179656 | tf_op jit(solution)/shard_map/ppermute | solution.py:339
  78.2 2.2 %collective-permute-start.16 = (bf16[256,768]{0,1:T(8,128)(2,1)S(1)}, bf16[256,768]{0,1:T(8,128)(2,1)S(1)}, u32[]{:S(2)}, u32[]{:S(2)}) collective-permute-start(bf16[256,768]{0,1:T(8,128)(2,1)S(1)} %get-tuple-element.110), channel_id=1, source_target_pairs={{0,1},{1,0},{2,3},{3,2},{4,5},{5,4},{6,7},{7,6},{8,9},{9,8},{10,11... | collective-permute-start | bytes 1179656 | tf_op jit(solution)/shard_map/ppermute | solution.py:339
  80.5 1.9 %copy-start.20 = (f32[1024,512]{1,0:T(8,128)S(1)}, f32[1024,512]{1,0:T(8,128)}, u32[]{:S(2)}) copy-start(f32[1024,512]{1,0:T(8,128)} %get-tuple-element.82) | copy-start | bytes 6291460
  81.1 1.4 copy-start.8
  81.1 2.1 %copy-start.19 = (f32[1024,512]{1,0:T(8,128)S(1)}, f32[1024,512]{1,0:T(8,128)}, u32[]{:S(2)}) copy-start(f32[1024,512]{1,0:T(8,128)} %get-tuple-element.81) | copy-start | bytes 6291460
  81.7 14.8 %collective-permute-start.17 = (bf16[512,512]{1,0:T(8,128)(2,1)S(1)}, bf16[512,512]{1,0:T(8,128)(2,1)S(1)}, u32[]{:S(2)}, u32[]{:S(2)}) collective-permute-start(bf16[512,512]{1,0:T(8,128)(2,1)S(1)} %fusion.1), channel_id=1, source_target_pairs={{0,2},{1,3},{2,0},{3,1},{4,6},{5,7},{6,4},{7,5},{8,10},{9,11},{10,... | collective-permute-start | bytes 1572872 | tf_op jit(solution)/shard_map/ppermute | solution.py:342
  83.7 1.4 copy-start.15
  83.7 2.0 %copy-start.10 = (bf16[768,512]{1,0:T(8,128)(2,1)S(1)}, bf16[768,512]{1,0:T(8,128)(2,1)}, u32[]{:S(2)}) copy-start(bf16[768,512]{1,0:T(8,128)(2,1)} %get-tuple-element.74.refs_7_) | copy-start | bytes 2359300
  83.8 12.7 %copy-start.4 = (bf16[2048,256]{1,0:T(8,128)(2,1)}, bf16[2048,256]{1,0:T(8,128)(2,1)S(1)}, u32[]{:S(2)}) copy-start(bf16[2048,256]{1,0:T(8,128)(2,1)S(1)} %pad_maximum_fusion.refs_7_.refs_8_.refs_11_.refs_12_) | copy-start | bytes 3145732
  83.8 34.4 %collective-permute-start.18 = (bf16[2048,256]{1,0:T(8,128)(2,1)S(1)}, bf16[2048,256]{1,0:T(8,128)(2,1)S(1)}, u32[]{:S(2)}, u32[]{:S(2)}) collective-permute-start(bf16[2048,256]{1,0:T(8,128)(2,1)S(1)} %pad_maximum_fusion.refs_7_.refs_8_.refs_11_.refs_12_), channel_id=1, source_target_pairs={{0,2},{1,3},{2,0},{3,1},{4,6},{5,7},{6,4},{7,5},{8,10},{9,11},{10,... | collective-permute-start | bytes 3145736 | tf_op jit(solution)/shard_map/ppermute | solution.py:354
  96.5 4.2 %collective-permute-start.19 = (bf16[2048,256]{1,0:T(8,128)(2,1)S(1)}, bf16[2048,256]{1,0:T(8,128)(2,1)S(1)}, u32[]{:S(2)}, u32[]{:S(2)}) collective-permute-start(bf16[2048,256]{1,0:T(8,128)(2,1)S(1)} %pad_maximum_fusion.refs_7_.refs_8_.refs_11_.refs_12_), channel_id=1, source_target_pairs={{0,1},{1,0},{2,3},{3,2},{4,5},{5,4},{6,7},{7,6},{8,9},{9,8},{10,11... | collective-permute-start | bytes 3145736 | tf_op jit(solution)/shard_map/ppermute | solution.py:361
  96.8 2.9 %copy-start.23 = (bf16[512,256]{1,0:T(8,128)(2,1)}, bf16[512,256]{1,0:T(8,128)(2,1)S(1)}, u32[]{:S(2)}) copy-start(bf16[512,256]{1,0:T(8,128)(2,1)S(1)} %get-tuple-element.107.refs_9_) | copy-start | bytes 786436
  96.8 2.9 %copy-start.25 = (bf16[512,256]{1,0:T(8,128)(2,1)}, bf16[512,256]{1,0:T(8,128)(2,1)S(1)}, u32[]{:S(2)}) copy-start(bf16[512,256]{1,0:T(8,128)(2,1)S(1)} %get-tuple-element.106.refs_10_) | copy-start | bytes 786436
  97.1 4.6 %copy-start.11 = (bf16[1024,256]{1,0:T(8,128)(2,1)}, bf16[1024,256]{1,0:T(8,128)(2,1)S(1)}, u32[]{:S(2)}) copy-start(bf16[1024,256]{1,0:T(8,128)(2,1)S(1)} %pad_maximum_fusion.1.refs_13_.refs_14_) | copy-start | bytes 1572868
  97.1 3.5 %collective-permute-start.22 = (bf16[1024,256]{1,0:T(8,128)(2,1)S(1)}, bf16[1024,256]{1,0:T(8,128)(2,1)S(1)}, u32[]{:S(2)}, u32[]{:S(2)}) collective-permute-start(bf16[1024,256]{1,0:T(8,128)(2,1)S(1)} %pad_maximum_fusion.1.refs_13_.refs_14_), channel_id=1, source_target_pairs={{0,1},{1,0},{2,3},{3,2},{4,5},{5,4},{6,7},{7,6},{8,9},{9,8},{10,11... | collective-permute-start | bytes 1572872 | tf_op jit(solution)/shard_map/ppermute | solution.py:363
  97.7 2.6 %collective-permute-start.21 = (bf16[512,256]{1,0:T(8,128)(2,1)S(1)}, bf16[512,256]{1,0:T(8,128)(2,1)S(1)}, u32[]{:S(2)}, u32[]{:S(2)}) collective-permute-start(bf16[512,256]{1,0:T(8,128)(2,1)S(1)} %get-tuple-element.106.refs_10_), channel_id=1, source_target_pairs={{0,1},{1,0},{2,3},{3,2},{4,5},{5,4},{6,7},{7,6},{8,9},{9,8},{10,11... | collective-permute-start | bytes 786440 | tf_op jit(solution)/shard_map/ppermute | solution.py:362
  97.8 2.9 %collective-permute-start.20 = (bf16[512,256]{1,0:T(8,128)(2,1)S(1)}, bf16[512,256]{1,0:T(8,128)(2,1)S(1)}, u32[]{:S(2)}, u32[]{:S(2)}) collective-permute-start(bf16[512,256]{1,0:T(8,128)(2,1)S(1)} %get-tuple-element.107.refs_9_), channel_id=1, source_target_pairs={{0,1},{1,0},{2,3},{3,2},{4,5},{5,4},{6,7},{7,6},{8,9},{9,8},{10,11... | collective-permute-start | bytes 786440 | tf_op jit(solution)/shard_map/ppermute | solution.py:362
  100.3 1.4 copy-start.28
  100.7 1.1 copy-start.29
  100.7 1.2 copy-start.18
  100.7 1.0 copy-start.7
  101.9 16.9 %copy-start.24 = (bf16[512,256]{1,0:T(8,128)(2,1)S(1)}, bf16[512,256]{1,0:T(8,128)(2,1)}, u32[]{:S(2)}) copy-start(bf16[512,256]{1,0:T(8,128)(2,1)} %copy-done.23) | copy-start | bytes 786436
  101.9 18.3 %copy-start.12 = (bf16[1024,256]{1,0:T(8,128)(2,1)S(1)}, bf16[1024,256]{1,0:T(8,128)(2,1)}, u32[]{:S(2)}) copy-start(bf16[1024,256]{1,0:T(8,128)(2,1)} %copy-done.11) | copy-start | bytes 1572868
  118.2 17.6 %copy-start.5 = (bf16[2048,256]{1,0:T(8,128)(2,1)}, bf16[2048,256]{1,0:T(8,128)(2,1)S(1)}, u32[]{:S(2)}) copy-start(bf16[2048,256]{1,0:T(8,128)(2,1)S(1)} %collective-permute-done.18.refs_7_.refs_8_) | copy-start | bytes 3145732
  118.2 17.6 %collective-permute-start.26 = (bf16[2048,256]{1,0:T(8,128)(2,1)S(1)}, bf16[2048,256]{1,0:T(8,128)(2,1)S(1)}, u32[]{:S(2)}, u32[]{:S(2)}) collective-permute-start(bf16[2048,256]{1,0:T(8,128)(2,1)S(1)} %collective-permute-done.18.refs_7_.refs_8_), channel_id=1, source_target_pairs={{0,1},{1,0},{2,3},{3,2},{4,5},{5,4},{6,7},{7,6},{8,9},{9,8},{10,11... | collective-permute-start | bytes 3145736 | tf_op jit(solution)/shard_map/ppermute | solution.py:380
  118.2 9.3 %collective-permute-start.25 = (bf16[512,256]{1,0:T(8,128)(2,1)}, bf16[512,256]{1,0:T(8,128)(2,1)S(1)}, u32[]{:S(2)}, u32[]{:S(2)}) collective-permute-start(bf16[512,256]{1,0:T(8,128)(2,1)} %copy-done.25), channel_id=1, source_target_pairs={{0,2},{1,3},{2,0},{3,1},{4,6},{5,7},{6,4},{7,5},{8,10},{9,11},{10,... | collective-permute-start | bytes 786440 | tf_op jit(solution)/shard_map/ppermute | solution.py:359
  118.8 14.3 %collective-permute-start.24 = (bf16[512,256]{1,0:T(8,128)(2,1)S(1)}, bf16[512,256]{1,0:T(8,128)(2,1)S(1)}, u32[]{:S(2)}, u32[]{:S(2)}) collective-permute-start(bf16[512,256]{1,0:T(8,128)(2,1)S(1)} %copy-done.24), channel_id=1, source_target_pairs={{0,2},{1,3},{2,0},{3,1},{4,6},{5,7},{6,4},{7,5},{8,10},{9,11},{10,... | collective-permute-start | bytes 786440 | tf_op jit(solution)/shard_map/ppermute | solution.py:359
  120.2 23.7 %collective-permute-start.23 = (bf16[1024,256]{1,0:T(8,128)(2,1)S(1)}, bf16[1024,256]{1,0:T(8,128)(2,1)S(1)}, u32[]{:S(2)}, u32[]{:S(2)}) collective-permute-start(bf16[1024,256]{1,0:T(8,128)(2,1)S(1)} %copy-done.12), channel_id=1, source_target_pairs={{0,2},{1,3},{2,0},{3,1},{4,6},{5,7},{6,4},{7,5},{8,10},{9,11},{10,... | collective-permute-start | bytes 1572872 | tf_op jit(solution)/shard_map/ppermute | solution.py:360
  127.5 8.3 %copy-start.26 = (bf16[512,256]{1,0:T(8,128)(2,1)}, bf16[512,256]{1,0:T(8,128)(2,1)S(1)}, u32[]{:S(2)}) copy-start(bf16[512,256]{1,0:T(8,128)(2,1)S(1)} %collective-permute-done.25.refs_10_) | copy-start | bytes 786436
  133.1 2.6 %copy-start.27 = (bf16[512,256]{1,0:T(8,128)(2,1)}, bf16[512,256]{1,0:T(8,128)(2,1)S(1)}, u32[]{:S(2)}) copy-start(bf16[512,256]{1,0:T(8,128)(2,1)S(1)} %collective-permute-done.24.refs_9_) | copy-start | bytes 786436
  133.1 1.5 collective-permute-start.27
  133.1 1.9 %collective-permute-start.28 = (bf16[512,256]{1,0:T(8,128)(2,1)S(1)}, bf16[512,256]{1,0:T(8,128)(2,1)S(1)}, u32[]{:S(2)}, u32[]{:S(2)}) collective-permute-start(bf16[512,256]{1,0:T(8,128)(2,1)S(1)} %collective-permute-done.25.refs_10_), channel_id=1, source_target_pairs={{0,1},{1,0},{2,3},{3,2},{4,5},{5,4},{6,7},{7,6},{8,9},{9,8},{10,11... | collective-permute-start | bytes 786440 | tf_op jit(solution)/shard_map/ppermute | solution.py:381
  134.7 1.1 copy-start.30
  135.8 1.0 copy-start.6
  144.0 1.9 %copy-start.16 = (bf16[1024,256]{1,0:T(8,128)(2,1)}, bf16[1024,256]{1,0:T(8,128)(2,1)S(1)}, u32[]{:S(2)}) copy-start(bf16[1024,256]{1,0:T(8,128)(2,1)S(1)} %collective-permute-done.23.refs_9_.refs_10_) | copy-start | bytes 1572868
  144.0 1.9 %collective-permute-start.29 = (bf16[1024,256]{1,0:T(8,128)(2,1)S(1)}, bf16[1024,256]{1,0:T(8,128)(2,1)S(1)}, u32[]{:S(2)}, u32[]{:S(2)}) collective-permute-start(bf16[1024,256]{1,0:T(8,128)(2,1)S(1)} %collective-permute-done.23.refs_9_.refs_10_), channel_id=1, source_target_pairs={{0,1},{1,0},{2,3},{3,2},{4,5},{5,4},{6,7},{7,6},{8,9},{9,8},{10,11... | collective-permute-start | bytes 1572872 | tf_op jit(solution)/shard_map/ppermute | solution.py:384
  145.9 0.8 copy-start.17
  146.7 7.3 %copy-start.1 = (bf16[1024,768]{1,0:T(8,128)(2,1)S(1)}, bf16[1024,768]{1,0:T(8,128)(2,1)}, u32[]{:S(2)}) copy-start(bf16[1024,768]{1,0:T(8,128)(2,1)} %param.6) | copy-start | bytes 4718596
  (3 other events, 2.2 us)

commit v3 on v2

--- a/solution.py
+++ b/solution.py
@@ -292,7 +292,7 @@
     rows_blk, cols_blk = mean.shape
     count = indices.shape[0]
     part = cols_blk // 4
-    half, few, most = n_rows // 2, count // 2, count * 3 // 4
+    half, few = n_rows // 2, count // 2
     salt = lax.dynamic_index_in_dim(block_salts, dp_pos * n_shard + shard_pos, 0, keepdims=False)
     scal = jnp.stack([dp_pos, salt, dp_pos * rows_blk, shard_pos * cols_blk, member * half]).astype(jnp.int32)
     both = ("shard", "dp")
@@ -309,7 +309,7 @@
     x1 = cols(after(grad_out, own_a), 2, 0, count)
     x1, idx_core, idx_chip, idx_cross = sync((x1, idx_core, idx_chip, idx_cross))
     x1_in = lax.ppermute(x1, "dp", CHIP)
-    x2 = cols(after(grad_out, x1), 3, 0, most)
+    x2 = cols(after(grad_out, x1), 3, 0, count)
     x2_in = lax.ppermute(x2, "dp", CROSS)
     go1 = after(grad_out, x2)
     go_mine = [cols(go1, 1, r, few) for r in (0, few)]
@@ -319,28 +319,27 @@
     )
     groups = [(indices, grad_out, 0), (idx_core[:few], go_core[0], None), (idx_core[few:], go_core[1], None)]
     sums = sum_rows(scal, groups, n_rows, part, None, [w_near])
-    x3 = cols(after(grad_out, *sums), 3, most, count - most)
-    x1_in, x2_in, near_a, far_a, w_far_send, w_near_send, w_far, w_near, s0, s1, x3 = sync(
-        (x1_in, x2_in, near_a, far_a, w_far_send, w_near_send, w_far, w_near, *sums, x3)
+    x1_in, near_a, far_a, w_far_send, w_near_send, w_far, w_near, s0, s1 = sync(
+        (x1_in, near_a, far_a, w_far_send, w_near_send, w_far, w_near, *sums)
     )
     tab_a = jnp.where(shard_pos == dp_pos, own_a, near_a + far_a)
     tab_b = lax.ppermute(tab_a, "members", [(0, 1), (1, 0)])
     core_a = lax.ppermute(tab_a, "dp", CORE)
     w_core_far = lax.ppermute(w_far_send, "dp", CORE)
     w_core_near = lax.ppermute(w_near_send, "dp", CORE)
+    core_a, w_core_far, x2_in = sync((core_a, w_core_far, x2_in))
     out_a = (dot(tab_a, w_far) + dot(core_a, w_core_far)).astype(BF16)
     pre_a = lax.ppermute(out_a, "dp", CHIP)
-    own_pre_a = dot(after(tab_a, out_a), w_near) + dot(core_a, w_core_near)
-    x3_in = lax.ppermute(x3, "dp", CROSS)
-    groups = [(idx_chip, x1_in, None), (idx_cross[:most], x2_in, None), (idx_cross[most:], x3_in, None)]
-    sums = sum_rows(scal, groups, n_rows, part, (s0, s1), [own_pre_a])
-    pre_a, tab_b, s0, s1 = sync((pre_a, tab_b, *sums))
+    sums = sum_rows(scal, [(idx_chip, x1_in, None), (idx_cross, x2_in, None)], n_rows, part, (s0, s1), [out_a])
+    tab_b, s0, s1 = sync((tab_b, *sums))
     quarter = half // 2
     core_b = [lax.ppermute(t, "dp", CORE) for t in (tab_b[:quarter], tab_b[quarter:])]
+    core_b, pre_a = sync((core_b, pre_a))
     core_b = jnp.concatenate(core_b, 0)
     out_b = (dot(tab_b, w_far) + dot(core_b, w_core_far)).astype(BF16)
     pre_b = lax.ppermute(out_b, "dp", CHIP)
     pre_a, pb = after(pre_a, out_b), after(tab_b, out_b)
+    own_pre_a = dot(after(tab_a, out_b), w_near) + dot(core_a, w_core_near)
     own_pre_b = dot(pb, w_near) + dot(core_b, w_core_near)
 
     cut = part // 2

time: 155 us -> 147 us (0.948)
  waiting for transfers between devices: 44.2 us -> 36.6 us
  local copies, waits for them, and re-layouts: 17.4 us -> 15.6 us
    ppermute x1 -> x0, waiting for transfers between devices: 2.92 us -> none  [on_device(): x3_in = lax.ppermute(x3, 'dp', CROSS)]
    ppermute x1, waiting for transfers between devices: 0.01 us -> 2.5 us  [on_device(): tab_b = lax.ppermute(tab_a, 'members', [(0, 1), (1, 0)])]
    ppermute x1, waiting for transfers between devices: 5.6 us -> 3.56 us  [on_device(): x2_in = lax.ppermute(x2, 'dp', CROSS)]
    ppermute x2, waiting for transfers between devices: 1.74 us -> 0.01 us  [on_device(): lax.ppermute(t, 'dp', CORE)]
    dynamic_slice x4 -> x3, local copies, waits for them, and re-layouts: 6.54 us -> 5.84 us  [cols(): return lax.dynamic_slice(a, (row, (dp_pos ^ flip) * part), (rows, part))]
    unnamed x76 -> x72, local copies, waits for them, and re-layouts: 7.01 us -> 7.11 us
  transfers between devices with their start and end apart: 30 -> 29, of which waited for: 16 -> 13; matrix products, arithmetic and copies ran while one was open for 9% -> 14% of each run, Pallas kernels for 32% -> 34%
where the time goes in v3:
time: 147 us; the launch traced here: 146 us
  Pallas kernels  56.4 us (38%)
  waiting for transfers between devices  36.6 us (25%)
  starting transfers between devices  23.7 us (16%)
  local copies, waits for them, and re-layouts  15.6 us (11%)
  matrix products  6.99 us (5%)
  other arithmetic  5.25 us (4%)
    pallas_call x6, Pallas kernels, call(): pl.pallas_call(body, grid_spec=pltpu.PrefetchScalarGridSpec(num_scalar_pr...  56.4 us
    ppermute x2, waiting for transfers between devices, on_device(): far_b0 = [lax.ppermute(s, 'dp', CHIP) for s in b0]  11.6 us
    ppermute x1, waiting for transfers between devices, on_device(): pre_b = lax.ppermute(out_b, 'dp', CHIP)  8.64 us
    unnamed x72, local copies, waits for them, and re-layouts  7.11 us
    dot_general x8, matrix products, dot(): return jnp.dot(a, b, preferred_element_type=F32)  6.99 us
    ppermute x1, starting transfers between devices, on_device(): far_a = lax.ppermute(own_a, both, to_far)  6.43 us
    dynamic_slice x3, local copies, waits for them, and re-layouts, cols(): return lax.dynamic_slice(a, (row, (dp_pos ^ flip) * part), (rows, part))  5.84 us
    ppermute x1, waiting for transfers between devices, on_device(): far_a = lax.ppermute(send_a, 'dp', CHIP)  4.4 us
  transfers between devices with their start and end apart: 29, of which 13 were waited for; matrix products, arithmetic and copies ran while one was open for 14% of the time, Pallas kernels for 34%

profile of v3, /device:TPU:0, one launch (start us, length us, event | category | flops | bytes accessed | tf_op | source)
XLA Modules:
  0.0 145.7 jit_solution(9225515098118881204)
XLA Ops:
  0.6 3.0 %collective-permute-start.1 = (s32[1024]{0:T(1024)}, s32[1024]{0:T(1024)S(1)}, u32[]{:S(2)}, u32[]{:S(2)}) collective-permute-start(s32[1024]{0:T(1024)} %param.7), channel_id=1, source_target_pairs={{0,2},{1,3},{2,0},{3,1},{4,6},{5,7},{6,4},{7,5},{8,10},{9,11},{10,... | collective-permute-start | bytes 12296 | tf_op jit(solution)/shard_map/ppermute | solution.py:305
  3.9 0.3 copy.13
  4.2 1.3 constant_dynamic-slice_fusion.2
  5.5 1.4 collective-permute-done.2
  6.9 0.7 collective-permute-start.3
  7.6 6.4 %collective-permute-start.5 = (bf16[512,768]{0,1:T(8,128)(2,1)S(1)}, bf16[512,768]{0,1:T(8,128)(2,1)}, u32[]{:S(2)}, u32[]{:S(2)}) collective-permute-start(bf16[512,768]{0,1:T(8,128)(2,1)S(1)} %copy.13), channel_id=1, source_target_pairs={{0,12},{15,3},{4,13},{11,2},{16,28},{31,19},{20,29},{27,18}} | collective-permute-start | bytes 2359304 | tf_op jit(solution)/shard_map/ppermute | solution.py:308
  14.0 3.0 %collective-permute-start.4 = (bf16[512,768]{0,1:T(8,128)(2,1)S(1)}, bf16[512,768]{0,1:T(8,128)(2,1)}, u32[]{:S(2)}, u32[]{:S(2)}) collective-permute-start(bf16[512,768]{0,1:T(8,128)(2,1)S(1)} %copy.13), channel_id=1, source_target_pairs={{0,4},{15,11},{1,8},{14,7},{4,1},{11,14},{5,9},{10,6},{16,20},{31,... | collective-permute-start | bytes 2359304 | tf_op jit(solution)/shard_map/ppermute | solution.py:307
  17.0 2.3 %constant_dynamic-slice_fusion.1 = bf16[1024,512]{1,0:T(8,128)(2,1)} fusion(bf16[1024,2048]{1,0:T(8,128)(2,1)} %refs_2_.3, s32[]{:T(128)S(6)} %select_n.29), kind=kLoop, calls=%fused_computation.28 | loop fusion | bytes 2097156 | tf_op jit(solution)/shard_map/dynamic_slice | solution.py:303
  19.3 2.2 %constant_dynamic-slice_fusion.4 = (bf16[512,512]{1,0:T(8,128)(2,1)}, bf16[512,512]{1,0:T(8,128)(2,1)}) fusion(bf16[1024,2048]{1,0:T(8,128)(2,1)} %refs_2_.3, s32[]{:T(128)S(6)} %select_n.30), kind=kLoop, calls=%fused_computation.31 | loop fusion | bytes 2097156 | tf_op jit(solution)/shard_map/dynamic_slice | solution.py:303
  21.6 0.5 collective-permute-start.6
  22.1 0.6 dynamic_slice.19
  22.7 1.3 stack.20.refs_0_
  24.0 0.6 fusion.3
  24.6 0.8 copy-done.20
  25.4 0.8 copy-done.21
  26.2 12.5 %shard_map.77 = (bf16[768,512]{1,0:T(8,128)(2,1)}, bf16[768,512]{1,0:T(8,128)(2,1)}, bf16[768,512]{1,0:T(8,128)(2,1)}, bf16[768,512]{1,0:T(8,128)(2,1)}) custom-call(s32[5]{0:T(128)} %stack.20.refs_0_, f32[768,2048]{1,0:T(8,128)} %refs_5_.5, f32[768,2048]{1,0:T(8,128)} %refs_6_.5, bf16[512,512]{1,0:T(8,128)(2,1)} %copy-done.21, bf16[512,512]{1,0:T(8,128)(2,1)} %copy-done.20), custom_call_target="tpu_custom_call" | custom-call | flops 1 | bytes 1 | tf_op jit(solution)/shard_map/pallas_call | solution.py:129
  38.7 8.7 %shard_map.78 = (f32[1024,512]{1,0:T(8,128)}, f32[1024,512]{1,0:T(8,128)}) custom-call(s32[5]{0:T(128)} %stack.20.refs_0_, s32[1,1024]{1,0:T(1,128)} %bitcast.37, bf16[1024,2048]{1,0:T(8,128)(2,1)} %refs_2_.3, s32[1,512]{1,0:T(1,128)} %bitcast.36, bf16[512,512]{1,0:T(8,128)(2,1)} %copy-done.21, s32[1,512]{1,0:T(1,128)} %bitcast.35, ...), custom_call_target="tpu_custom_call" | custom-call | flops 1 | bytes 1 | tf_op jit(solution)/shard_map/pallas_call | solution.py:129
  47.4 1.6 %add_select_fusion = bf16[512,768]{0,1:T(8,128)(2,1)S(1)} fusion(bf16[512,768]{0,1:T(8,128)(2,1)S(1)} %copy.13, bf16[512,768]{0,1:T(8,128)(2,1)} %collective-permute-done.4, bf16[512,768]{0,1:T(8,128)(2,1)} %collective-permute-done.5, pred[]{:T(512)S(6)} %eq.3), kind=kLoop, calls=%fused_computation.9 | loop fusion | flops 786432 | bytes 3145729 | tf_op jit(solution)/shard_map/jit(_where)/select_n | solution.py:325
  49.1 0.4 collective-permute-start.10
  49.6 1.5 %collective-permute-start.8 = (bf16[512,768]{0,1:T(8,128)(2,1)S(1)}, bf16[512,768]{0,1:T(8,128)(2,1)S(1)}, u32[]{:S(2)}, u32[]{:S(2)}) collective-permute-start(bf16[512,768]{0,1:T(8,128)(2,1)S(1)} %add_select_fusion), channel_id=1, source_target_pairs={{0,16},{16,0},{1,17},{17,1},{2,18},{18,2},{3,19},{19,3},{4,20},{20... | collective-permute-start | bytes 2359304 | tf_op jit(solution)/shard_map/ppermute | solution.py:326
  51.1 3.6 %collective-permute-done.11.refs_4_ = bf16[1024,512]{1,0:T(8,128)(2,1)} collective-permute-done((bf16[1024,512]{1,0:T(8,128)(2,1)}, bf16[1024,512]{1,0:T(8,128)(2,1)}, u32[]{:S(2)}, u32[]{:S(2)}) %collective-permute-start.11) | collective-permute-done | bytes 1048608 | tf_op jit(solution)/shard_map/ppermute | solution.py:313
  54.7 0.9 copy-done.14
  55.5 0.6 fusion.4
  56.2 1.4 fusion.refs_7_
  57.5 9.1 %shard_map.79 = (f32[1024,512]{1,0:T(8,128)}, f32[1024,512]{1,0:T(8,128)}) custom-call(s32[5]{0:T(128)} %stack.20.refs_0_, s32[1,1024]{1,0:T(1,128)} %bitcast.38, bf16[1024,512]{1,0:T(8,128)(2,1)} %collective-permute-done.3.refs_2_, s32[1,1024]{1,0:T(1,128)} %bitcast.39, bf16[1024,512]{1,0:T(8,128)(2,1)} %collective-permute-done.11.refs_4_, ...), custom_call_target="tpu_custom_call" | custom-call | flops 1 | bytes 1 | tf_op jit(solution)/shard_map/pallas_call | solution.py:129
  66.6 2.5 %collective-permute-done.8 = bf16[512,768]{0,1:T(8,128)(2,1)S(1)} collective-permute-done((bf16[512,768]{0,1:T(8,128)(2,1)S(1)}, bf16[512,768]{0,1:T(8,128)(2,1)S(1)}, u32[]{:S(2)}, u32[]{:S(2)}) %collective-permute-start.8) | collective-permute-done | bytes 786464 | tf_op jit(solution)/shard_map/ppermute | solution.py:326
  69.2 0.5 collective-permute-start.12
  69.7 2.0 %fusion.6 = f32[512,512]{1,0:T(8,128)S(1)} fusion(bf16[512,768]{0,1:T(8,128)(2,1)} %copy-done.14, bf16[768,512]{1,0:T(8,128)(2,1)S(1)} %collective-permute-done.16), kind=kOutput, calls=%fused_computation.36 | convolution fusion | flops 402653184 | bytes 2621440 | tf_op jit(solution)/shard_map/dot_general | solution.py:34
  71.8 0.3 collective-permute-done.14
  72.2 0.6 fusion.5
  72.8 0.6 fusion.1
  73.4 1.1 collective-permute-start.15
  74.5 0.6 convolution_add_fusion.1
  75.1 0.3 copy-done.18
  75.4 1.6 %multiply_convert_fusion.9 = (bf16[512,256]{1,0:T(8,128)(2,1)S(1)}, bf16[512,256]{1,0:T(8,128)(2,1)S(1)}, bf16[512,256]{1,0:T(8,128)(2,1)S(1)}, bf16[512,256]{1,0:T(8,128)(2,1)S(1)}) fusion(f32[1024,512]{1,0:T(8,128)S(1)} %copy-done.18, f32[512,512]{1,0:T(8,128)S(1)} %convolution_add_fusion.1, bf16[512,512]{1,0:T(8,128)(2,1)} %collective-permute-done.14, ...), kind=kLoop, calls=%fused_computation.23 | loop fusion | flops 3670016 | bytes 4718592 | tf_op jit(solution)/shard_map/convert_element_type | solution.py:58
  77.0 1.1 collective-permute-start.17
  78.1 0.3 copy-done.13
  78.4 0.6 fusion.7
  79.0 0.6 convolution_add_fusion
  79.6 8.6 %collective-permute-done.15 = bf16[512,512]{1,0:T(8,128)(2,1)S(1)} collective-permute-done((bf16[512,512]{1,0:T(8,128)(2,1)S(1)}, bf16[512,512]{1,0:T(8,128)(2,1)S(1)}, u32[]{:S(2)}, u32[]{:S(2)}) %collective-permute-start.15) | collective-permute-done | bytes 524320 | tf_op jit(solution)/shard_map/ppermute | solution.py:340
  88.3 0.3 multiply_convert_fusion.4
  88.6 0.3 multiply_convert_fusion.3
  88.9 0.6 collective-permute-start.21
  89.6 0.4 collective-permute-start.19
  90.0 1.5 %multiply_convert_fusion = (bf16[768,512]{1,0:T(8,128)(2,1)}, bf16[768,512]{1,0:T(8,128)(2,1)}) fusion(bf16[512,768]{0,1:T(8,128)(2,1)S(1)} %collective-permute-done.8, bf16[512,768]{0,1:T(8,128)(2,1)S(1)} %add_select_fusion), kind=kLoop, calls=%fused_computation | loop fusion | flops 2359296 | bytes 3145728 | tf_op jit(solution)/shard_map/convert_element_type | solution.py:43
  91.5 0.6 collective-permute-done.20.refs_18_
  92.1 0.4 collective-permute-done.19.refs_17_
  92.5 1.0 copy-done.7
  93.6 11.5 %shard_map.80 = (f32[768,2048]{1,0:T(8,128)}, f32[768,2048]{1,0:T(8,128)}) custom-call(s32[5]{0:T(128)} %stack.20.refs_0_, bf16[768,512]{1,0:T(8,128)(2,1)} %bitcast.32, bf16[768,512]{1,0:T(8,128)(2,1)} %bitcast.29, bf16[768,512]{1,0:T(8,128)(2,1)} %get-tuple-element.119.refs_3_, bf16[768,512]{1,0:T(8,128)(2,1)} %get-tuple-element.118.refs_4_, ...), custom_call_target="tpu_custom_call" | custom-call | flops 1 | bytes 1 | tf_op jit(solution)/shard_map/pallas_call | solution.py:129
  105.1 4.4 %collective-permute-done.17.refs_7_.refs_8_ = bf16[2048,256]{1,0:T(8,128)(2,1)S(1)} collective-permute-done((bf16[2048,256]{1,0:T(8,128)(2,1)S(1)}, bf16[2048,256]{1,0:T(8,128)(2,1)S(1)}, u32[]{:S(2)}, u32[]{:S(2)}) %collective-permute-start.17) | collective-permute-done | bytes 1048608 | tf_op jit(solution)/shard_map/ppermute | solution.py:353
  109.5 1.3 collective-permute-start.24
  110.8 0.7 collective-permute-start.23
  111.6 1.3 collective-permute-start.22
  112.9 6.0 %collective-permute-done.24.refs_10_ = bf16[512,256]{1,0:T(8,128)(2,1)S(1)} collective-permute-done((bf16[512,256]{1,0:T(8,128)(2,1)}, bf16[512,256]{1,0:T(8,128)(2,1)S(1)}, u32[]{:S(2)}, u32[]{:S(2)}) %collective-permute-start.24) | collective-permute-done | bytes 262176 | tf_op jit(solution)/shard_map/ppermute | solution.py:358
  118.9 5.6 %collective-permute-done.23.refs_9_ = bf16[512,256]{1,0:T(8,128)(2,1)S(1)} collective-permute-done((bf16[512,256]{1,0:T(8,128)(2,1)S(1)}, bf16[512,256]{1,0:T(8,128)(2,1)S(1)}, u32[]{:S(2)}, u32[]{:S(2)}) %collective-permute-start.23) | collective-permute-done | bytes 262176 | tf_op jit(solution)/shard_map/ppermute | solution.py:358
  124.5 0.5 collective-permute-start.27
  125.0 1.0 collective-permute-done.26.refs_13_
  126.0 0.4 collective-permute-done.27.refs_14_
  126.4 0.7 copy-done.30
  127.1 1.0 copy-done.6
  128.1 7.3 %shard_map.81 = (f32[768,2048]{1,0:T(8,128)}, f32[768,2048]{1,0:T(8,128)}) custom-call(s32[5]{0:T(128)} %stack.20.refs_0_, bf16[768,512]{1,0:T(8,128)(2,1)} %bitcast.33, bf16[768,512]{1,0:T(8,128)(2,1)} %bitcast.30, bf16[768,512]{1,0:T(8,128)(2,1)} %get-tuple-element.119.refs_3_, ...), custom_call_target="tpu_custom_call", output_to_operand_aliasing={{0}: (15, {}), {1}: (16, {})} | custom-call | flops 1 | bytes 1 | tf_op jit(solution)/shard_map/pallas_call | solution.py:129
  135.7 1.8 %collective-permute-done.28.refs_13_.refs_14_ = bf16[1024,256]{1,0:T(8,128)(2,1)S(1)} collective-permute-done((bf16[1024,256]{1,0:T(8,128)(2,1)S(1)}, bf16[1024,256]{1,0:T(8,128)(2,1)S(1)}, u32[]{:S(2)}, u32[]{:S(2)}) %collective-permute-start.28) | collective-permute-done | bytes 524320 | tf_op jit(solution)/shard_map/ppermute | solution.py:383
  137.5 0.8 copy-done.16
  138.2 7.3 %shard_map.82 = (f32[768,2048]{1,0:T(8,128)}, f32[768,2048]{1,0:T(8,128)}) custom-call(s32[5]{0:T(128)} %stack.20.refs_0_, bf16[768,512]{1,0:T(8,128)(2,1)} %bitcast.34, bf16[768,512]{1,0:T(8,128)(2,1)} %bitcast.31, bf16[768,512]{1,0:T(8,128)(2,1)} %get-tuple-element.119.refs_3_, ...), custom_call_target="tpu_custom_call", output_to_operand_aliasing={{0}: (15, {}), {1}: (16, {})} | custom-call | flops 1 | bytes 1 | tf_op jit(solution)/shard_map/pallas_call | solution.py:129
  (96 shorter events, 1.3 us)
Async XLA Ops:
  0.6 3.2 %copy-start = (bf16[1024,768]{1,0:T(8,128)(2,1)S(1)}, bf16[1024,768]{1,0:T(8,128)(2,1)}, u32[]{:S(2)}) copy-start(bf16[1024,768]{1,0:T(8,128)(2,1)} %param.6) | copy-start | bytes 4718596
  0.6 4.9 %collective-permute-start.1 = (s32[1024]{0:T(1024)}, s32[1024]{0:T(1024)S(1)}, u32[]{:S(2)}, u32[]{:S(2)}) collective-permute-start(s32[1024]{0:T(1024)} %param.7), channel_id=1, source_target_pairs={{0,2},{1,3},{2,0},{3,1},{4,6},{5,7},{6,4},{7,5},{8,10},{9,11},{10,... | collective-permute-start | bytes 12296 | tf_op jit(solution)/shard_map/ppermute | solution.py:305
  3.6 1.9 %collective-permute-start = (s32[1024]{0:T(1024)}, s32[1024]{0:T(1024)S(1)}, u32[]{:S(2)}, u32[]{:S(2)}) collective-permute-start(s32[1024]{0:T(1024)} %param.7), channel_id=1, source_target_pairs={{0,1},{1,0},{2,3},{3,2},{4,5},{5,4},{6,7},{7,6},{8,9},{9,8},{10,11... | collective-permute-start | bytes 12296 | tf_op jit(solution)/shard_map/ppermute | solution.py:305
  3.7 3.2 %collective-permute-start.2 = (s32[1024]{0:T(1024)}, s32[1024]{0:T(1024)S(1)}, u32[]{:S(2)}, u32[]{:S(2)}) collective-permute-start(s32[1024]{0:T(1024)} %param.7), channel_id=1, source_target_pairs={{0,3},{1,2},{2,1},{3,0},{4,7},{5,6},{6,5},{7,4},{8,11},{9,10},{10,... | collective-permute-start | bytes 12296 | tf_op jit(solution)/shard_map/ppermute | solution.py:305
  5.5 16.0 %copy-start.31 = (s32[1024]{0:T(1024)}, s32[1024]{0:T(1024)S(1)}, u32[]{:S(2)}) copy-start(s32[1024]{0:T(1024)S(1)} %collective-permute-done.1) | copy-start | bytes 12292
  6.9 14.7 %copy-start.32 = (s32[1024]{0:T(1024)}, s32[1024]{0:T(1024)S(1)}, u32[]{:S(2)}) copy-start(s32[1024]{0:T(1024)S(1)} %collective-permute-done.2) | copy-start | bytes 12292
  6.9 40.5 %collective-permute-start.3 = (bf16[1024,512]{1,0:T(8,128)(2,1)S(1)}, bf16[1024,512]{1,0:T(8,128)(2,1)}, u32[]{:S(2)}, u32[]{:S(2)}) collective-permute-start(bf16[1024,512]{1,0:T(8,128)(2,1)S(1)} %constant_dynamic-slice_fusion.2), channel_id=1, source_target_pairs={{0,2},{1,3},{2,0},{3,1},{4,6},{5,7},{6,4},{7,5},{8,10},{9,11},{10,... | collective-permute-start | bytes 3145736 | tf_op jit(solution)/shard_map/ppermute | solution.py:311
  7.6 39.8 %collective-permute-start.5 = (bf16[512,768]{0,1:T(8,128)(2,1)S(1)}, bf16[512,768]{0,1:T(8,128)(2,1)}, u32[]{:S(2)}, u32[]{:S(2)}) collective-permute-start(bf16[512,768]{0,1:T(8,128)(2,1)S(1)} %copy.13), channel_id=1, source_target_pairs={{0,12},{15,3},{4,13},{11,2},{16,28},{31,19},{20,29},{27,18}} | collective-permute-start | bytes 2359304 | tf_op jit(solution)/shard_map/ppermute | solution.py:308
  14.0 33.4 %collective-permute-start.4 = (bf16[512,768]{0,1:T(8,128)(2,1)S(1)}, bf16[512,768]{0,1:T(8,128)(2,1)}, u32[]{:S(2)}, u32[]{:S(2)}) collective-permute-start(bf16[512,768]{0,1:T(8,128)(2,1)S(1)} %copy.13), channel_id=1, source_target_pairs={{0,4},{15,11},{1,8},{14,7},{4,1},{11,14},{5,9},{10,6},{16,20},{31,... | collective-permute-start | bytes 2359304 | tf_op jit(solution)/shard_map/ppermute | solution.py:307
  17.0 5.1 %copy-start.34 = (s32[16]{0:T(128)S(1)}, s32[16]{0:T(128)}, u32[]{:S(2)}) copy-start(s32[16]{0:T(128)} %param.11) | copy-start | bytes 196
  21.6 3.0 %collective-permute-start.7 = (bf16[512,512]{1,0:T(8,128)(2,1)}, bf16[512,512]{1,0:T(8,128)(2,1)S(1)}, u32[]{:S(2)}, u32[]{:S(2)}) collective-permute-start(bf16[512,512]{1,0:T(8,128)(2,1)} %get-tuple-element.102), channel_id=1, source_target_pairs={{0,1},{1,0},{2,3},{3,2},{4,5},{5,4},{6,7},{7,6},{8,9},{9,8},{10,11... | collective-permute-start | bytes 1572872 | tf_op jit(solution)/shard_map/ppermute | solution.py:316
  21.6 3.0 %collective-permute-start.6 = (bf16[512,512]{1,0:T(8,128)(2,1)}, bf16[512,512]{1,0:T(8,128)(2,1)S(1)}, u32[]{:S(2)}, u32[]{:S(2)}) collective-permute-start(bf16[512,512]{1,0:T(8,128)(2,1)} %get-tuple-element.103), channel_id=1, source_target_pairs={{0,1},{1,0},{2,3},{3,2},{4,5},{5,4},{6,7},{7,6},{8,9},{9,8},{10,11... | collective-permute-start | bytes 1572872 | tf_op jit(solution)/shard_map/ppermute | solution.py:316
  24.6 0.8 copy-start.20
  24.6 30.1 %collective-permute-start.11 = (bf16[1024,512]{1,0:T(8,128)(2,1)}, bf16[1024,512]{1,0:T(8,128)(2,1)}, u32[]{:S(2)}, u32[]{:S(2)}) collective-permute-start(bf16[1024,512]{1,0:T(8,128)(2,1)} %constant_dynamic-slice_fusion.1), channel_id=1, source_target_pairs={{0,3},{1,2},{2,1},{3,0},{4,7},{5,6},{6,5},{7,4},{8,11},{9,10},{10,... | collective-permute-start | bytes 3145736 | tf_op jit(solution)/shard_map/ppermute | solution.py:313
  25.4 0.8 copy-start.21
  47.4 1.8 %copy-start.33 = (bf16[768,512]{1,0:T(8,128)(2,1)S(1)}, bf16[768,512]{1,0:T(8,128)(2,1)}, u32[]{:S(2)}) copy-start(bf16[768,512]{1,0:T(8,128)(2,1)} %get-tuple-element.68) | copy-start | bytes 2359300
  49.0 41.0 %copy-start.3 = (bf16[512,768]{0,1:T(8,128)(2,1)}, bf16[512,768]{0,1:T(8,128)(2,1)S(1)}, u32[]{:S(2)}) copy-start(bf16[512,768]{0,1:T(8,128)(2,1)S(1)} %add_select_fusion) | copy-start | bytes 2359300
  49.0 7.2 %copy-start.11 = (bf16[768,512]{1,0:T(8,128)(2,1)S(1)}, bf16[768,512]{1,0:T(8,128)(2,1)}, u32[]{:S(2)}) copy-start(bf16[768,512]{1,0:T(8,128)(2,1)} %get-tuple-element.72) | copy-start | bytes 2359300
  49.0 5.7 %collective-permute-start.9 = (bf16[512,768]{0,1:T(8,128)(2,1)S(1)}, bf16[512,768]{0,1:T(8,128)(2,1)S(1)}, u32[]{:S(2)}, u32[]{:S(2)}) collective-permute-start(bf16[512,768]{0,1:T(8,128)(2,1)S(1)} %add_select_fusion), channel_id=1, source_target_pairs={{0,1},{1,0},{2,3},{3,2},{4,5},{5,4},{6,7},{7,6},{8,9},{9,8},{10,11... | collective-permute-start | bytes 2359304 | tf_op jit(solution)/shard_map/ppermute | solution.py:327
  49.1 5.5 %collective-permute-start.10 = (bf16[768,512]{1,0:T(8,128)(2,1)S(1)}, bf16[768,512]{1,0:T(8,128)(2,1)S(1)}, u32[]{:S(2)}, u32[]{:S(2)}) collective-permute-start(bf16[768,512]{1,0:T(8,128)(2,1)S(1)} %copy-done.33), channel_id=1, source_target_pairs={{0,1},{1,0},{2,3},{3,2},{4,5},{5,4},{6,7},{7,6},{8,9},{9,8},{10,11... | collective-permute-start | bytes 2359304 | tf_op jit(solution)/shard_map/ppermute | solution.py:328
  49.6 19.5 %collective-permute-start.8 = (bf16[512,768]{0,1:T(8,128)(2,1)S(1)}, bf16[512,768]{0,1:T(8,128)(2,1)S(1)}, u32[]{:S(2)}, u32[]{:S(2)}) collective-permute-start(bf16[512,768]{0,1:T(8,128)(2,1)S(1)} %add_select_fusion), channel_id=1, source_target_pairs={{0,16},{16,0},{1,17},{17,1},{2,18},{18,2},{3,19},{19,3},{4,20},{20... | collective-permute-start | bytes 2359304 | tf_op jit(solution)/shard_map/ppermute | solution.py:326
  51.1 18.6 %collective-permute-start.16 = (bf16[768,512]{1,0:T(8,128)(2,1)}, bf16[768,512]{1,0:T(8,128)(2,1)S(1)}, u32[]{:S(2)}, u32[]{:S(2)}) collective-permute-start(bf16[768,512]{1,0:T(8,128)(2,1)} %get-tuple-element.84), channel_id=1, source_target_pairs={{0,1},{1,0},{2,3},{3,2},{4,5},{5,4},{6,7},{7,6},{8,9},{9,8},{10,11... | collective-permute-start | bytes 2359304 | tf_op jit(solution)/shard_map/ppermute | solution.py:329
  54.7 0.9 copy-start.14
  57.5 14.5 %collective-permute-start.14 = (bf16[512,512]{1,0:T(8,128)(2,1)}, bf16[512,512]{1,0:T(8,128)(2,1)}, u32[]{:S(2)}, u32[]{:S(2)}) collective-permute-start(bf16[512,512]{1,0:T(8,128)(2,1)} %fusion.refs_7_), channel_id=1, source_target_pairs={{0,2},{1,3},{2,0},{3,1},{4,6},{5,7},{6,4},{7,5},{8,10},{9,11},{10,... | collective-permute-start | bytes 1572872 | tf_op jit(solution)/shard_map/ppermute | solution.py:332
  69.1 20.9 %copy-start.2 = (bf16[512,768]{0,1:T(8,128)(2,1)}, bf16[512,768]{0,1:T(8,128)(2,1)S(1)}, u32[]{:S(2)}) copy-start(bf16[512,768]{0,1:T(8,128)(2,1)S(1)} %collective-permute-done.8) | copy-start | bytes 2359300
  69.2 2.6 %collective-permute-start.13 = (bf16[256,768]{0,1:T(8,128)(2,1)S(1)}, bf16[256,768]{0,1:T(8,128)(2,1)S(1)}, u32[]{:S(2)}, u32[]{:S(2)}) collective-permute-start(bf16[256,768]{0,1:T(8,128)(2,1)S(1)} %get-tuple-element.114), channel_id=1, source_target_pairs={{0,1},{1,0},{2,3},{3,2},{4,5},{5,4},{6,7},{7,6},{8,9},{9,8},{10,11... | collective-permute-start | bytes 1179656 | tf_op jit(solution)/shard_map/ppermute | solution.py:336
  69.2 2.5 %collective-permute-start.12 = (bf16[256,768]{0,1:T(8,128)(2,1)S(1)}, bf16[256,768]{0,1:T(8,128)(2,1)S(1)}, u32[]{:S(2)}, u32[]{:S(2)}) collective-permute-start(bf16[256,768]{0,1:T(8,128)(2,1)S(1)} %get-tuple-element.115), channel_id=1, source_target_pairs={{0,1},{1,0},{2,3},{3,2},{4,5},{5,4},{6,7},{7,6},{8,9},{9,8},{10,11... | collective-permute-start | bytes 1179656 | tf_op jit(solution)/shard_map/ppermute | solution.py:336
  69.7 2.4 %copy-start.12 = (bf16[768,512]{1,0:T(8,128)(2,1)}, bf16[768,512]{1,0:T(8,128)(2,1)S(1)}, u32[]{:S(2)}) copy-start(bf16[768,512]{1,0:T(8,128)(2,1)S(1)} %collective-permute-done.16) | copy-start | bytes 2359300
  72.7 1.7 %copy-start.8 = (bf16[768,512]{1,0:T(8,128)(2,1)S(1)}, bf16[768,512]{1,0:T(8,128)(2,1)}, u32[]{:S(2)}) copy-start(bf16[768,512]{1,0:T(8,128)(2,1)} %get-tuple-element.83.refs_7_) | copy-start | bytes 2359300
  72.8 2.3 %copy-start.19 = (f32[1024,512]{1,0:T(8,128)S(1)}, f32[1024,512]{1,0:T(8,128)}, u32[]{:S(2)}) copy-start(f32[1024,512]{1,0:T(8,128)} %get-tuple-element.86) | copy-start | bytes 6291460
  73.4 2.0 %copy-start.18 = (f32[1024,512]{1,0:T(8,128)S(1)}, f32[1024,512]{1,0:T(8,128)}, u32[]{:S(2)}) copy-start(f32[1024,512]{1,0:T(8,128)} %get-tuple-element.85) | copy-start | bytes 6291460
  73.4 14.9 %collective-permute-start.15 = (bf16[512,512]{1,0:T(8,128)(2,1)S(1)}, bf16[512,512]{1,0:T(8,128)(2,1)S(1)}, u32[]{:S(2)}, u32[]{:S(2)}) collective-permute-start(bf16[512,512]{1,0:T(8,128)(2,1)S(1)} %fusion.1), channel_id=1, source_target_pairs={{0,2},{1,3},{2,0},{3,1},{4,6},{5,7},{6,4},{7,5},{8,10},{9,11},{10,... | collective-permute-start | bytes 1572872 | tf_op jit(solution)/shard_map/ppermute | solution.py:340
  76.9 1.5 %copy-start.13 = (bf16[768,512]{1,0:T(8,128)(2,1)S(1)}, bf16[768,512]{1,0:T(8,128)(2,1)}, u32[]{:S(2)}) copy-start(bf16[768,512]{1,0:T(8,128)(2,1)} %copy-done.12) | copy-start | bytes 2359300
  77.0 11.2 %copy-start.4 = (bf16[2048,256]{1,0:T(8,128)(2,1)}, bf16[2048,256]{1,0:T(8,128)(2,1)S(1)}, u32[]{:S(2)}) copy-start(bf16[2048,256]{1,0:T(8,128)(2,1)S(1)} %pad_maximum_fusion.refs_7_.refs_8_.refs_11_.refs_12_) | copy-start | bytes 3145732
  77.0 32.5 %collective-permute-start.17 = (bf16[2048,256]{1,0:T(8,128)(2,1)S(1)}, bf16[2048,256]{1,0:T(8,128)(2,1)S(1)}, u32[]{:S(2)}, u32[]{:S(2)}) collective-permute-start(bf16[2048,256]{1,0:T(8,128)(2,1)S(1)} %pad_maximum_fusion.refs_7_.refs_8_.refs_11_.refs_12_), channel_id=1, source_target_pairs={{0,2},{1,3},{2,0},{3,1},{4,6},{5,7},{6,4},{7,5},{8,10},{9,11},{10,... | collective-permute-start | bytes 3145736 | tf_op jit(solution)/shard_map/ppermute | solution.py:353
  88.3 4.2 %collective-permute-start.18 = (bf16[2048,256]{1,0:T(8,128)(2,1)S(1)}, bf16[2048,256]{1,0:T(8,128)(2,1)S(1)}, u32[]{:S(2)}, u32[]{:S(2)}) collective-permute-start(bf16[2048,256]{1,0:T(8,128)(2,1)S(1)} %pad_maximum_fusion.refs_7_.refs_8_.refs_11_.refs_12_), channel_id=1, source_target_pairs={{0,1},{1,0},{2,3},{3,2},{4,5},{5,4},{6,7},{7,6},{8,9},{9,8},{10,11... | collective-permute-start | bytes 3145736 | tf_op jit(solution)/shard_map/ppermute | solution.py:360
  88.5 2.9 %copy-start.22 = (bf16[512,256]{1,0:T(8,128)(2,1)}, bf16[512,256]{1,0:T(8,128)(2,1)S(1)}, u32[]{:S(2)}) copy-start(bf16[512,256]{1,0:T(8,128)(2,1)S(1)} %get-tuple-element.111.refs_9_) | copy-start | bytes 786436
  88.6 2.9 %copy-start.24 = (bf16[512,256]{1,0:T(8,128)(2,1)}, bf16[512,256]{1,0:T(8,128)(2,1)S(1)}, u32[]{:S(2)}) copy-start(bf16[512,256]{1,0:T(8,128)(2,1)S(1)} %get-tuple-element.110.refs_10_) | copy-start | bytes 786436
  88.9 4.6 %copy-start.9 = (bf16[1024,256]{1,0:T(8,128)(2,1)}, bf16[1024,256]{1,0:T(8,128)(2,1)S(1)}, u32[]{:S(2)}) copy-start(bf16[1024,256]{1,0:T(8,128)(2,1)S(1)} %pad_maximum_fusion.1.refs_13_.refs_14_) | copy-start | bytes 1572868
  88.9 3.5 %collective-permute-start.21 = (bf16[1024,256]{1,0:T(8,128)(2,1)S(1)}, bf16[1024,256]{1,0:T(8,128)(2,1)S(1)}, u32[]{:S(2)}, u32[]{:S(2)}) collective-permute-start(bf16[1024,256]{1,0:T(8,128)(2,1)S(1)} %pad_maximum_fusion.1.refs_13_.refs_14_), channel_id=1, source_target_pairs={{0,1},{1,0},{2,3},{3,2},{4,5},{5,4},{6,7},{7,6},{8,9},{9,8},{10,11... | collective-permute-start | bytes 1572872 | tf_op jit(solution)/shard_map/ppermute | solution.py:362
  89.5 2.6 %collective-permute-start.20 = (bf16[512,256]{1,0:T(8,128)(2,1)S(1)}, bf16[512,256]{1,0:T(8,128)(2,1)S(1)}, u32[]{:S(2)}, u32[]{:S(2)}) collective-permute-start(bf16[512,256]{1,0:T(8,128)(2,1)S(1)} %get-tuple-element.110.refs_10_), channel_id=1, source_target_pairs={{0,1},{1,0},{2,3},{3,2},{4,5},{5,4},{6,7},{7,6},{8,9},{9,8},{10,11... | collective-permute-start | bytes 786440 | tf_op jit(solution)/shard_map/ppermute | solution.py:361
  89.6 2.9 %collective-permute-start.19 = (bf16[512,256]{1,0:T(8,128)(2,1)S(1)}, bf16[512,256]{1,0:T(8,128)(2,1)S(1)}, u32[]{:S(2)}, u32[]{:S(2)}) collective-permute-start(bf16[512,256]{1,0:T(8,128)(2,1)S(1)} %get-tuple-element.111.refs_9_), channel_id=1, source_target_pairs={{0,1},{1,0},{2,3},{3,2},{4,5},{5,4},{6,7},{7,6},{8,9},{9,8},{10,11... | collective-permute-start | bytes 786440 | tf_op jit(solution)/shard_map/ppermute | solution.py:361
  92.1 1.4 copy-start.27
  92.4 1.1 copy-start.28
  92.4 1.2 copy-start.17
  92.4 1.0 copy-start.7
  93.6 17.2 %copy-start.23 = (bf16[512,256]{1,0:T(8,128)(2,1)S(1)}, bf16[512,256]{1,0:T(8,128)(2,1)}, u32[]{:S(2)}) copy-start(bf16[512,256]{1,0:T(8,128)(2,1)} %copy-done.22) | copy-start | bytes 786436
  93.6 17.9 %copy-start.10 = (bf16[1024,256]{1,0:T(8,128)(2,1)S(1)}, bf16[1024,256]{1,0:T(8,128)(2,1)}, u32[]{:S(2)}) copy-start(bf16[1024,256]{1,0:T(8,128)(2,1)} %copy-done.9) | copy-start | bytes 1572868
  109.5 17.6 %copy-start.5 = (bf16[2048,256]{1,0:T(8,128)(2,1)}, bf16[2048,256]{1,0:T(8,128)(2,1)S(1)}, u32[]{:S(2)}) copy-start(bf16[2048,256]{1,0:T(8,128)(2,1)S(1)} %collective-permute-done.17.refs_7_.refs_8_) | copy-start | bytes 3145732
  109.5 17.6 %collective-permute-start.25 = (bf16[2048,256]{1,0:T(8,128)(2,1)S(1)}, bf16[2048,256]{1,0:T(8,128)(2,1)S(1)}, u32[]{:S(2)}, u32[]{:S(2)}) collective-permute-start(bf16[2048,256]{1,0:T(8,128)(2,1)S(1)} %collective-permute-done.17.refs_7_.refs_8_), channel_id=1, source_target_pairs={{0,1},{1,0},{2,3},{3,2},{4,5},{5,4},{6,7},{7,6},{8,9},{9,8},{10,11... | collective-permute-start | bytes 3145736 | tf_op jit(solution)/shard_map/ppermute | solution.py:379
  109.5 9.3 %collective-permute-start.24 = (bf16[512,256]{1,0:T(8,128)(2,1)}, bf16[512,256]{1,0:T(8,128)(2,1)S(1)}, u32[]{:S(2)}, u32[]{:S(2)}) collective-permute-start(bf16[512,256]{1,0:T(8,128)(2,1)} %copy-done.24), channel_id=1, source_target_pairs={{0,2},{1,3},{2,0},{3,1},{4,6},{5,7},{6,4},{7,5},{8,10},{9,11},{10,... | collective-permute-start | bytes 786440 | tf_op jit(solution)/shard_map/ppermute | solution.py:358
  110.8 13.6 %collective-permute-start.23 = (bf16[512,256]{1,0:T(8,128)(2,1)S(1)}, bf16[512,256]{1,0:T(8,128)(2,1)S(1)}, u32[]{:S(2)}, u32[]{:S(2)}) collective-permute-start(bf16[512,256]{1,0:T(8,128)(2,1)S(1)} %copy-done.23), channel_id=1, source_target_pairs={{0,2},{1,3},{2,0},{3,1},{4,6},{5,7},{6,4},{7,5},{8,10},{9,11},{10,... | collective-permute-start | bytes 786440 | tf_op jit(solution)/shard_map/ppermute | solution.py:358
  111.6 23.9 %collective-permute-start.22 = (bf16[1024,256]{1,0:T(8,128)(2,1)S(1)}, bf16[1024,256]{1,0:T(8,128)(2,1)S(1)}, u32[]{:S(2)}, u32[]{:S(2)}) collective-permute-start(bf16[1024,256]{1,0:T(8,128)(2,1)S(1)} %copy-done.10), channel_id=1, source_target_pairs={{0,2},{1,3},{2,0},{3,1},{4,6},{5,7},{6,4},{7,5},{8,10},{9,11},{10,... | collective-permute-start | bytes 1572872 | tf_op jit(solution)/shard_map/ppermute | solution.py:359
  118.9 8.2 %copy-start.25 = (bf16[512,256]{1,0:T(8,128)(2,1)}, bf16[512,256]{1,0:T(8,128)(2,1)S(1)}, u32[]{:S(2)}) copy-start(bf16[512,256]{1,0:T(8,128)(2,1)S(1)} %collective-permute-done.24.refs_10_) | copy-start | bytes 786436
  124.5 2.6 %copy-start.26 = (bf16[512,256]{1,0:T(8,128)(2,1)}, bf16[512,256]{1,0:T(8,128)(2,1)S(1)}, u32[]{:S(2)}) copy-start(bf16[512,256]{1,0:T(8,128)(2,1)S(1)} %collective-permute-done.23.refs_9_) | copy-start | bytes 786436
  124.5 1.5 %collective-permute-start.26 = (bf16[512,256]{1,0:T(8,128)(2,1)S(1)}, bf16[512,256]{1,0:T(8,128)(2,1)S(1)}, u32[]{:S(2)}, u32[]{:S(2)}) collective-permute-start(bf16[512,256]{1,0:T(8,128)(2,1)S(1)} %collective-permute-done.23.refs_9_), channel_id=1, source_target_pairs={{0,1},{1,0},{2,3},{3,2},{4,5},{5,4},{6,7},{7,6},{8,9},{9,8},{10,11... | collective-permute-start | bytes 786440 | tf_op jit(solution)/shard_map/ppermute | solution.py:380
  124.5 1.9 %collective-permute-start.27 = (bf16[512,256]{1,0:T(8,128)(2,1)S(1)}, bf16[512,256]{1,0:T(8,128)(2,1)S(1)}, u32[]{:S(2)}, u32[]{:S(2)}) collective-permute-start(bf16[512,256]{1,0:T(8,128)(2,1)S(1)} %collective-permute-done.24.refs_10_), channel_id=1, source_target_pairs={{0,1},{1,0},{2,3},{3,2},{4,5},{5,4},{6,7},{7,6},{8,9},{9,8},{10,11... | collective-permute-start | bytes 786440 | tf_op jit(solution)/shard_map/ppermute | solution.py:380
  126.0 1.1 copy-start.29
  126.4 0.7 copy-start.30
  127.1 1.0 copy-start.6
  135.5 2.0 %copy-start.15 = (bf16[1024,256]{1,0:T(8,128)(2,1)}, bf16[1024,256]{1,0:T(8,128)(2,1)S(1)}, u32[]{:S(2)}) copy-start(bf16[1024,256]{1,0:T(8,128)(2,1)S(1)} %collective-permute-done.22.refs_9_.refs_10_) | copy-start | bytes 1572868
  135.5 2.0 %collective-permute-start.28 = (bf16[1024,256]{1,0:T(8,128)(2,1)S(1)}, bf16[1024,256]{1,0:T(8,128)(2,1)S(1)}, u32[]{:S(2)}, u32[]{:S(2)}) collective-permute-start(bf16[1024,256]{1,0:T(8,128)(2,1)S(1)} %collective-permute-done.22.refs_9_.refs_10_), channel_id=1, source_target_pairs={{0,1},{1,0},{2,3},{3,2},{4,5},{5,4},{6,7},{7,6},{8,9},{9,8},{10,11... | collective-permute-start | bytes 1572872 | tf_op jit(solution)/shard_map/ppermute | solution.py:383
  137.5 0.8 copy-start.16
  138.2 7.3 %copy-start.1 = (bf16[1024,768]{1,0:T(8,128)(2,1)S(1)}, bf16[1024,768]{1,0:T(8,128)(2,1)}, u32[]{:S(2)}) copy-start(bf16[1024,768]{1,0:T(8,128)(2,1)} %param.6) | copy-start | bytes 4718596

commit v4 on v3

--- a/solution.py
+++ b/solution.py
@@ -115,7 +115,7 @@
 FINAL_LIMIT = 28 * 1024 * 1024
 
 
-def call(kernel, scalars, grid, ins, outs, deps=(), scratch=(), alias=None, limit=VMEM_LIMIT, cost=(1, 1)):
+def call(kernel, scalars, grid, ins, outs, deps=(), scratch=(), alias=None, alias_in=None, limit=VMEM_LIMIT, cost=(1, 1)):
     n_in, n_out, n_dep = len(ins), len(outs), len(deps)
 
     def body(*refs):
@@ -136,7 +136,8 @@
             scratch_shapes=list(scratch),
         ),
         out_shape=[jax.ShapeDtypeStruct(s, d) for s, d, _, _ in outs],
-        input_output_aliases={1 + n_in + i: o for i, o in (alias or {}).items()},
+        input_output_aliases={1 + n_in + i: o for i, o in (alias or {}).items()}
+        | {1 + i: o for i, o in (alias_in or {}).items()},
         compiler_params=pltpu.CompilerParams(vmem_limit_bytes=VMEM_LIMIT),
         cost_estimate=pl.CostEstimate(flops=cost[0], bytes_accessed=cost[1], transcendentals=0),
     )(scalars, *[a for a, _, _ in ins], *deps)
@@ -280,6 +281,52 @@
         [(mean.shape, F32, block, place)] * 2,
         tuple(before),
         alias={0: 0, 1: 1} if before else None,
+        limit=FINAL_LIMIT,
+    )
+
+
+def final_halves(scal, tab_t, tab_t_sq, pieces, mean, precision, part, width, before, second):
+    rows, half = tab_t.shape
+    cut = pieces[0][0][0][0].shape[1]
+    n = len(pieces)
+    inv_root, inv_width = 1.0 / (width ** 0.5), 1.0 / width
+    state = (mean, *before) if second else (precision,)
+    first_s = 2 + len(state)
+
+    def kernel(sc, ins, outs, scratch):
+        for m in range(n):
+            @pl.when(pl.program_id(0) == m)
+            def _(m=m):
+                grad = dot(ins[0][...], ins[first_s + 2 * m][...]) * inv_root
+                sq_sum = dot(ins[1][...], ins[first_s + 1 + 2 * m][...]) * (0.3 * inv_width)
+                if second:
+                    old = ins[2][...]
+                    new_precision = ins[4][...] + sq_sum
+                    outs[0][...] = old - 0.5 * (ins[3][...] + grad + 0.1 * old) / (new_precision + 0.1)
+                    outs[1][...] = new_precision
+                else:
+                    outs[0][...] = grad
+                    outs[1][...] = 0.7 * ins[2][...] + sq_sum
+
+    def place(p, sc):
+        at = [(sc[0] ^ flip) * part + start for _, flip, start in pieces]
+        out = at[0]
+        for m in range(1, n):
+            out = jnp.where(p == m, at[m], out)
+        return 0, pl.multiple_of(out, 128)
+
+    whole = lambda p, sc: (0, 0)
+    block = (pl.Element(rows), pl.Element(cut))
+    slots = [slot for pair, _, _ in pieces for slot in pair]
+    return call(
+        kernel, scal, (n,),
+        [(a, a.shape, whole) for a in (tab_t, tab_t_sq)]
+        + [(a, block, place) for a in state]
+        + [(s, (half, cut), lambda p, sc, h=h: (h, 0)) for s, h in slots],
+        [(mean.shape, F32, block, place)] * 2,
+        () if second else tuple(before),
+        alias=None if second else {0: 0, 1: 1},
+        alias_in={3: 0, 4: 1} if second else None,
         limit=FINAL_LIMIT,
     )
 
@@ -375,13 +422,27 @@
     outs = write(
         (), chunk0(send_a, b0, 0), chunk1(send_a, last, 0), chunk0(core_a2, core_b0, 1), chunk1(core_a2, core_last, 1)
     )
-    far_a, far_b0 = after(far_a, *outs), [after(s, *outs) for s in far_b0]
+    far_a = after(far_a, *outs)
     fwd_a = lax.ppermute(far_a, "dp", CORE)
+
+    def write_half(outs, second, *pieces):
+        h = int(second)
+        return final_halves(scal, tab_t[h], tab_t_sq[h], pieces, mean, precision, part, width, outs, second)
+
+    pairs = [[(s, 2 * k), (s, 2 * k + 1)] for s in (far_a, fwd_a) for k in (0, 1)]
+    outs = write_half(
+        outs, False, (pairs[0], 2, starts[0]), (pairs[1], 2, starts[1]), (pairs[2], 3, starts[0]), (pairs[3], 3, starts[1])
+    )
+    far_b0 = [after(s, *outs) for s in far_b0]
     fwd_b0 = [lax.ppermute(s, "dp", CORE) for s in far_b0]
-    outs = write(outs, chunk0(far_a, far_b0, 2), chunk0(fwd_a, fwd_b0, 3))
+    outs = write_half(
+        outs, True, ([(s, 0) for s in far_b0], 2, starts[0]), ([(s, 0) for s in fwd_b0], 3, starts[0])
+    )
     far_last = after(far_last, *outs)
     fwd_last = lax.ppermute(far_last, "dp", CORE)
-    outs = write(outs, chunk1(far_a, far_last, 2), chunk1(fwd_a, fwd_last, 3))
+    outs = write_half(
+        outs, True, ([(far_last, 0), (far_last, 1)], 2, starts[1]), ([(fwd_last, 0), (fwd_last, 1)], 3, starts[1])
+    )
     return tuple(outs)
 
 

time: 147 us -> 145 us (0.986)
  waiting for transfers between devices: 36.6 us -> 29.4 us
  Pallas kernels: 56.4 us -> 61.8 us
    ppermute x2, waiting for transfers between devices: 11.6 us -> 2.97 us  [on_device(): far_b0 = [lax.ppermute(s, 'dp', CHIP) for s in b0]]
    pallas_call x6 -> x7, Pallas kernels: 56.4 us -> 61.8 us  [call(): pl.pallas_call(body, grid_spec=pltpu.PrefetchScalarGridSpec(num_scalar_pr...]
    ppermute x1, waiting for transfers between devices: 0.01 us -> 1.95 us  [on_device(): far_last = lax.ppermute(last, 'dp', CHIP)]
    unnamed x72 -> x70, local copies, waits for them, and re-layouts: 7.11 us -> 8.43 us
  transfers between devices with their start and end apart: 29 -> 29, of which waited for: 13 -> 12; matrix products, arithmetic and copies ran while one was open for 14% -> 14% of each run, Pallas kernels for 34% -> 39%
where the time goes in v4:
time: 145 us
  Pallas kernels  61.8 us (43%)
  waiting for transfers between devices  29.4 us (20%)
  starting transfers between devices  22.4 us (15%)
  local copies, waits for them, and re-layouts  16.9 us (12%)
  matrix products  7.05 us (5%)
  other arithmetic  5.83 us (4%)
    pallas_call x7, Pallas kernels, call(): pl.pallas_call(body, grid_spec=pltpu.PrefetchScalarGridSpec(num_scalar_pr...  61.8 us
    ppermute x1, waiting for transfers between devices, on_device(): pre_b = lax.ppermute(out_b, 'dp', CHIP)  9.25 us
    unnamed x70, local copies, waits for them, and re-layouts  8.43 us
    dot_general x8, matrix products, dot(): return jnp.dot(a, b, preferred_element_type=F32)  7.05 us
    ppermute x1, starting transfers between devices, on_device(): far_a = lax.ppermute(own_a, both, to_far)  6.41 us
    dynamic_slice x3, local copies, waits for them, and re-layouts, cols(): return lax.dynamic_slice(a, (row, (dp_pos ^ flip) * part), (rows, part))  5.86 us
    ppermute x1, waiting for transfers between devices, on_device(): far_a = lax.ppermute(send_a, 'dp', CHIP)  4.33 us
    ppermute x1, waiting for transfers between devices, on_device(): x2_in = lax.ppermute(x2, 'dp', CROSS)  3.57 us
  transfers between devices with their start and end apart: 29, of which 12 were waited for; matrix products, arithmetic and copies ran while one was open for 14% of the time, Pallas kernels for 39%

profile of v4, /device:TPU:0, one launch (start us, length us, event | category | flops | bytes accessed | tf_op | source)
XLA Modules:
  0.0 144.5 jit_solution(12486132325677125946)
XLA Ops:
  0.6 3.0 %collective-permute-start.1 = (s32[1024]{0:T(1024)}, s32[1024]{0:T(1024)S(1)}, u32[]{:S(2)}, u32[]{:S(2)}) collective-permute-start(s32[1024]{0:T(1024)} %param.7), channel_id=1, source_target_pairs={{0,2},{1,3},{2,0},{3,1},{4,6},{5,7},{6,4},{7,5},{8,10},{9,11},{10,... | collective-permute-start | bytes 12296 | tf_op jit(solution)/shard_map/ppermute | solution.py:352
  4.2 1.3 constant_dynamic-slice_fusion.2
  5.5 1.4 collective-permute-done.2
  6.9 0.7 collective-permute-start.3
  7.6 6.4 %collective-permute-start.5 = (bf16[512,768]{0,1:T(8,128)(2,1)S(1)}, bf16[512,768]{0,1:T(8,128)(2,1)}, u32[]{:S(2)}, u32[]{:S(2)}) collective-permute-start(bf16[512,768]{0,1:T(8,128)(2,1)S(1)} %copy.15), channel_id=1, source_target_pairs={{0,12},{15,3},{4,13},{11,2},{16,28},{31,19},{20,29},{27,18}} | collective-permute-start | bytes 2359304 | tf_op jit(solution)/shard_map/ppermute | solution.py:355
  14.0 3.0 %collective-permute-start.4 = (bf16[512,768]{0,1:T(8,128)(2,1)S(1)}, bf16[512,768]{0,1:T(8,128)(2,1)}, u32[]{:S(2)}, u32[]{:S(2)}) collective-permute-start(bf16[512,768]{0,1:T(8,128)(2,1)S(1)} %copy.15), channel_id=1, source_target_pairs={{0,4},{15,11},{1,8},{14,7},{4,1},{11,14},{5,9},{10,6},{16,20},{31,... | collective-permute-start | bytes 2359304 | tf_op jit(solution)/shard_map/ppermute | solution.py:354
  17.0 2.3 %constant_dynamic-slice_fusion.1 = bf16[1024,512]{1,0:T(8,128)(2,1)} fusion(bf16[1024,2048]{1,0:T(8,128)(2,1)} %refs_2_.3, s32[]{:T(128)S(6)} %select_n.29), kind=kLoop, calls=%fused_computation.28 | loop fusion | bytes 2097156 | tf_op jit(solution)/shard_map/dynamic_slice | solution.py:350
  19.3 2.2 %constant_dynamic-slice_fusion.4 = (bf16[512,512]{1,0:T(8,128)(2,1)}, bf16[512,512]{1,0:T(8,128)(2,1)}) fusion(bf16[1024,2048]{1,0:T(8,128)(2,1)} %refs_2_.3, s32[]{:T(128)S(6)} %select_n.30), kind=kLoop, calls=%fused_computation.31 | loop fusion | bytes 2097156 | tf_op jit(solution)/shard_map/dynamic_slice | solution.py:350
  21.6 0.5 collective-permute-start.6
  22.1 0.6 dynamic_slice.19
  22.7 1.2 stack.20.refs_0_
  24.0 0.6 fusion.3
  24.6 0.8 copy-done.19
  25.4 0.8 copy-done.20
  26.2 12.6 %shard_map.77 = (bf16[768,512]{1,0:T(8,128)(2,1)}, bf16[768,512]{1,0:T(8,128)(2,1)}, bf16[768,512]{1,0:T(8,128)(2,1)}, bf16[768,512]{1,0:T(8,128)(2,1)}) custom-call(s32[5]{0:T(128)} %stack.20.refs_0_, f32[768,2048]{1,0:T(8,128)} %refs_3_.5, f32[768,2048]{1,0:T(8,128)} %refs_3_.3, bf16[512,512]{1,0:T(8,128)(2,1)} %copy-done.20, bf16[512,512]{1,0:T(8,128)(2,1)} %copy-done.19), custom_call_target="tpu_custom_call" | custom-call | flops 1 | bytes 1 | tf_op jit(solution)/shard_map/pallas_call | solution.py:129
  38.7 8.6 %shard_map.78 = (f32[1024,512]{1,0:T(8,128)}, f32[1024,512]{1,0:T(8,128)}) custom-call(s32[5]{0:T(128)} %stack.20.refs_0_, s32[1,1024]{1,0:T(1,128)} %bitcast.36, bf16[1024,2048]{1,0:T(8,128)(2,1)} %refs_2_.3, s32[1,512]{1,0:T(1,128)} %bitcast.35, bf16[512,512]{1,0:T(8,128)(2,1)} %copy-done.20, s32[1,512]{1,0:T(1,128)} %bitcast.34, ...), custom_call_target="tpu_custom_call" | custom-call | flops 1 | bytes 1 | tf_op jit(solution)/shard_map/pallas_call | solution.py:129
  47.4 1.6 %add_select_fusion = bf16[512,768]{0,1:T(8,128)(2,1)S(1)} fusion(bf16[512,768]{0,1:T(8,128)(2,1)S(1)} %copy.15, bf16[512,768]{0,1:T(8,128)(2,1)} %collective-permute-done.4, bf16[512,768]{0,1:T(8,128)(2,1)} %collective-permute-done.5, pred[]{:T(512)S(6)} %eq.3), kind=kLoop, calls=%fused_computation.9 | loop fusion | flops 786432 | bytes 3145729 | tf_op jit(solution)/shard_map/jit(_where)/select_n | solution.py:372
  49.1 0.4 collective-permute-start.10
  49.6 1.5 %collective-permute-start.8 = (bf16[512,768]{0,1:T(8,128)(2,1)S(1)}, bf16[512,768]{0,1:T(8,128)(2,1)S(1)}, u32[]{:S(2)}, u32[]{:S(2)}) collective-permute-start(bf16[512,768]{0,1:T(8,128)(2,1)S(1)} %add_select_fusion), channel_id=1, source_target_pairs={{0,16},{16,0},{1,17},{17,1},{2,18},{18,2},{3,19},{19,3},{4,20},{20... | collective-permute-start | bytes 2359304 | tf_op jit(solution)/shard_map/ppermute | solution.py:373
  51.1 3.6 %collective-permute-done.11.refs_4_ = bf16[1024,512]{1,0:T(8,128)(2,1)} collective-permute-done((bf16[1024,512]{1,0:T(8,128)(2,1)}, bf16[1024,512]{1,0:T(8,128)(2,1)}, u32[]{:S(2)}, u32[]{:S(2)}) %collective-permute-start.11) | collective-permute-done | bytes 1048608 | tf_op jit(solution)/shard_map/ppermute | solution.py:360
  54.7 0.9 copy-done.11
  55.6 1.7 %fusion.4 = f32[512,512]{1,0:T(8,128)S(1)} fusion(bf16[512,768]{0,1:T(8,128)(2,1)} %collective-permute-done.9, bf16[768,512]{1,0:T(8,128)(2,1)S(1)} %collective-permute-done.10), kind=kOutput, calls=%fused_computation.34 | convolution fusion | flops 402653184 | bytes 2621440 | tf_op jit(solution)/shard_map/dot_general | solution.py:34
  57.3 0.6 fusion.refs_7_
  58.0 0.7 copy-done.18
  58.7 9.1 %shard_map.79 = (f32[1024,512]{1,0:T(8,128)}, f32[1024,512]{1,0:T(8,128)}) custom-call(s32[5]{0:T(128)} %stack.20.refs_0_, s32[1,1024]{1,0:T(1,128)} %bitcast.37, bf16[1024,512]{1,0:T(8,128)(2,1)} %collective-permute-done.3.refs_2_, s32[1,1024]{1,0:T(1,128)} %bitcast.38, bf16[1024,512]{1,0:T(8,128)(2,1)} %collective-permute-done.11.refs_4_, ...), custom_call_target="tpu_custom_call" | custom-call | flops 1 | bytes 1 | tf_op jit(solution)/shard_map/pallas_call | solution.py:129
  67.8 1.3 collective-permute-done.8
  69.2 0.5 collective-permute-start.12
  69.7 1.7 %fusion.6 = f32[512,512]{1,0:T(8,128)S(1)} fusion(bf16[512,768]{0,1:T(8,128)(2,1)} %collective-permute-done.9, bf16[768,512]{1,0:T(8,128)(2,1)S(1)} %collective-permute-done.16), kind=kOutput, calls=%fused_computation.36 | convolution fusion | flops 402653184 | bytes 2621440 | tf_op jit(solution)/shard_map/dot_general | solution.py:34
  71.5 0.8 collective-permute-done.14
  72.4 0.6 fusion.5
  73.1 0.6 fusion.1
  73.7 0.5 collective-permute-start.15
  74.2 0.6 convolution_add_fusion.1
  74.9 0.8 copy-done.16
  75.7 1.6 %multiply_convert_fusion.9 = (bf16[512,256]{1,0:T(8,128)(2,1)S(1)}, bf16[512,256]{1,0:T(8,128)(2,1)S(1)}, bf16[512,256]{1,0:T(8,128)(2,1)S(1)}, bf16[512,256]{1,0:T(8,128)(2,1)S(1)}) fusion(f32[1024,512]{1,0:T(8,128)S(1)} %copy-done.16, f32[512,512]{1,0:T(8,128)S(1)} %convolution_add_fusion.1, bf16[512,512]{1,0:T(8,128)(2,1)} %collective-permute-done.14, ...), kind=kLoop, calls=%fused_computation.23 | loop fusion | flops 3670016 | bytes 4718592 | tf_op jit(solution)/shard_map/convert_element_type | solution.py:58
  77.3 0.8 collective-permute-start.17
  78.1 0.6 fusion.7
  78.7 0.6 convolution_add_fusion
  79.3 9.3 %collective-permute-done.15 = bf16[512,512]{1,0:T(8,128)(2,1)S(1)} collective-permute-done((bf16[512,512]{1,0:T(8,128)(2,1)S(1)}, bf16[512,512]{1,0:T(8,128)(2,1)S(1)}, u32[]{:S(2)}, u32[]{:S(2)}) %collective-permute-start.15) | collective-permute-done | bytes 524320 | tf_op jit(solution)/shard_map/ppermute | solution.py:387
  89.2 0.6 collective-permute-start.20
  89.9 0.4 collective-permute-start.21
  90.3 1.0 multiply_convert_fusion.1.refs_4_.refs_2_
  91.3 1.0 multiply_convert_fusion.refs_3_.refs_2_
  92.4 0.4 collective-permute-done.21.refs_21_.refs_22_
  93.2 0.4 copy-done.14
  93.6 0.3 copy-done.5
  93.9 11.5 %shard_map.80 = (f32[768,2048]{1,0:T(8,128)}, f32[768,2048]{1,0:T(8,128)}) custom-call(s32[5]{0:T(128)} %stack.20.refs_0_, bf16[768,512]{1,0:T(8,128)(2,1)} %bitcast.32, bf16[768,512]{1,0:T(8,128)(2,1)} %bitcast.29, bf16[768,512]{1,0:T(8,128)(2,1)} %multiply_convert_fusion.refs_3_.refs_2_, bf16[768,512]{1,0:T(8,128)(2,1)} %multiply_convert_fusion.1.refs_4_.refs_2_, ...), custom_call_target="tpu_custom_call" | custom-call | flops 1 | bytes 1 | tf_op jit(solution)/shard_map/pallas_call | solution.py:129
  105.5 4.3 %collective-permute-done.17.refs_4_.refs_5_.refs_6_.refs_7_ = bf16[2048,256]{1,0:T(8,128)(2,1)} collective-permute-done((bf16[2048,256]{1,0:T(8,128)(2,1)S(1)}, bf16[2048,256]{1,0:T(8,128)(2,1)}, u32[]{:S(2)}, u32[]{:S(2)}) %collective-permute-start.17) | collective-permute-done | bytes 1048608 | tf_op jit(solution)/shard_map/ppermute | solution.py:400
  109.8 0.9 collective-permute-start.24
  110.7 1.1 collective-permute-start.23
  111.8 0.9 collective-permute-start.27
  112.8 1.0 copy-done.6
  113.7 8.0 %shard_map.81 = (f32[768,2048]{1,0:T(8,128)}, f32[768,2048]{1,0:T(8,128)}) custom-call(s32[5]{0:T(128)} %stack.20.refs_0_, bf16[768,512]{1,0:T(8,128)(2,1)} %bitcast.33, bf16[768,512]{1,0:T(8,128)(2,1)} %multiply_convert_fusion.refs_3_.refs_2_, f32[768,2048]{1,0:T(8,128)} %refs_3_.3, ...), custom_call_target="tpu_custom_call", output_to_operand_aliasing={{0}: (12, {}), {1}: (13, {})} | custom-call | flops 1 | bytes 1 | tf_op jit(solution)/shard_map/pallas_call | solution.py:129
  121.8 3.0 %collective-permute-done.23.refs_6_ = bf16[512,256]{1,0:T(8,128)(2,1)S(1)} collective-permute-done((bf16[512,256]{1,0:T(8,128)(2,1)S(1)}, bf16[512,256]{1,0:T(8,128)(2,1)S(1)}, u32[]{:S(2)}, u32[]{:S(2)}) %collective-permute-start.23) | collective-permute-done | bytes 262176 | tf_op jit(solution)/shard_map/ppermute | solution.py:405
  124.7 0.5 collective-permute-start.26
  125.2 1.0 collective-permute-done.25.refs_8_
  126.3 0.4 collective-permute-done.26.refs_9_
  126.6 0.3 copy-done.28
  127.0 0.7 copy-done.29
  127.7 5.9 %shard_map.82 = (f32[768,2048]{1,0:T(8,128)}, f32[768,2048]{1,0:T(8,128)}) custom-call(s32[5]{0:T(128)} %stack.20.refs_0_, bf16[768,512]{1,0:T(8,128)(2,1)} %bitcast.30, bf16[768,512]{1,0:T(8,128)(2,1)} %multiply_convert_fusion.1.refs_4_.refs_2_, f32[768,2048]{1,0:T(8,128)} %refs_3_.5, ...), custom_call_target="tpu_custom_call", output_to_operand_aliasing={{0}: (4, {}), {1}: (5, {})} | custom-call | flops 1 | bytes 1 | tf_op jit(solution)/shard_map/pallas_call | solution.py:129
  133.6 1.9 %collective-permute-done.27.refs_6_.refs_7_ = bf16[1024,256]{1,0:T(8,128)(2,1)S(1)} collective-permute-done((bf16[1024,256]{1,0:T(8,128)(2,1)S(1)}, bf16[1024,256]{1,0:T(8,128)(2,1)S(1)}, u32[]{:S(2)}, u32[]{:S(2)}) %collective-permute-start.27) | collective-permute-done | bytes 524320 | tf_op jit(solution)/shard_map/ppermute | solution.py:406
  135.6 1.9 %collective-permute-done.28.refs_8_.refs_9_ = bf16[1024,256]{1,0:T(8,128)(2,1)S(1)} collective-permute-done((bf16[1024,256]{1,0:T(8,128)(2,1)S(1)}, bf16[1024,256]{1,0:T(8,128)(2,1)S(1)}, u32[]{:S(2)}, u32[]{:S(2)}) %collective-permute-start.28) | collective-permute-done | bytes 524320 | tf_op jit(solution)/shard_map/ppermute | solution.py:442
  137.5 0.8 copy-done.15
  138.3 6.1 %shard_map.83 = (f32[768,2048]{1,0:T(8,128)}, f32[768,2048]{1,0:T(8,128)}) custom-call(s32[5]{0:T(128)} %stack.20.refs_0_, bf16[768,512]{1,0:T(8,128)(2,1)} %bitcast.31, bf16[768,512]{1,0:T(8,128)(2,1)} %multiply_convert_fusion.1.refs_4_.refs_2_, f32[768,2048]{1,0:T(8,128)} %refs_3_.5, ...), custom_call_target="tpu_custom_call", output_to_operand_aliasing={{0}: (4, {}), {1}: (5, {})} | custom-call | flops 1 | bytes 1 | tf_op jit(solution)/shard_map/pallas_call | solution.py:129
  (96 shorter events, 2.4 us)
Async XLA Ops:
  0.6 3.2 %copy-start = (bf16[1024,768]{1,0:T(8,128)(2,1)S(1)}, bf16[1024,768]{1,0:T(8,128)(2,1)}, u32[]{:S(2)}) copy-start(bf16[1024,768]{1,0:T(8,128)(2,1)} %param.6) | copy-start | bytes 4718596
  0.6 4.9 %collective-permute-start.1 = (s32[1024]{0:T(1024)}, s32[1024]{0:T(1024)S(1)}, u32[]{:S(2)}, u32[]{:S(2)}) collective-permute-start(s32[1024]{0:T(1024)} %param.7), channel_id=1, source_target_pairs={{0,2},{1,3},{2,0},{3,1},{4,6},{5,7},{6,4},{7,5},{8,10},{9,11},{10,... | collective-permute-start | bytes 12296 | tf_op jit(solution)/shard_map/ppermute | solution.py:352
  3.6 1.9 %collective-permute-start = (s32[1024]{0:T(1024)}, s32[1024]{0:T(1024)S(1)}, u32[]{:S(2)}, u32[]{:S(2)}) collective-permute-start(s32[1024]{0:T(1024)} %param.7), channel_id=1, source_target_pairs={{0,1},{1,0},{2,3},{3,2},{4,5},{5,4},{6,7},{7,6},{8,9},{9,8},{10,11... | collective-permute-start | bytes 12296 | tf_op jit(solution)/shard_map/ppermute | solution.py:352
  3.7 3.2 %collective-permute-start.2 = (s32[1024]{0:T(1024)}, s32[1024]{0:T(1024)S(1)}, u32[]{:S(2)}, u32[]{:S(2)}) collective-permute-start(s32[1024]{0:T(1024)} %param.7), channel_id=1, source_target_pairs={{0,3},{1,2},{2,1},{3,0},{4,7},{5,6},{6,5},{7,4},{8,11},{9,10},{10,... | collective-permute-start | bytes 12296 | tf_op jit(solution)/shard_map/ppermute | solution.py:352
  5.5 16.1 %copy-start.30 = (s32[1024]{0:T(1024)}, s32[1024]{0:T(1024)S(1)}, u32[]{:S(2)}) copy-start(s32[1024]{0:T(1024)S(1)} %collective-permute-done.1) | copy-start | bytes 12292
  6.9 14.7 %copy-start.31 = (s32[1024]{0:T(1024)}, s32[1024]{0:T(1024)S(1)}, u32[]{:S(2)}) copy-start(s32[1024]{0:T(1024)S(1)} %collective-permute-done.2) | copy-start | bytes 12292
  6.9 40.5 %collective-permute-start.3 = (bf16[1024,512]{1,0:T(8,128)(2,1)S(1)}, bf16[1024,512]{1,0:T(8,128)(2,1)}, u32[]{:S(2)}, u32[]{:S(2)}) collective-permute-start(bf16[1024,512]{1,0:T(8,128)(2,1)S(1)} %constant_dynamic-slice_fusion.2), channel_id=1, source_target_pairs={{0,2},{1,3},{2,0},{3,1},{4,6},{5,7},{6,4},{7,5},{8,10},{9,11},{10,... | collective-permute-start | bytes 3145736 | tf_op jit(solution)/shard_map/ppermute | solution.py:358
  7.6 39.8 %collective-permute-start.5 = (bf16[512,768]{0,1:T(8,128)(2,1)S(1)}, bf16[512,768]{0,1:T(8,128)(2,1)}, u32[]{:S(2)}, u32[]{:S(2)}) collective-permute-start(bf16[512,768]{0,1:T(8,128)(2,1)S(1)} %copy.15), channel_id=1, source_target_pairs={{0,12},{15,3},{4,13},{11,2},{16,28},{31,19},{20,29},{27,18}} | collective-permute-start | bytes 2359304 | tf_op jit(solution)/shard_map/ppermute | solution.py:355
  14.0 33.4 %collective-permute-start.4 = (bf16[512,768]{0,1:T(8,128)(2,1)S(1)}, bf16[512,768]{0,1:T(8,128)(2,1)}, u32[]{:S(2)}, u32[]{:S(2)}) collective-permute-start(bf16[512,768]{0,1:T(8,128)(2,1)S(1)} %copy.15), channel_id=1, source_target_pairs={{0,4},{15,11},{1,8},{14,7},{4,1},{11,14},{5,9},{10,6},{16,20},{31,... | collective-permute-start | bytes 2359304 | tf_op jit(solution)/shard_map/ppermute | solution.py:354
  17.0 5.1 %copy-start.33 = (s32[16]{0:T(128)S(1)}, s32[16]{0:T(128)}, u32[]{:S(2)}) copy-start(s32[16]{0:T(128)} %param.11) | copy-start | bytes 196
  21.6 3.0 %collective-permute-start.7 = (bf16[512,512]{1,0:T(8,128)(2,1)}, bf16[512,512]{1,0:T(8,128)(2,1)S(1)}, u32[]{:S(2)}, u32[]{:S(2)}) collective-permute-start(bf16[512,512]{1,0:T(8,128)(2,1)} %get-tuple-element.106), channel_id=1, source_target_pairs={{0,1},{1,0},{2,3},{3,2},{4,5},{5,4},{6,7},{7,6},{8,9},{9,8},{10,11... | collective-permute-start | bytes 1572872 | tf_op jit(solution)/shard_map/ppermute | solution.py:363
  21.6 3.0 %collective-permute-start.6 = (bf16[512,512]{1,0:T(8,128)(2,1)}, bf16[512,512]{1,0:T(8,128)(2,1)S(1)}, u32[]{:S(2)}, u32[]{:S(2)}) collective-permute-start(bf16[512,512]{1,0:T(8,128)(2,1)} %get-tuple-element.107), channel_id=1, source_target_pairs={{0,1},{1,0},{2,3},{3,2},{4,5},{5,4},{6,7},{7,6},{8,9},{9,8},{10,11... | collective-permute-start | bytes 1572872 | tf_op jit(solution)/shard_map/ppermute | solution.py:363
  24.6 0.8 copy-start.19
  24.6 30.1 %collective-permute-start.11 = (bf16[1024,512]{1,0:T(8,128)(2,1)}, bf16[1024,512]{1,0:T(8,128)(2,1)}, u32[]{:S(2)}, u32[]{:S(2)}) collective-permute-start(bf16[1024,512]{1,0:T(8,128)(2,1)} %constant_dynamic-slice_fusion.1), channel_id=1, source_target_pairs={{0,3},{1,2},{2,1},{3,0},{4,7},{5,6},{6,5},{7,4},{8,11},{9,10},{10,... | collective-permute-start | bytes 3145736 | tf_op jit(solution)/shard_map/ppermute | solution.py:360
  25.4 0.8 copy-start.20
  47.4 1.8 %copy-start.32 = (bf16[768,512]{1,0:T(8,128)(2,1)S(1)}, bf16[768,512]{1,0:T(8,128)(2,1)}, u32[]{:S(2)}) copy-start(bf16[768,512]{1,0:T(8,128)(2,1)} %get-tuple-element.70) | copy-start | bytes 2359300
  49.0 42.3 %copy-start.3 = (bf16[512,768]{0,1:T(8,128)(2,1)}, bf16[512,768]{0,1:T(8,128)(2,1)S(1)}, u32[]{:S(2)}) copy-start(bf16[512,768]{0,1:T(8,128)(2,1)S(1)} %add_select_fusion) | copy-start | bytes 2359300
  49.0 8.3 %copy-start.10 = (bf16[768,512]{1,0:T(8,128)(2,1)S(1)}, bf16[768,512]{1,0:T(8,128)(2,1)}, u32[]{:S(2)}) copy-start(bf16[768,512]{1,0:T(8,128)(2,1)} %get-tuple-element.74) | copy-start | bytes 2359300
  49.0 5.7 %collective-permute-start.9 = (bf16[512,768]{0,1:T(8,128)(2,1)S(1)}, bf16[512,768]{0,1:T(8,128)(2,1)}, u32[]{:S(2)}, u32[]{:S(2)}) collective-permute-start(bf16[512,768]{0,1:T(8,128)(2,1)S(1)} %add_select_fusion), channel_id=1, source_target_pairs={{0,1},{1,0},{2,3},{3,2},{4,5},{5,4},{6,7},{7,6},{8,9},{9,8},{10,11... | collective-permute-start | bytes 2359304 | tf_op jit(solution)/shard_map/ppermute | solution.py:374
  49.1 5.5 %collective-permute-start.10 = (bf16[768,512]{1,0:T(8,128)(2,1)S(1)}, bf16[768,512]{1,0:T(8,128)(2,1)S(1)}, u32[]{:S(2)}, u32[]{:S(2)}) collective-permute-start(bf16[768,512]{1,0:T(8,128)(2,1)S(1)} %copy-done.32), channel_id=1, source_target_pairs={{0,1},{1,0},{2,3},{3,2},{4,5},{5,4},{6,7},{7,6},{8,9},{9,8},{10,11... | collective-permute-start | bytes 2359304 | tf_op jit(solution)/shard_map/ppermute | solution.py:375
  49.6 19.5 %collective-permute-start.8 = (bf16[512,768]{0,1:T(8,128)(2,1)S(1)}, bf16[512,768]{0,1:T(8,128)(2,1)S(1)}, u32[]{:S(2)}, u32[]{:S(2)}) collective-permute-start(bf16[512,768]{0,1:T(8,128)(2,1)S(1)} %add_select_fusion), channel_id=1, source_target_pairs={{0,16},{16,0},{1,17},{17,1},{2,18},{18,2},{3,19},{19,3},{4,20},{20... | collective-permute-start | bytes 2359304 | tf_op jit(solution)/shard_map/ppermute | solution.py:373
  51.1 18.7 %collective-permute-start.16 = (bf16[768,512]{1,0:T(8,128)(2,1)}, bf16[768,512]{1,0:T(8,128)(2,1)S(1)}, u32[]{:S(2)}, u32[]{:S(2)}) collective-permute-start(bf16[768,512]{1,0:T(8,128)(2,1)} %get-tuple-element.86), channel_id=1, source_target_pairs={{0,1},{1,0},{2,3},{3,2},{4,5},{5,4},{6,7},{7,6},{8,9},{9,8},{10,11... | collective-permute-start | bytes 2359304 | tf_op jit(solution)/shard_map/ppermute | solution.py:376
  54.7 0.9 copy-start.11
  57.9 0.8 copy-start.18
  57.9 14.4 %collective-permute-start.14 = (bf16[512,512]{1,0:T(8,128)(2,1)S(1)}, bf16[512,512]{1,0:T(8,128)(2,1)}, u32[]{:S(2)}, u32[]{:S(2)}) collective-permute-start(bf16[512,512]{1,0:T(8,128)(2,1)S(1)} %fusion.refs_7_), channel_id=1, source_target_pairs={{0,2},{1,3},{2,0},{3,1},{4,6},{5,7},{6,4},{7,5},{8,10},{9,11},{10,... | collective-permute-start | bytes 1572872 | tf_op jit(solution)/shard_map/ppermute | solution.py:379
  69.1 21.2 %copy-start.2 = (bf16[512,768]{0,1:T(8,128)(2,1)}, bf16[512,768]{0,1:T(8,128)(2,1)S(1)}, u32[]{:S(2)}) copy-start(bf16[512,768]{0,1:T(8,128)(2,1)S(1)} %collective-permute-done.8) | copy-start | bytes 2359300
  69.2 2.3 %collective-permute-start.13 = (bf16[256,768]{0,1:T(8,128)(2,1)S(1)}, bf16[256,768]{0,1:T(8,128)(2,1)S(1)}, u32[]{:S(2)}, u32[]{:S(2)}) collective-permute-start(bf16[256,768]{0,1:T(8,128)(2,1)S(1)} %get-tuple-element.118), channel_id=1, source_target_pairs={{0,1},{1,0},{2,3},{3,2},{4,5},{5,4},{6,7},{7,6},{8,9},{9,8},{10,11... | collective-permute-start | bytes 1179656 | tf_op jit(solution)/shard_map/ppermute | solution.py:383
  69.2 3.2 %copy-start.12 = (bf16[768,512]{1,0:T(8,128)(2,1)S(1)}, bf16[768,512]{1,0:T(8,128)(2,1)}, u32[]{:S(2)}) copy-start(bf16[768,512]{1,0:T(8,128)(2,1)} %copy-done.11) | copy-start | bytes 2359300
  69.2 2.3 %collective-permute-start.12 = (bf16[256,768]{0,1:T(8,128)(2,1)S(1)}, bf16[256,768]{0,1:T(8,128)(2,1)S(1)}, u32[]{:S(2)}, u32[]{:S(2)}) collective-permute-start(bf16[256,768]{0,1:T(8,128)(2,1)S(1)} %get-tuple-element.119), channel_id=1, source_target_pairs={{0,1},{1,0},{2,3},{3,2},{4,5},{5,4},{6,7},{7,6},{8,9},{9,8},{10,11... | collective-permute-start | bytes 1179656 | tf_op jit(solution)/shard_map/ppermute | solution.py:383
  73.0 1.1 copy-start.7
  73.1 1.8 %copy-start.17 = (f32[1024,512]{1,0:T(8,128)S(1)}, f32[1024,512]{1,0:T(8,128)}, u32[]{:S(2)}) copy-start(f32[1024,512]{1,0:T(8,128)} %get-tuple-element.88) | copy-start | bytes 6291460
  73.7 2.0 %copy-start.16 = (f32[1024,512]{1,0:T(8,128)S(1)}, f32[1024,512]{1,0:T(8,128)}, u32[]{:S(2)}) copy-start(f32[1024,512]{1,0:T(8,128)} %get-tuple-element.87) | copy-start | bytes 6291460
  73.7 14.9 %collective-permute-start.15 = (bf16[512,512]{1,0:T(8,128)(2,1)S(1)}, bf16[512,512]{1,0:T(8,128)(2,1)S(1)}, u32[]{:S(2)}, u32[]{:S(2)}) collective-permute-start(bf16[512,512]{1,0:T(8,128)(2,1)S(1)} %fusion.1), channel_id=1, source_target_pairs={{0,2},{1,3},{2,0},{3,1},{4,6},{5,7},{6,4},{7,5},{8,10},{9,11},{10,... | collective-permute-start | bytes 1572872 | tf_op jit(solution)/shard_map/ppermute | solution.py:387
  77.3 11.3 %copy-start.4 = (bf16[2048,256]{1,0:T(8,128)(2,1)}, bf16[2048,256]{1,0:T(8,128)(2,1)S(1)}, u32[]{:S(2)}) copy-start(bf16[2048,256]{1,0:T(8,128)(2,1)S(1)} %pad_maximum_fusion.refs_7_.refs_8_.refs_11_.refs_12_) | copy-start | bytes 3145732
  77.3 32.5 %collective-permute-start.17 = (bf16[2048,256]{1,0:T(8,128)(2,1)S(1)}, bf16[2048,256]{1,0:T(8,128)(2,1)}, u32[]{:S(2)}, u32[]{:S(2)}) collective-permute-start(bf16[2048,256]{1,0:T(8,128)(2,1)S(1)} %pad_maximum_fusion.refs_7_.refs_8_.refs_11_.refs_12_), channel_id=1, source_target_pairs={{0,2},{1,3},{2,0},{3,1},{4,6},{5,7},{6,4},{7,5},{8,10},{9,11},{10,... | collective-permute-start | bytes 3145736 | tf_op jit(solution)/shard_map/ppermute | solution.py:400
  88.6 4.2 %collective-permute-start.18 = (bf16[2048,256]{1,0:T(8,128)(2,1)S(1)}, bf16[2048,256]{1,0:T(8,128)(2,1)S(1)}, u32[]{:S(2)}, u32[]{:S(2)}) collective-permute-start(bf16[2048,256]{1,0:T(8,128)(2,1)S(1)} %pad_maximum_fusion.refs_7_.refs_8_.refs_11_.refs_12_), channel_id=1, source_target_pairs={{0,1},{1,0},{2,3},{3,2},{4,5},{5,4},{6,7},{7,6},{8,9},{9,8},{10,11... | collective-permute-start | bytes 3145736 | tf_op jit(solution)/shard_map/ppermute | solution.py:407
  88.9 2.5 %copy-start.21 = (bf16[512,256]{1,0:T(8,128)(2,1)}, bf16[512,256]{1,0:T(8,128)(2,1)S(1)}, u32[]{:S(2)}) copy-start(bf16[512,256]{1,0:T(8,128)(2,1)S(1)} %get-tuple-element.115.refs_9_) | copy-start | bytes 786436
  88.9 3.9 %copy-start.23 = (bf16[512,256]{1,0:T(8,128)(2,1)}, bf16[512,256]{1,0:T(8,128)(2,1)S(1)}, u32[]{:S(2)}) copy-start(bf16[512,256]{1,0:T(8,128)(2,1)S(1)} %get-tuple-element.114.refs_10_) | copy-start | bytes 786436
  89.2 3.6 %copy-start.8 = (bf16[1024,256]{1,0:T(8,128)(2,1)}, bf16[1024,256]{1,0:T(8,128)(2,1)S(1)}, u32[]{:S(2)}) copy-start(bf16[1024,256]{1,0:T(8,128)(2,1)S(1)} %pad_maximum_fusion.1.refs_13_.refs_14_) | copy-start | bytes 1572868
  89.2 3.2 %collective-permute-start.20 = (bf16[512,256]{1,0:T(8,128)(2,1)S(1)}, bf16[512,256]{1,0:T(8,128)(2,1)S(1)}, u32[]{:S(2)}, u32[]{:S(2)}) collective-permute-start(bf16[512,256]{1,0:T(8,128)(2,1)S(1)} %get-tuple-element.114.refs_10_), channel_id=1, source_target_pairs={{0,1},{1,0},{2,3},{3,2},{4,5},{5,4},{6,7},{7,6},{8,9},{9,8},{10,11... | collective-permute-start | bytes 786440 | tf_op jit(solution)/shard_map/ppermute | solution.py:408
  89.8 2.6 %collective-permute-start.19 = (bf16[512,256]{1,0:T(8,128)(2,1)S(1)}, bf16[512,256]{1,0:T(8,128)(2,1)S(1)}, u32[]{:S(2)}, u32[]{:S(2)}) collective-permute-start(bf16[512,256]{1,0:T(8,128)(2,1)S(1)} %get-tuple-element.115.refs_9_), channel_id=1, source_target_pairs={{0,1},{1,0},{2,3},{3,2},{4,5},{5,4},{6,7},{7,6},{8,9},{9,8},{10,11... | collective-permute-start | bytes 786440 | tf_op jit(solution)/shard_map/ppermute | solution.py:408
  89.9 2.9 %collective-permute-start.21 = (bf16[1024,256]{1,0:T(8,128)(2,1)S(1)}, bf16[1024,256]{1,0:T(8,128)(2,1)S(1)}, u32[]{:S(2)}, u32[]{:S(2)}) collective-permute-start(bf16[1024,256]{1,0:T(8,128)(2,1)S(1)} %pad_maximum_fusion.1.refs_13_.refs_14_), channel_id=1, source_target_pairs={{0,1},{1,0},{2,3},{3,2},{4,5},{5,4},{6,7},{7,6},{8,9},{9,8},{10,11... | collective-permute-start | bytes 1572872 | tf_op jit(solution)/shard_map/ppermute | solution.py:409
  92.4 0.7 copy-start.26
  92.4 0.8 copy-start.27
  92.7 0.9 copy-start.14
  92.8 1.2 copy-start.5
  93.9 16.8 %copy-start.22 = (bf16[512,256]{1,0:T(8,128)(2,1)S(1)}, bf16[512,256]{1,0:T(8,128)(2,1)}, u32[]{:S(2)}) copy-start(bf16[512,256]{1,0:T(8,128)(2,1)} %copy-done.21) | copy-start | bytes 786436
  93.9 17.9 %copy-start.9 = (bf16[1024,256]{1,0:T(8,128)(2,1)S(1)}, bf16[1024,256]{1,0:T(8,128)(2,1)}, u32[]{:S(2)}) copy-start(bf16[1024,256]{1,0:T(8,128)(2,1)} %copy-done.8) | copy-start | bytes 1572868
  109.8 3.0 %collective-permute-start.22 = (bf16[2048,256]{1,0:T(8,128)(2,1)}, bf16[2048,256]{1,0:T(8,128)(2,1)S(1)}, u32[]{:S(2)}, u32[]{:S(2)}) collective-permute-start(bf16[2048,256]{1,0:T(8,128)(2,1)} %collective-permute-done.17.refs_4_.refs_5_.refs_6_.refs_7_), channel_id=1, source_target_pairs={{0,1},{1,0},{2,3},{3,2},{4,5},{5,4},{6,7},{7,6},{8,9},{9,8},{10,11... | collective-permute-start | bytes 3145736 | tf_op jit(solution)/shard_map/ppermute | solution.py:426
  109.8 11.9 %collective-permute-start.24 = (bf16[512,256]{1,0:T(8,128)(2,1)}, bf16[512,256]{1,0:T(8,128)(2,1)S(1)}, u32[]{:S(2)}, u32[]{:S(2)}) collective-permute-start(bf16[512,256]{1,0:T(8,128)(2,1)} %copy-done.23), channel_id=1, source_target_pairs={{0,2},{1,3},{2,0},{3,1},{4,6},{5,7},{6,4},{7,5},{8,10},{9,11},{10,... | collective-permute-start | bytes 786440 | tf_op jit(solution)/shard_map/ppermute | solution.py:405
  110.7 14.0 %collective-permute-start.23 = (bf16[512,256]{1,0:T(8,128)(2,1)S(1)}, bf16[512,256]{1,0:T(8,128)(2,1)S(1)}, u32[]{:S(2)}, u32[]{:S(2)}) collective-permute-start(bf16[512,256]{1,0:T(8,128)(2,1)S(1)} %copy-done.22), channel_id=1, source_target_pairs={{0,2},{1,3},{2,0},{3,1},{4,6},{5,7},{6,4},{7,5},{8,10},{9,11},{10,... | collective-permute-start | bytes 786440 | tf_op jit(solution)/shard_map/ppermute | solution.py:405
  111.8 23.7 %collective-permute-start.27 = (bf16[1024,256]{1,0:T(8,128)(2,1)S(1)}, bf16[1024,256]{1,0:T(8,128)(2,1)S(1)}, u32[]{:S(2)}, u32[]{:S(2)}) collective-permute-start(bf16[1024,256]{1,0:T(8,128)(2,1)S(1)} %copy-done.9), channel_id=1, source_target_pairs={{0,2},{1,3},{2,0},{3,1},{4,6},{5,7},{6,4},{7,5},{8,10},{9,11},{10,... | collective-permute-start | bytes 1572872 | tf_op jit(solution)/shard_map/ppermute | solution.py:406
  112.8 1.0 copy-start.6
  121.7 4.9 %copy-start.24 = (bf16[512,256]{1,0:T(8,128)(2,1)}, bf16[512,256]{1,0:T(8,128)(2,1)S(1)}, u32[]{:S(2)}) copy-start(bf16[512,256]{1,0:T(8,128)(2,1)S(1)} %collective-permute-done.24.refs_7_) | copy-start | bytes 786436
  124.7 1.9 %copy-start.25 = (bf16[512,256]{1,0:T(8,128)(2,1)}, bf16[512,256]{1,0:T(8,128)(2,1)S(1)}, u32[]{:S(2)}) copy-start(bf16[512,256]{1,0:T(8,128)(2,1)S(1)} %collective-permute-done.23.refs_6_) | copy-start | bytes 786436
  124.7 1.5 %collective-permute-start.25 = (bf16[512,256]{1,0:T(8,128)(2,1)S(1)}, bf16[512,256]{1,0:T(8,128)(2,1)S(1)}, u32[]{:S(2)}, u32[]{:S(2)}) collective-permute-start(bf16[512,256]{1,0:T(8,128)(2,1)S(1)} %collective-permute-done.23.refs_6_), channel_id=1, source_target_pairs={{0,1},{1,0},{2,3},{3,2},{4,5},{5,4},{6,7},{7,6},{8,9},{9,8},{10,11... | collective-permute-start | bytes 786440 | tf_op jit(solution)/shard_map/ppermute | solution.py:437
  124.7 1.9 %collective-permute-start.26 = (bf16[512,256]{1,0:T(8,128)(2,1)S(1)}, bf16[512,256]{1,0:T(8,128)(2,1)S(1)}, u32[]{:S(2)}, u32[]{:S(2)}) collective-permute-start(bf16[512,256]{1,0:T(8,128)(2,1)S(1)} %collective-permute-done.24.refs_7_), channel_id=1, source_target_pairs={{0,1},{1,0},{2,3},{3,2},{4,5},{5,4},{6,7},{7,6},{8,9},{9,8},{10,11... | collective-permute-start | bytes 786440 | tf_op jit(solution)/shard_map/ppermute | solution.py:437
  126.3 0.7 copy-start.28
  127.0 0.7 copy-start.29
  135.6 1.9 %copy-start.13 = (bf16[1024,256]{1,0:T(8,128)(2,1)}, bf16[1024,256]{1,0:T(8,128)(2,1)S(1)}, u32[]{:S(2)}) copy-start(bf16[1024,256]{1,0:T(8,128)(2,1)S(1)} %collective-permute-done.27.refs_6_.refs_7_) | copy-start | bytes 1572868
  135.6 1.9 %collective-permute-start.28 = (bf16[1024,256]{1,0:T(8,128)(2,1)S(1)}, bf16[1024,256]{1,0:T(8,128)(2,1)S(1)}, u32[]{:S(2)}, u32[]{:S(2)}) collective-permute-start(bf16[1024,256]{1,0:T(8,128)(2,1)S(1)} %collective-permute-done.27.refs_6_.refs_7_), channel_id=1, source_target_pairs={{0,1},{1,0},{2,3},{3,2},{4,5},{5,4},{6,7},{7,6},{8,9},{9,8},{10,11... | collective-permute-start | bytes 1572872 | tf_op jit(solution)/shard_map/ppermute | solution.py:442
  137.5 0.8 copy-start.15
  138.3 6.1 %copy-start.1 = (bf16[1024,768]{1,0:T(8,128)(2,1)S(1)}, bf16[1024,768]{1,0:T(8,128)(2,1)}, u32[]{:S(2)}) copy-start(bf16[1024,768]{1,0:T(8,128)(2,1)} %param.6) | copy-start | bytes 4718596

commit v5 on v4

--- a/solution.py
+++ b/solution.py
@@ -374,8 +374,9 @@
     core_a = lax.ppermute(tab_a, "dp", CORE)
     w_core_far = lax.ppermute(w_far_send, "dp", CORE)
     w_core_near = lax.ppermute(w_near_send, "dp", CORE)
-    core_a, w_core_far, x2_in = sync((core_a, w_core_far, x2_in))
-    out_a = (dot(tab_a, w_far) + dot(core_a, w_core_far)).astype(BF16)
+    out_a = dot(tab_a, w_far)
+    core_a, w_core_far, x2_in, out_a = sync((core_a, w_core_far, x2_in, out_a))
+    out_a = (out_a + dot(core_a, w_core_far)).astype(BF16)
     pre_a = lax.ppermute(out_a, "dp", CHIP)
     sums = sum_rows(scal, [(idx_chip, x1_in, None), (idx_cross, x2_in, None)], n_rows, part, (s0, s1), [out_a])
     tab_b, s0, s1 = sync((tab_b, *sums))

time: 145 us -> 145 us (level)
  no operation moved by 1% of the time
where the time goes in v5:
time: 145 us; the launch traced here: 144 us
  Pallas kernels  61.8 us (43%)
  waiting for transfers between devices  28.3 us (20%)
  starting transfers between devices  23.2 us (16%)
  local copies, waits for them, and re-layouts  16.5 us (11%)
  matrix products  7.05 us (5%)
  other arithmetic  6.13 us (4%)
    pallas_call x7, Pallas kernels, call(): pl.pallas_call(body, grid_spec=pltpu.PrefetchScalarGridSpec(num_scalar_pr...  61.8 us
    ppermute x1, waiting for transfers between devices, on_device(): pre_b = lax.ppermute(out_b, 'dp', CHIP)  9.17 us
    unnamed x70, local copies, waits for them, and re-layouts  8.02 us
    dot_general x8, matrix products, dot(): return jnp.dot(a, b, preferred_element_type=F32)  7.05 us
    ppermute x1, starting transfers between devices, on_device(): far_a = lax.ppermute(own_a, both, to_far)  6.41 us
    dynamic_slice x3, local copies, waits for them, and re-layouts, cols(): return lax.dynamic_slice(a, (row, (dp_pos ^ flip) * part), (rows, part))  5.86 us
    ppermute x1, waiting for transfers between devices, on_device(): far_a = lax.ppermute(send_a, 'dp', CHIP)  4.38 us
    ppermute x3, starting transfers between devices, on_device(): lax.ppermute(indices, 'dp', p)  3.21 us
  transfers between devices with their start and end apart: 29, of which 12 were waited for; matrix products, arithmetic and copies ran while one was open for 14% of the time, Pallas kernels for 39%

profile of v5, /device:TPU:0, one launch (start us, length us, event | category | flops | bytes accessed | tf_op | source)
XLA Modules:
  0.0 144.2 jit_solution(12471070584712274062)
XLA Ops:
  0.6 3.0 %collective-permute-start.1 = (s32[1024]{0:T(1024)}, s32[1024]{0:T(1024)S(1)}, u32[]{:S(2)}, u32[]{:S(2)}) collective-permute-start(s32[1024]{0:T(1024)} %param.7), channel_id=1, source_target_pairs={{0,2},{1,3},{2,0},{3,1},{4,6},{5,7},{6,4},{7,5},{8,10},{9,11},{10,... | collective-permute-start | bytes 12296 | tf_op jit(solution)/shard_map/ppermute | solution.py:352
  4.2 1.3 constant_dynamic-slice_fusion.2
  5.5 1.4 collective-permute-done.2
  6.9 0.7 collective-permute-start.3
  7.6 6.4 %collective-permute-start.5 = (bf16[512,768]{0,1:T(8,128)(2,1)S(1)}, bf16[512,768]{0,1:T(8,128)(2,1)}, u32[]{:S(2)}, u32[]{:S(2)}) collective-permute-start(bf16[512,768]{0,1:T(8,128)(2,1)S(1)} %copy.15), channel_id=1, source_target_pairs={{0,12},{15,3},{4,13},{11,2},{16,28},{31,19},{20,29},{27,18}} | collective-permute-start | bytes 2359304 | tf_op jit(solution)/shard_map/ppermute | solution.py:355
  14.0 3.0 %collective-permute-start.4 = (bf16[512,768]{0,1:T(8,128)(2,1)S(1)}, bf16[512,768]{0,1:T(8,128)(2,1)}, u32[]{:S(2)}, u32[]{:S(2)}) collective-permute-start(bf16[512,768]{0,1:T(8,128)(2,1)S(1)} %copy.15), channel_id=1, source_target_pairs={{0,4},{15,11},{1,8},{14,7},{4,1},{11,14},{5,9},{10,6},{16,20},{31,... | collective-permute-start | bytes 2359304 | tf_op jit(solution)/shard_map/ppermute | solution.py:354
  17.0 2.3 %constant_dynamic-slice_fusion.1 = bf16[1024,512]{1,0:T(8,128)(2,1)} fusion(bf16[1024,2048]{1,0:T(8,128)(2,1)} %refs_2_.3, s32[]{:T(128)S(6)} %select_n.29), kind=kLoop, calls=%fused_computation.27 | loop fusion | bytes 2097156 | tf_op jit(solution)/shard_map/dynamic_slice | solution.py:350
  19.3 2.2 %constant_dynamic-slice_fusion.4 = (bf16[512,512]{1,0:T(8,128)(2,1)}, bf16[512,512]{1,0:T(8,128)(2,1)}) fusion(bf16[1024,2048]{1,0:T(8,128)(2,1)} %refs_2_.3, s32[]{:T(128)S(6)} %select_n.30), kind=kLoop, calls=%fused_computation.30 | loop fusion | bytes 2097156 | tf_op jit(solution)/shard_map/dynamic_slice | solution.py:350
  21.6 0.5 collective-permute-start.6
  22.1 0.6 dynamic_slice.19
  22.7 1.2 stack.20.refs_0_
  24.0 0.6 fusion.2
  24.6 0.8 copy-done.19
  25.4 0.8 copy-done.20
  26.2 12.6 %shard_map.77 = (bf16[768,512]{1,0:T(8,128)(2,1)}, bf16[768,512]{1,0:T(8,128)(2,1)}, bf16[768,512]{1,0:T(8,128)(2,1)}, bf16[768,512]{1,0:T(8,128)(2,1)}) custom-call(s32[5]{0:T(128)} %stack.20.refs_0_, f32[768,2048]{1,0:T(8,128)} %refs_3_.5, f32[768,2048]{1,0:T(8,128)} %refs_3_.3, bf16[512,512]{1,0:T(8,128)(2,1)} %copy-done.20, bf16[512,512]{1,0:T(8,128)(2,1)} %copy-done.19), custom_call_target="tpu_custom_call" | custom-call | flops 1 | bytes 1 | tf_op jit(solution)/shard_map/pallas_call | solution.py:129
  38.7 8.6 %shard_map.78 = (f32[1024,512]{1,0:T(8,128)}, f32[1024,512]{1,0:T(8,128)}) custom-call(s32[5]{0:T(128)} %stack.20.refs_0_, s32[1,1024]{1,0:T(1,128)} %bitcast.36, bf16[1024,2048]{1,0:T(8,128)(2,1)} %refs_2_.3, s32[1,512]{1,0:T(1,128)} %bitcast.35, bf16[512,512]{1,0:T(8,128)(2,1)} %copy-done.20, s32[1,512]{1,0:T(1,128)} %bitcast.34, ...), custom_call_target="tpu_custom_call" | custom-call | flops 1 | bytes 1 | tf_op jit(solution)/shard_map/pallas_call | solution.py:129
  47.4 1.6 %add_select_fusion = bf16[512,768]{0,1:T(8,128)(2,1)S(1)} fusion(bf16[512,768]{0,1:T(8,128)(2,1)S(1)} %copy.15, bf16[512,768]{0,1:T(8,128)(2,1)} %collective-permute-done.4, bf16[512,768]{0,1:T(8,128)(2,1)} %collective-permute-done.5, pred[]{:T(512)S(6)} %eq.3), kind=kLoop, calls=%fused_computation.8 | loop fusion | flops 786432 | bytes 3145729 | tf_op jit(solution)/shard_map/jit(_where)/select_n | solution.py:372
  49.2 0.4 collective-permute-start.10
  49.6 1.5 %collective-permute-start.8 = (bf16[512,768]{0,1:T(8,128)(2,1)S(1)}, bf16[512,768]{0,1:T(8,128)(2,1)S(1)}, u32[]{:S(2)}, u32[]{:S(2)}) collective-permute-start(bf16[512,768]{0,1:T(8,128)(2,1)S(1)} %add_select_fusion), channel_id=1, source_target_pairs={{0,16},{16,0},{1,17},{17,1},{2,18},{18,2},{3,19},{19,3},{4,20},{20... | collective-permute-start | bytes 2359304 | tf_op jit(solution)/shard_map/ppermute | solution.py:373
  51.1 0.6 fusion.3
  51.7 2.9 %collective-permute-done.11.refs_4_ = bf16[1024,512]{1,0:T(8,128)(2,1)} collective-permute-done((bf16[1024,512]{1,0:T(8,128)(2,1)}, bf16[1024,512]{1,0:T(8,128)(2,1)}, u32[]{:S(2)}, u32[]{:S(2)}) %collective-permute-start.11) | collective-permute-done | bytes 1048608 | tf_op jit(solution)/shard_map/ppermute | solution.py:360
  54.7 0.9 copy-done.11
  55.6 1.7 %fusion.4 = f32[512,512]{1,0:T(8,128)S(1)} fusion(bf16[512,768]{0,1:T(8,128)(2,1)} %collective-permute-done.9, bf16[768,512]{1,0:T(8,128)(2,1)S(1)} %collective-permute-done.10), kind=kOutput, calls=%fused_computation.34 | convolution fusion | flops 402653184 | bytes 2621440 | tf_op jit(solution)/shard_map/dot_general | solution.py:34
  57.7 0.7 copy-done.18
  58.4 9.1 %shard_map.79 = (f32[1024,512]{1,0:T(8,128)}, f32[1024,512]{1,0:T(8,128)}) custom-call(s32[5]{0:T(128)} %stack.20.refs_0_, s32[1,1024]{1,0:T(1,128)} %bitcast.37, bf16[1024,512]{1,0:T(8,128)(2,1)} %collective-permute-done.3.refs_2_, s32[1,1024]{1,0:T(1,128)} %bitcast.38, bf16[1024,512]{1,0:T(8,128)(2,1)} %collective-permute-done.11.refs_4_, ...), custom_call_target="tpu_custom_call" | custom-call | flops 1 | bytes 1 | tf_op jit(solution)/shard_map/pallas_call | solution.py:129
  67.4 1.7 %collective-permute-done.8 = bf16[512,768]{0,1:T(8,128)(2,1)S(1)} collective-permute-done((bf16[512,768]{0,1:T(8,128)(2,1)S(1)}, bf16[512,768]{0,1:T(8,128)(2,1)S(1)}, u32[]{:S(2)}, u32[]{:S(2)}) %collective-permute-start.8) | collective-permute-done | bytes 786464 | tf_op jit(solution)/shard_map/ppermute | solution.py:373
  69.3 0.5 collective-permute-start.12
  69.8 1.7 %fusion.6 = f32[512,512]{1,0:T(8,128)S(1)} fusion(bf16[512,768]{0,1:T(8,128)(2,1)} %collective-permute-done.9, bf16[768,512]{1,0:T(8,128)(2,1)S(1)} %collective-permute-done.16), kind=kOutput, calls=%fused_computation.36 | convolution fusion | flops 402653184 | bytes 2621440 | tf_op jit(solution)/shard_map/dot_general | solution.py:34
  71.5 0.5 collective-permute-done.14
  72.1 0.6 fusion.5
  72.7 0.6 fusion
  73.3 0.9 collective-permute-start.15
  74.2 0.6 convolution_add_fusion.1
  74.8 0.5 copy-done.16
  75.3 1.6 %multiply_convert_fusion.9 = (bf16[512,256]{1,0:T(8,128)(2,1)S(1)}, bf16[512,256]{1,0:T(8,128)(2,1)S(1)}, bf16[512,256]{1,0:T(8,128)(2,1)S(1)}, bf16[512,256]{1,0:T(8,128)(2,1)S(1)}) fusion(f32[1024,512]{1,0:T(8,128)S(1)} %copy-done.16, f32[512,512]{1,0:T(8,128)S(1)} %convolution_add_fusion.1, bf16[512,512]{1,0:T(8,128)(2,1)} %collective-permute-done.14, ...), kind=kLoop, calls=%fused_computation.22 | loop fusion | flops 3670016 | bytes 4718592 | tf_op jit(solution)/shard_map/convert_element_type | solution.py:58
  77.0 0.9 collective-permute-start.17
  77.9 0.6 fusion.7
  78.5 0.6 convolution_add_fusion
  79.1 9.2 %collective-permute-done.15 = bf16[512,512]{1,0:T(8,128)(2,1)S(1)} collective-permute-done((bf16[512,512]{1,0:T(8,128)(2,1)S(1)}, bf16[512,512]{1,0:T(8,128)(2,1)S(1)}, u32[]{:S(2)}, u32[]{:S(2)}) %collective-permute-start.15) | collective-permute-done | bytes 524320 | tf_op jit(solution)/shard_map/ppermute | solution.py:388
  88.8 0.6 collective-permute-start.20
  89.5 0.4 collective-permute-start.21
  89.9 1.0 multiply_convert_fusion.1.refs_4_.refs_2_
  91.0 1.0 multiply_convert_fusion.refs_3_.refs_2_
  92.0 0.4 collective-permute-done.21.refs_21_.refs_22_
  92.9 0.4 copy-done.14
  93.3 0.3 copy-done.5
  93.6 11.5 %shard_map.80 = (f32[768,2048]{1,0:T(8,128)}, f32[768,2048]{1,0:T(8,128)}) custom-call(s32[5]{0:T(128)} %stack.20.refs_0_, bf16[768,512]{1,0:T(8,128)(2,1)} %bitcast.32, bf16[768,512]{1,0:T(8,128)(2,1)} %bitcast.29, bf16[768,512]{1,0:T(8,128)(2,1)} %multiply_convert_fusion.refs_3_.refs_2_, bf16[768,512]{1,0:T(8,128)(2,1)} %multiply_convert_fusion.1.refs_4_.refs_2_, ...), custom_call_target="tpu_custom_call" | custom-call | flops 1 | bytes 1 | tf_op jit(solution)/shard_map/pallas_call | solution.py:129
  105.1 4.4 %collective-permute-done.17.refs_4_.refs_5_.refs_6_.refs_7_ = bf16[2048,256]{1,0:T(8,128)(2,1)} collective-permute-done((bf16[2048,256]{1,0:T(8,128)(2,1)S(1)}, bf16[2048,256]{1,0:T(8,128)(2,1)}, u32[]{:S(2)}, u32[]{:S(2)}) %collective-permute-start.17) | collective-permute-done | bytes 1048608 | tf_op jit(solution)/shard_map/ppermute | solution.py:401
  109.5 1.3 collective-permute-start.24
  110.8 0.8 collective-permute-start.23
  111.5 1.3 collective-permute-start.27
  112.8 1.0 copy-done.6
  113.8 8.0 %shard_map.81 = (f32[768,2048]{1,0:T(8,128)}, f32[768,2048]{1,0:T(8,128)}) custom-call(s32[5]{0:T(128)} %stack.20.refs_0_, bf16[768,512]{1,0:T(8,128)(2,1)} %bitcast.33, bf16[768,512]{1,0:T(8,128)(2,1)} %multiply_convert_fusion.refs_3_.refs_2_, f32[768,2048]{1,0:T(8,128)} %refs_3_.3, ...), custom_call_target="tpu_custom_call", output_to_operand_aliasing={{0}: (12, {}), {1}: (13, {})} | custom-call | flops 1 | bytes 1 | tf_op jit(solution)/shard_map/pallas_call | solution.py:129
  121.8 2.6 %collective-permute-done.23.refs_6_ = bf16[512,256]{1,0:T(8,128)(2,1)S(1)} collective-permute-done((bf16[512,256]{1,0:T(8,128)(2,1)S(1)}, bf16[512,256]{1,0:T(8,128)(2,1)S(1)}, u32[]{:S(2)}, u32[]{:S(2)}) %collective-permute-start.23) | collective-permute-done | bytes 262176 | tf_op jit(solution)/shard_map/ppermute | solution.py:406
  124.4 0.5 collective-permute-start.26
  124.9 1.0 collective-permute-done.25.refs_8_
  126.0 0.4 collective-permute-done.26.refs_9_
  126.3 0.3 copy-done.28
  126.7 0.7 copy-done.29
  127.4 5.9 %shard_map.82 = (f32[768,2048]{1,0:T(8,128)}, f32[768,2048]{1,0:T(8,128)}) custom-call(s32[5]{0:T(128)} %stack.20.refs_0_, bf16[768,512]{1,0:T(8,128)(2,1)} %bitcast.30, bf16[768,512]{1,0:T(8,128)(2,1)} %multiply_convert_fusion.1.refs_4_.refs_2_, f32[768,2048]{1,0:T(8,128)} %refs_3_.5, ...), custom_call_target="tpu_custom_call", output_to_operand_aliasing={{0}: (4, {}), {1}: (5, {})} | custom-call | flops 1 | bytes 1 | tf_op jit(solution)/shard_map/pallas_call | solution.py:129
  133.3 1.9 %collective-permute-done.27.refs_6_.refs_7_ = bf16[1024,256]{1,0:T(8,128)(2,1)S(1)} collective-permute-done((bf16[1024,256]{1,0:T(8,128)(2,1)S(1)}, bf16[1024,256]{1,0:T(8,128)(2,1)S(1)}, u32[]{:S(2)}, u32[]{:S(2)}) %collective-permute-start.27) | collective-permute-done | bytes 524320 | tf_op jit(solution)/shard_map/ppermute | solution.py:407
  135.3 1.9 %collective-permute-done.28.refs_8_.refs_9_ = bf16[1024,256]{1,0:T(8,128)(2,1)S(1)} collective-permute-done((bf16[1024,256]{1,0:T(8,128)(2,1)S(1)}, bf16[1024,256]{1,0:T(8,128)(2,1)S(1)}, u32[]{:S(2)}, u32[]{:S(2)}) %collective-permute-start.28) | collective-permute-done | bytes 524320 | tf_op jit(solution)/shard_map/ppermute | solution.py:443
  137.2 0.8 copy-done.15
  138.0 6.1 %shard_map.83 = (f32[768,2048]{1,0:T(8,128)}, f32[768,2048]{1,0:T(8,128)}) custom-call(s32[5]{0:T(128)} %stack.20.refs_0_, bf16[768,512]{1,0:T(8,128)(2,1)} %bitcast.31, bf16[768,512]{1,0:T(8,128)(2,1)} %multiply_convert_fusion.1.refs_4_.refs_2_, f32[768,2048]{1,0:T(8,128)} %refs_3_.5, ...), custom_call_target="tpu_custom_call", output_to_operand_aliasing={{0}: (4, {}), {1}: (5, {})} | custom-call | flops 1 | bytes 1 | tf_op jit(solution)/shard_map/pallas_call | solution.py:129
  (97 shorter events, 2.5 us)
Async XLA Ops:
  0.6 3.2 %copy-start = (bf16[1024,768]{1,0:T(8,128)(2,1)S(1)}, bf16[1024,768]{1,0:T(8,128)(2,1)}, u32[]{:S(2)}) copy-start(bf16[1024,768]{1,0:T(8,128)(2,1)} %param.6) | copy-start | bytes 4718596
  0.6 4.9 %collective-permute-start.1 = (s32[1024]{0:T(1024)}, s32[1024]{0:T(1024)S(1)}, u32[]{:S(2)}, u32[]{:S(2)}) collective-permute-start(s32[1024]{0:T(1024)} %param.7), channel_id=1, source_target_pairs={{0,2},{1,3},{2,0},{3,1},{4,6},{5,7},{6,4},{7,5},{8,10},{9,11},{10,... | collective-permute-start | bytes 12296 | tf_op jit(solution)/shard_map/ppermute | solution.py:352
  3.6 1.9 %collective-permute-start = (s32[1024]{0:T(1024)}, s32[1024]{0:T(1024)S(1)}, u32[]{:S(2)}, u32[]{:S(2)}) collective-permute-start(s32[1024]{0:T(1024)} %param.7), channel_id=1, source_target_pairs={{0,1},{1,0},{2,3},{3,2},{4,5},{5,4},{6,7},{7,6},{8,9},{9,8},{10,11... | collective-permute-start | bytes 12296 | tf_op jit(solution)/shard_map/ppermute | solution.py:352
  3.7 3.2 %collective-permute-start.2 = (s32[1024]{0:T(1024)}, s32[1024]{0:T(1024)S(1)}, u32[]{:S(2)}, u32[]{:S(2)}) collective-permute-start(s32[1024]{0:T(1024)} %param.7), channel_id=1, source_target_pairs={{0,3},{1,2},{2,1},{3,0},{4,7},{5,6},{6,5},{7,4},{8,11},{9,10},{10,... | collective-permute-start | bytes 12296 | tf_op jit(solution)/shard_map/ppermute | solution.py:352
  5.5 16.1 %copy-start.30 = (s32[1024]{0:T(1024)}, s32[1024]{0:T(1024)S(1)}, u32[]{:S(2)}) copy-start(s32[1024]{0:T(1024)S(1)} %collective-permute-done.1) | copy-start | bytes 12292
  6.9 14.7 %copy-start.31 = (s32[1024]{0:T(1024)}, s32[1024]{0:T(1024)S(1)}, u32[]{:S(2)}) copy-start(s32[1024]{0:T(1024)S(1)} %collective-permute-done.2) | copy-start | bytes 12292
  6.9 40.5 %collective-permute-start.3 = (bf16[1024,512]{1,0:T(8,128)(2,1)S(1)}, bf16[1024,512]{1,0:T(8,128)(2,1)}, u32[]{:S(2)}, u32[]{:S(2)}) collective-permute-start(bf16[1024,512]{1,0:T(8,128)(2,1)S(1)} %constant_dynamic-slice_fusion.2), channel_id=1, source_target_pairs={{0,2},{1,3},{2,0},{3,1},{4,6},{5,7},{6,4},{7,5},{8,10},{9,11},{10,... | collective-permute-start | bytes 3145736 | tf_op jit(solution)/shard_map/ppermute | solution.py:358
  7.6 39.8 %collective-permute-start.5 = (bf16[512,768]{0,1:T(8,128)(2,1)S(1)}, bf16[512,768]{0,1:T(8,128)(2,1)}, u32[]{:S(2)}, u32[]{:S(2)}) collective-permute-start(bf16[512,768]{0,1:T(8,128)(2,1)S(1)} %copy.15), channel_id=1, source_target_pairs={{0,12},{15,3},{4,13},{11,2},{16,28},{31,19},{20,29},{27,18}} | collective-permute-start | bytes 2359304 | tf_op jit(solution)/shard_map/ppermute | solution.py:355
  14.0 33.4 %collective-permute-start.4 = (bf16[512,768]{0,1:T(8,128)(2,1)S(1)}, bf16[512,768]{0,1:T(8,128)(2,1)}, u32[]{:S(2)}, u32[]{:S(2)}) collective-permute-start(bf16[512,768]{0,1:T(8,128)(2,1)S(1)} %copy.15), channel_id=1, source_target_pairs={{0,4},{15,11},{1,8},{14,7},{4,1},{11,14},{5,9},{10,6},{16,20},{31,... | collective-permute-start | bytes 2359304 | tf_op jit(solution)/shard_map/ppermute | solution.py:354
  17.0 5.1 %copy-start.33 = (s32[16]{0:T(128)S(1)}, s32[16]{0:T(128)}, u32[]{:S(2)}) copy-start(s32[16]{0:T(128)} %param.11) | copy-start | bytes 196
  21.6 3.0 %collective-permute-start.7 = (bf16[512,512]{1,0:T(8,128)(2,1)}, bf16[512,512]{1,0:T(8,128)(2,1)S(1)}, u32[]{:S(2)}, u32[]{:S(2)}) collective-permute-start(bf16[512,512]{1,0:T(8,128)(2,1)} %get-tuple-element.108), channel_id=1, source_target_pairs={{0,1},{1,0},{2,3},{3,2},{4,5},{5,4},{6,7},{7,6},{8,9},{9,8},{10,11... | collective-permute-start | bytes 1572872 | tf_op jit(solution)/shard_map/ppermute | solution.py:363
  21.6 3.0 %collective-permute-start.6 = (bf16[512,512]{1,0:T(8,128)(2,1)}, bf16[512,512]{1,0:T(8,128)(2,1)S(1)}, u32[]{:S(2)}, u32[]{:S(2)}) collective-permute-start(bf16[512,512]{1,0:T(8,128)(2,1)} %get-tuple-element.109), channel_id=1, source_target_pairs={{0,1},{1,0},{2,3},{3,2},{4,5},{5,4},{6,7},{7,6},{8,9},{9,8},{10,11... | collective-permute-start | bytes 1572872 | tf_op jit(solution)/shard_map/ppermute | solution.py:363
  24.6 0.8 copy-start.19
  24.6 30.1 %collective-permute-start.11 = (bf16[1024,512]{1,0:T(8,128)(2,1)}, bf16[1024,512]{1,0:T(8,128)(2,1)}, u32[]{:S(2)}, u32[]{:S(2)}) collective-permute-start(bf16[1024,512]{1,0:T(8,128)(2,1)} %constant_dynamic-slice_fusion.1), channel_id=1, source_target_pairs={{0,3},{1,2},{2,1},{3,0},{4,7},{5,6},{6,5},{7,4},{8,11},{9,10},{10,... | collective-permute-start | bytes 3145736 | tf_op jit(solution)/shard_map/ppermute | solution.py:360
  25.4 0.8 copy-start.20
  47.4 1.8 %copy-start.32 = (bf16[768,512]{1,0:T(8,128)(2,1)S(1)}, bf16[768,512]{1,0:T(8,128)(2,1)}, u32[]{:S(2)}) copy-start(bf16[768,512]{1,0:T(8,128)(2,1)} %get-tuple-element.71) | copy-start | bytes 2359300
  47.4 3.7 %copy-start.10 = (bf16[768,512]{1,0:T(8,128)(2,1)S(1)}, bf16[768,512]{1,0:T(8,128)(2,1)}, u32[]{:S(2)}) copy-start(bf16[768,512]{1,0:T(8,128)(2,1)} %get-tuple-element.72) | copy-start | bytes 2359300
  49.0 41.9 %copy-start.3 = (bf16[512,768]{0,1:T(8,128)(2,1)}, bf16[512,768]{0,1:T(8,128)(2,1)S(1)}, u32[]{:S(2)}) copy-start(bf16[512,768]{0,1:T(8,128)(2,1)S(1)} %add_select_fusion) | copy-start | bytes 2359300
  49.0 5.6 %collective-permute-start.9 = (bf16[512,768]{0,1:T(8,128)(2,1)S(1)}, bf16[512,768]{0,1:T(8,128)(2,1)}, u32[]{:S(2)}, u32[]{:S(2)}) collective-permute-start(bf16[512,768]{0,1:T(8,128)(2,1)S(1)} %add_select_fusion), channel_id=1, source_target_pairs={{0,1},{1,0},{2,3},{3,2},{4,5},{5,4},{6,7},{7,6},{8,9},{9,8},{10,11... | collective-permute-start | bytes 2359304 | tf_op jit(solution)/shard_map/ppermute | solution.py:374
  49.2 5.5 %collective-permute-start.10 = (bf16[768,512]{1,0:T(8,128)(2,1)S(1)}, bf16[768,512]{1,0:T(8,128)(2,1)S(1)}, u32[]{:S(2)}, u32[]{:S(2)}) collective-permute-start(bf16[768,512]{1,0:T(8,128)(2,1)S(1)} %copy-done.32), channel_id=1, source_target_pairs={{0,1},{1,0},{2,3},{3,2},{4,5},{5,4},{6,7},{7,6},{8,9},{9,8},{10,11... | collective-permute-start | bytes 2359304 | tf_op jit(solution)/shard_map/ppermute | solution.py:375
  49.6 19.5 %collective-permute-start.8 = (bf16[512,768]{0,1:T(8,128)(2,1)S(1)}, bf16[512,768]{0,1:T(8,128)(2,1)S(1)}, u32[]{:S(2)}, u32[]{:S(2)}) collective-permute-start(bf16[512,768]{0,1:T(8,128)(2,1)S(1)} %add_select_fusion), channel_id=1, source_target_pairs={{0,16},{16,0},{1,17},{17,1},{2,18},{18,2},{3,19},{19,3},{4,20},{20... | collective-permute-start | bytes 2359304 | tf_op jit(solution)/shard_map/ppermute | solution.py:373
  51.1 18.7 %collective-permute-start.16 = (bf16[768,512]{1,0:T(8,128)(2,1)}, bf16[768,512]{1,0:T(8,128)(2,1)S(1)}, u32[]{:S(2)}, u32[]{:S(2)}) collective-permute-start(bf16[768,512]{1,0:T(8,128)(2,1)} %get-tuple-element.88), channel_id=1, source_target_pairs={{0,1},{1,0},{2,3},{3,2},{4,5},{5,4},{6,7},{7,6},{8,9},{9,8},{10,11... | collective-permute-start | bytes 2359304 | tf_op jit(solution)/shard_map/ppermute | solution.py:376
  54.7 0.9 copy-start.11
  57.6 0.8 copy-start.18
  57.6 14.4 %collective-permute-start.14 = (bf16[512,512]{1,0:T(8,128)(2,1)S(1)}, bf16[512,512]{1,0:T(8,128)(2,1)}, u32[]{:S(2)}, u32[]{:S(2)}) collective-permute-start(bf16[512,512]{1,0:T(8,128)(2,1)S(1)} %add_convert_fusion.refs_7_), channel_id=1, source_target_pairs={{0,2},{1,3},{2,0},{3,1},{4,6},{5,7},{6,4},{7,5},{8,10},{9,11},{10,... | collective-permute-start | bytes 1572872 | tf_op jit(solution)/shard_map/ppermute | solution.py:380
  69.1 20.8 %copy-start.2 = (bf16[512,768]{0,1:T(8,128)(2,1)}, bf16[512,768]{0,1:T(8,128)(2,1)S(1)}, u32[]{:S(2)}) copy-start(bf16[512,768]{0,1:T(8,128)(2,1)S(1)} %collective-permute-done.8) | copy-start | bytes 2359300
  69.2 2.3 %collective-permute-start.13 = (bf16[256,768]{0,1:T(8,128)(2,1)S(1)}, bf16[256,768]{0,1:T(8,128)(2,1)S(1)}, u32[]{:S(2)}, u32[]{:S(2)}) collective-permute-start(bf16[256,768]{0,1:T(8,128)(2,1)S(1)} %get-tuple-element.120), channel_id=1, source_target_pairs={{0,1},{1,0},{2,3},{3,2},{4,5},{5,4},{6,7},{7,6},{8,9},{9,8},{10,11... | collective-permute-start | bytes 1179656 | tf_op jit(solution)/shard_map/ppermute | solution.py:384
  69.3 2.8 %copy-start.12 = (bf16[768,512]{1,0:T(8,128)(2,1)S(1)}, bf16[768,512]{1,0:T(8,128)(2,1)}, u32[]{:S(2)}) copy-start(bf16[768,512]{1,0:T(8,128)(2,1)} %copy-done.11) | copy-start | bytes 2359300
  69.3 2.3 %collective-permute-start.12 = (bf16[256,768]{0,1:T(8,128)(2,1)S(1)}, bf16[256,768]{0,1:T(8,128)(2,1)S(1)}, u32[]{:S(2)}, u32[]{:S(2)}) collective-permute-start(bf16[256,768]{0,1:T(8,128)(2,1)S(1)} %get-tuple-element.121), channel_id=1, source_target_pairs={{0,1},{1,0},{2,3},{3,2},{4,5},{5,4},{6,7},{7,6},{8,9},{9,8},{10,11... | collective-permute-start | bytes 1179656 | tf_op jit(solution)/shard_map/ppermute | solution.py:384
  72.7 1.5 %copy-start.7 = (bf16[768,512]{1,0:T(8,128)(2,1)S(1)}, bf16[768,512]{1,0:T(8,128)(2,1)}, u32[]{:S(2)}) copy-start(bf16[768,512]{1,0:T(8,128)(2,1)} %get-tuple-element.87.refs_7_) | copy-start | bytes 2359300
  72.7 2.1 %copy-start.17 = (f32[1024,512]{1,0:T(8,128)S(1)}, f32[1024,512]{1,0:T(8,128)}, u32[]{:S(2)}) copy-start(f32[1024,512]{1,0:T(8,128)} %get-tuple-element.90) | copy-start | bytes 6291460
  73.3 2.0 %copy-start.16 = (f32[1024,512]{1,0:T(8,128)S(1)}, f32[1024,512]{1,0:T(8,128)}, u32[]{:S(2)}) copy-start(f32[1024,512]{1,0:T(8,128)} %get-tuple-element.89) | copy-start | bytes 6291460
  73.3 14.9 %collective-permute-start.15 = (bf16[512,512]{1,0:T(8,128)(2,1)S(1)}, bf16[512,512]{1,0:T(8,128)(2,1)S(1)}, u32[]{:S(2)}, u32[]{:S(2)}) collective-permute-start(bf16[512,512]{1,0:T(8,128)(2,1)S(1)} %fusion), channel_id=1, source_target_pairs={{0,2},{1,3},{2,0},{3,1},{4,6},{5,7},{6,4},{7,5},{8,10},{9,11},{10,... | collective-permute-start | bytes 1572872 | tf_op jit(solution)/shard_map/ppermute | solution.py:388
  77.0 11.3 %copy-start.4 = (bf16[2048,256]{1,0:T(8,128)(2,1)}, bf16[2048,256]{1,0:T(8,128)(2,1)S(1)}, u32[]{:S(2)}) copy-start(bf16[2048,256]{1,0:T(8,128)(2,1)S(1)} %pad_maximum_fusion.refs_7_.refs_8_.refs_11_.refs_12_) | copy-start | bytes 3145732
  77.0 32.5 %collective-permute-start.17 = (bf16[2048,256]{1,0:T(8,128)(2,1)S(1)}, bf16[2048,256]{1,0:T(8,128)(2,1)}, u32[]{:S(2)}, u32[]{:S(2)}) collective-permute-start(bf16[2048,256]{1,0:T(8,128)(2,1)S(1)} %pad_maximum_fusion.refs_7_.refs_8_.refs_11_.refs_12_), channel_id=1, source_target_pairs={{0,2},{1,3},{2,0},{3,1},{4,6},{5,7},{6,4},{7,5},{8,10},{9,11},{10,... | collective-permute-start | bytes 3145736 | tf_op jit(solution)/shard_map/ppermute | solution.py:401
  88.2 4.2 %collective-permute-start.18 = (bf16[2048,256]{1,0:T(8,128)(2,1)S(1)}, bf16[2048,256]{1,0:T(8,128)(2,1)S(1)}, u32[]{:S(2)}, u32[]{:S(2)}) collective-permute-start(bf16[2048,256]{1,0:T(8,128)(2,1)S(1)} %pad_maximum_fusion.refs_7_.refs_8_.refs_11_.refs_12_), channel_id=1, source_target_pairs={{0,1},{1,0},{2,3},{3,2},{4,5},{5,4},{6,7},{7,6},{8,9},{9,8},{10,11... | collective-permute-start | bytes 3145736 | tf_op jit(solution)/shard_map/ppermute | solution.py:408
  88.5 2.5 %copy-start.21 = (bf16[512,256]{1,0:T(8,128)(2,1)}, bf16[512,256]{1,0:T(8,128)(2,1)S(1)}, u32[]{:S(2)}) copy-start(bf16[512,256]{1,0:T(8,128)(2,1)S(1)} %get-tuple-element.117.refs_9_) | copy-start | bytes 786436
  88.5 3.9 %copy-start.23 = (bf16[512,256]{1,0:T(8,128)(2,1)}, bf16[512,256]{1,0:T(8,128)(2,1)S(1)}, u32[]{:S(2)}) copy-start(bf16[512,256]{1,0:T(8,128)(2,1)S(1)} %get-tuple-element.116.refs_10_) | copy-start | bytes 786436
  88.8 3.6 %copy-start.8 = (bf16[1024,256]{1,0:T(8,128)(2,1)}, bf16[1024,256]{1,0:T(8,128)(2,1)S(1)}, u32[]{:S(2)}) copy-start(bf16[1024,256]{1,0:T(8,128)(2,1)S(1)} %pad_maximum_fusion.1.refs_13_.refs_14_) | copy-start | bytes 1572868
  88.8 3.2 %collective-permute-start.20 = (bf16[512,256]{1,0:T(8,128)(2,1)S(1)}, bf16[512,256]{1,0:T(8,128)(2,1)S(1)}, u32[]{:S(2)}, u32[]{:S(2)}) collective-permute-start(bf16[512,256]{1,0:T(8,128)(2,1)S(1)} %get-tuple-element.116.refs_10_), channel_id=1, source_target_pairs={{0,1},{1,0},{2,3},{3,2},{4,5},{5,4},{6,7},{7,6},{8,9},{9,8},{10,11... | collective-permute-start | bytes 786440 | tf_op jit(solution)/shard_map/ppermute | solution.py:409
  89.4 2.6 %collective-permute-start.19 = (bf16[512,256]{1,0:T(8,128)(2,1)S(1)}, bf16[512,256]{1,0:T(8,128)(2,1)S(1)}, u32[]{:S(2)}, u32[]{:S(2)}) collective-permute-start(bf16[512,256]{1,0:T(8,128)(2,1)S(1)} %get-tuple-element.117.refs_9_), channel_id=1, source_target_pairs={{0,1},{1,0},{2,3},{3,2},{4,5},{5,4},{6,7},{7,6},{8,9},{9,8},{10,11... | collective-permute-start | bytes 786440 | tf_op jit(solution)/shard_map/ppermute | solution.py:409
  89.5 2.9 %collective-permute-start.21 = (bf16[1024,256]{1,0:T(8,128)(2,1)S(1)}, bf16[1024,256]{1,0:T(8,128)(2,1)S(1)}, u32[]{:S(2)}, u32[]{:S(2)}) collective-permute-start(bf16[1024,256]{1,0:T(8,128)(2,1)S(1)} %pad_maximum_fusion.1.refs_13_.refs_14_), channel_id=1, source_target_pairs={{0,1},{1,0},{2,3},{3,2},{4,5},{5,4},{6,7},{7,6},{8,9},{9,8},{10,11... | collective-permute-start | bytes 1572872 | tf_op jit(solution)/shard_map/ppermute | solution.py:410
  92.0 0.7 copy-start.26
  92.0 0.8 copy-start.27
  92.4 0.9 copy-start.14
  92.4 1.2 copy-start.5
  93.6 17.2 %copy-start.22 = (bf16[512,256]{1,0:T(8,128)(2,1)S(1)}, bf16[512,256]{1,0:T(8,128)(2,1)}, u32[]{:S(2)}) copy-start(bf16[512,256]{1,0:T(8,128)(2,1)} %copy-done.21) | copy-start | bytes 786436
  93.6 18.0 %copy-start.9 = (bf16[1024,256]{1,0:T(8,128)(2,1)S(1)}, bf16[1024,256]{1,0:T(8,128)(2,1)}, u32[]{:S(2)}) copy-start(bf16[1024,256]{1,0:T(8,128)(2,1)} %copy-done.8) | copy-start | bytes 1572868
  109.5 3.3 %collective-permute-start.22 = (bf16[2048,256]{1,0:T(8,128)(2,1)}, bf16[2048,256]{1,0:T(8,128)(2,1)S(1)}, u32[]{:S(2)}, u32[]{:S(2)}) collective-permute-start(bf16[2048,256]{1,0:T(8,128)(2,1)} %collective-permute-done.17.refs_4_.refs_5_.refs_6_.refs_7_), channel_id=1, source_target_pairs={{0,1},{1,0},{2,3},{3,2},{4,5},{5,4},{6,7},{7,6},{8,9},{9,8},{10,11... | collective-permute-start | bytes 3145736 | tf_op jit(solution)/shard_map/ppermute | solution.py:427
  109.5 12.3 %collective-permute-start.24 = (bf16[512,256]{1,0:T(8,128)(2,1)}, bf16[512,256]{1,0:T(8,128)(2,1)S(1)}, u32[]{:S(2)}, u32[]{:S(2)}) collective-permute-start(bf16[512,256]{1,0:T(8,128)(2,1)} %copy-done.23), channel_id=1, source_target_pairs={{0,2},{1,3},{2,0},{3,1},{4,6},{5,7},{6,4},{7,5},{8,10},{9,11},{10,... | collective-permute-start | bytes 786440 | tf_op jit(solution)/shard_map/ppermute | solution.py:406
  110.8 13.7 %collective-permute-start.23 = (bf16[512,256]{1,0:T(8,128)(2,1)S(1)}, bf16[512,256]{1,0:T(8,128)(2,1)S(1)}, u32[]{:S(2)}, u32[]{:S(2)}) collective-permute-start(bf16[512,256]{1,0:T(8,128)(2,1)S(1)} %copy-done.22), channel_id=1, source_target_pairs={{0,2},{1,3},{2,0},{3,1},{4,6},{5,7},{6,4},{7,5},{8,10},{9,11},{10,... | collective-permute-start | bytes 786440 | tf_op jit(solution)/shard_map/ppermute | solution.py:406
  111.5 23.7 %collective-permute-start.27 = (bf16[1024,256]{1,0:T(8,128)(2,1)S(1)}, bf16[1024,256]{1,0:T(8,128)(2,1)S(1)}, u32[]{:S(2)}, u32[]{:S(2)}) collective-permute-start(bf16[1024,256]{1,0:T(8,128)(2,1)S(1)} %copy-done.9), channel_id=1, source_target_pairs={{0,2},{1,3},{2,0},{3,1},{4,6},{5,7},{6,4},{7,5},{8,10},{9,11},{10,... | collective-permute-start | bytes 1572872 | tf_op jit(solution)/shard_map/ppermute | solution.py:407
  112.8 1.0 copy-start.6
  121.8 4.6 %copy-start.24 = (bf16[512,256]{1,0:T(8,128)(2,1)}, bf16[512,256]{1,0:T(8,128)(2,1)S(1)}, u32[]{:S(2)}) copy-start(bf16[512,256]{1,0:T(8,128)(2,1)S(1)} %collective-permute-done.24.refs_7_) | copy-start | bytes 786436
  124.4 1.9 %copy-start.25 = (bf16[512,256]{1,0:T(8,128)(2,1)}, bf16[512,256]{1,0:T(8,128)(2,1)S(1)}, u32[]{:S(2)}) copy-start(bf16[512,256]{1,0:T(8,128)(2,1)S(1)} %collective-permute-done.23.refs_6_) | copy-start | bytes 786436
  124.4 1.5 %collective-permute-start.25 = (bf16[512,256]{1,0:T(8,128)(2,1)S(1)}, bf16[512,256]{1,0:T(8,128)(2,1)S(1)}, u32[]{:S(2)}, u32[]{:S(2)}) collective-permute-start(bf16[512,256]{1,0:T(8,128)(2,1)S(1)} %collective-permute-done.23.refs_6_), channel_id=1, source_target_pairs={{0,1},{1,0},{2,3},{3,2},{4,5},{5,4},{6,7},{7,6},{8,9},{9,8},{10,11... | collective-permute-start | bytes 786440 | tf_op jit(solution)/shard_map/ppermute | solution.py:438
  124.4 1.9 %collective-permute-start.26 = (bf16[512,256]{1,0:T(8,128)(2,1)S(1)}, bf16[512,256]{1,0:T(8,128)(2,1)S(1)}, u32[]{:S(2)}, u32[]{:S(2)}) collective-permute-start(bf16[512,256]{1,0:T(8,128)(2,1)S(1)} %collective-permute-done.24.refs_7_), channel_id=1, source_target_pairs={{0,1},{1,0},{2,3},{3,2},{4,5},{5,4},{6,7},{7,6},{8,9},{9,8},{10,11... | collective-permute-start | bytes 786440 | tf_op jit(solution)/shard_map/ppermute | solution.py:438
  126.0 0.7 copy-start.28
  126.7 0.7 copy-start.29
  135.3 1.9 %copy-start.13 = (bf16[1024,256]{1,0:T(8,128)(2,1)}, bf16[1024,256]{1,0:T(8,128)(2,1)S(1)}, u32[]{:S(2)}) copy-start(bf16[1024,256]{1,0:T(8,128)(2,1)S(1)} %collective-permute-done.27.refs_6_.refs_7_) | copy-start | bytes 1572868
  135.3 1.9 %collective-permute-start.28 = (bf16[1024,256]{1,0:T(8,128)(2,1)S(1)}, bf16[1024,256]{1,0:T(8,128)(2,1)S(1)}, u32[]{:S(2)}, u32[]{:S(2)}) collective-permute-start(bf16[1024,256]{1,0:T(8,128)(2,1)S(1)} %collective-permute-done.27.refs_6_.refs_7_), channel_id=1, source_target_pairs={{0,1},{1,0},{2,3},{3,2},{4,5},{5,4},{6,7},{7,6},{8,9},{9,8},{10,11... | collective-permute-start | bytes 1572872 | tf_op jit(solution)/shard_map/ppermute | solution.py:443
  137.2 0.8 copy-start.15
  138.0 6.1 %copy-start.1 = (bf16[1024,768]{1,0:T(8,128)(2,1)S(1)}, bf16[1024,768]{1,0:T(8,128)(2,1)}, u32[]{:S(2)}) copy-start(bf16[1024,768]{1,0:T(8,128)(2,1)} %param.6) | copy-start | bytes 4718596
